TPU v7x, 128 devices: a whole 4x4x4 slice. The times are simulated.
128 devices in a mesh: dp: 64 (over x_hi, y, z, core), mp: 2 (over x_lo).
Axes of the slice: x: 4 (x_hi: 2, x_lo: 2; x = x_hi * 2 + x_lo), y: 4, z: 4, core: 2. Of those that a mesh axis runs over, the one named last changes fastest.
Arguments:
- image_emb: bfloat16 [8192, 1152], P('dp', 'mp'), may hold values from -0.1875 to 0.1875
- caption_emb: bfloat16 [12288, 1152], P('dp', 'mp'), may hold values from -0.1875 to 0.1875
- caption_count: int32 [8192], P('dp'), may hold values from 1 to 5, as said below
- caption_owner: int32 [12288], P('dp'), may hold values from 0 to 63, as said below
- pair_image: int32 [16384], P('dp'), may hold values from -1 to 127, as said below
Outputs:
- image_grad: bfloat16 [8192, 1152], P('dp', 'mp')
- caption_grad: bfloat16 [12288, 1152], P('dp', 'mp')
Inputs may be any that keep to these rules, and one draw needn't show every extreme that they name: `caption_owner`: each loader sends either 2 or 4 of its rows to each owner; some owner receives 4 rows from every loader. `pair_image`: slot s * 4 + r of owner o names an image exactly when loader s sends more than r rows to o, and holds -1 otherwise; every image of the owner is named at least once. caption_count[i] is the number of slots that name image i.
All inputs are finite; a program needn't handle non-finite values.
Results may differ from a plain program's by a relative error of at most 0.0013.
The roundings to bfloat16 on the way count: a program that leaves them out, or rounds other values in their place, can miss the bound.
Values may be sent and summed in bfloat16 or wider, within the bound.
No kernel may reach another device: no remote copies, remote signals or barrier semaphores. Data moves between devices by JAX's collectives and lax.ppermute only.
A program may use at most 192 MiB of HBM per device.

v0:
```python
import jax
import jax.numpy as jnp
from jax import lax
from jax.sharding import PartitionSpec as P

logit_scale = 10.0
logit_bias = -2.0


def cross_rows(left, right):
    return lax.dot_general(
        left, right, (((1,), (1,)), ((), ())), preferred_element_type=jnp.float32
    )


def down_rows(left, right):
    return lax.dot_general(
        left, right, (((0,), (0,)), ((), ())), preferred_element_type=jnp.float32
    )


def make_coefficient(products, positive, inverse_count):
    logits = logit_scale * products + logit_bias
    weight = 1.0 + positive * (inverse_count - 1.0)
    return (logit_scale * weight * (jax.nn.sigmoid(logits) - positive)).astype(jnp.bfloat16)


def body(image_emb, caption_emb, caption_count, caption_owner, pair_image):
    groups = lax.axis_size("dp")
    slot_count = pair_image.shape[0]
    load_count = caption_owner.shape[0]
    image_count = image_emb.shape[0]
    half_width = image_emb.shape[1]
    per_owner = slot_count // groups
    column = lax.axis_index("mp") * half_width
    holder = lax.axis_index("dp")
    positions = jnp.arange(load_count, dtype=jnp.int32)
    earlier = positions[None, :] < positions[:, None]
    same_owner = caption_owner[:, None] == caption_owner[None, :]
    rank_index = jnp.sum((same_owner & earlier).astype(jnp.int32), axis=1)
    slot_index = caption_owner * per_owner + rank_index
    placing = (jnp.arange(slot_count, dtype=jnp.int32)[:, None] == slot_index[None, :]).astype(
        jnp.bfloat16
    )
    outgoing = jnp.dot(placing, caption_emb, preferred_element_type=jnp.float32).astype(
        jnp.bfloat16
    )
    owned_rows = lax.all_to_all(outgoing, "dp", split_axis=0, concat_axis=0, tiled=True)
    images_wide, captions_wide = (
        lax.all_gather(image_emb, "mp", axis=1, tiled=True),
        lax.all_gather(owned_rows, "mp", axis=1, tiled=True),
    )
    local_rows = jnp.arange(image_count, dtype=jnp.int32)
    inverse_count = 1.0 / caption_count.astype(jnp.float32)
    slot_global = jnp.where(pair_image >= 0, holder * image_count + pair_image, -1)
    own_positive = (pair_image[None, :] == local_rows[:, None]).astype(jnp.float32)
    slot_inverse = jnp.sum(own_positive * inverse_count[:, None], axis=0)
    piece = lax.all_gather(images_wide, "dp", axis=0, tiled=True)
    count = piece.shape[0]
    piece_rows = jnp.arange(count, dtype=jnp.int32)
    positive = (piece_rows[:, None] == slot_global[None, :]).astype(jnp.float32)
    coefficient = make_coefficient(
        cross_rows(piece, captions_wide), positive, slot_inverse[None, :]
    )
    piece_half = lax.dynamic_slice_in_dim(piece, column, half_width, 1)
    text_total = down_rows(coefficient, piece_half)
    image_terms = jnp.dot(coefficient, owned_rows, preferred_element_type=jnp.float32)
    text_total, image_terms = (text_total, image_terms)
    image_total = lax.psum_scatter(image_terms, "dp", scatter_dimension=0, tiled=True)
    returned = lax.all_to_all(
        text_total.astype(jnp.bfloat16), "dp", split_axis=0, concat_axis=0, tiled=True
    )
    caption_grad = jnp.take(returned, slot_index, axis=0)
    return (image_total.astype(jnp.bfloat16), caption_grad)


def solution(mesh):
    in_specs = (P("dp", "mp"), P("dp", "mp"), P("dp"), P("dp"), P("dp"))
    out_specs = (P("dp", "mp"), P("dp", "mp"))
    return jax.shard_map(body, mesh=mesh, in_specs=in_specs, out_specs=out_specs, check_vma=False)
```

profile of v0, /device:TPU:0, one launch (start us, length us, event | category | flops | bytes accessed | tf_op | source)
XLA Modules:
  0.0 409.5 jit_solution(10440924156195011961)
XLA Ops:
  7.2 0.0 copy-start
  7.2 0.0 all-gather.2.cloned.1.call-start
  7.2 8.1 %all_gather.10 = bf16[128,1152]{0,1:T(8,128)(2,1)} all-gather(bf16[128,576]{0,1:T(8,128)(2,1)} %param.5), channel_id=1, replica_groups=mesh['dp'=64,'mp'=2] {'mp'}, dimensions={1}, use_global_device_ids=true | all-gather | bytes 442368 | tf_op jit(solution)/shard_map/all_gather | solution.py:50
  15.3 0.0 all-gather.2.cloned.1.call-update
  15.3 0.9 convert_reduce_fusion
  16.3 0.7 compare_and_fusion
  17.0 0.0 copy-done
  17.0 0.3 convolution_convert_fusion
  17.3 0.2 copy.13
  17.5 0.8 all_to_all.16
  18.3 11.1 %all-to-all-start = ((bf16[64,4,576]{2,1,0:T(4,128)(2,1)}), bf16[64,4,576]{2,1,0:T(4,128)(2,1)S(1)}, u32[]{:S(2)}, u32[]{:S(2)}) async-start(bf16[64,4,576]{2,1,0:T(4,128)(2,1)} %all_to_all.16), calls=%async_computation | async-start | bytes 655360 | tf_op jit(solution)/shard_map/all_to_all | solution.py:48
  29.4 0.0 reduce-scatter.2.cloned.1.call-start
  29.5 0.7 convert_divide_fusion
  30.1 0.7 compare_select_fusion.1
  30.8 0.8 select_reduce_fusion
  31.6 11.4 %all-to-all-done = bf16[64,4,576]{2,1,0:T(4,128)(2,1)S(1)} async-done(((bf16[64,4,576]{2,1,0:T(4,128)(2,1)}), bf16[64,4,576]{2,1,0:T(4,128)(2,1)S(1)}, u32[]{:S(2)}, u32[]{:S(2)}) %all-to-all-start) | async-done | bytes 294944 | tf_op jit(solution)/shard_map/all_to_all | solution.py:48
  43.0 0.2 all_to_all.18
  43.2 0.2 copy.14
  43.4 9.7 %all_gather.9 = bf16[256,1152]{0,1:T(8,128)(2,1)S(1)} all-gather(bf16[256,576]{0,1:T(8,128)(2,1)S(1)} %copy.14), channel_id=1, replica_groups=mesh['dp'=64,'mp'=2] {'mp'}, dimensions={1}, use_global_device_ids=true | all-gather | bytes 884736 | tf_op jit(solution)/shard_map/all_gather | solution.py:51
  53.1 114.2 %all-gather.2.cloned.1.call-done = bf16[8192,1152]{0,1:T(8,128)(2,1)} async-done(((bf16[128,1152]{0,1:T(8,128)(2,1)}), bf16[8192,1152]{0,1:T(8,128)(2,1)}) %all-gather.2.cloned.1.call-update) | async-done | bytes 18874384 | tf_op jit(solution)/shard_map/all_gather | solution.py:58
  167.3 13.1 %fusion.8 = bf16[8192,256]{0,1:T(8,128)(2,1)S(1)} fusion(bf16[256,1152]{0,1:T(8,128)(2,1)S(1)} %all_gather.9, bf16[8192,1152]{0,1:T(8,128)(2,1)} %all-gather.2.cloned.1.call-done, f32[256]{0:T(256)S(1)} %broadcast_add_fusion, s32[256]{0:T(256)S(1)} %compare_select_fusion.1), kind=kOutput, calls=%fused_computation.10 | convolution fusion | flops 4859101184 | bytes 23660544 | tf_op jit(solution)/shard_map/dot_general | solution.py:11
  180.4 0.0 copy-start.1
  180.4 1.9 copy-done.1
  182.3 8.0 %fusion.17 = f32[8192,576]{0,1:T(8,128)} fusion(bf16[8192,256]{0,1:T(8,128)(2,1)S(1)} %fusion.8, bf16[256,576]{1,0:T(8,128)(2,1)S(1)} %all_to_all.18), kind=kOutput, calls=%fused_computation.32 | convolution fusion | flops 2415919104 | bytes 23363584 | tf_op jit(solution)/shard_map/dot_general | solution.py:67
  190.3 0.0 reduce-scatter.2.cloned.1.call-update
  190.3 7.6 %fusion.11 = bf16[256,576]{0,1:T(8,128)(2,1)S(1)} fusion(bf16[8192,256]{0,1:T(8,128)(2,1)} %copy-done.1, bf16[8192,1152]{0,1:T(8,128)(2,1)} %all-gather.2.cloned.1.call-done, s32[]{:T(128)S(6)} %select_n.18), kind=kOutput, calls=%fused_computation.15 | convolution fusion | flops 2416066560 | bytes 13926404 | tf_op jit(solution)/shard_map/dot_general | solution.py:17
  197.9 0.2 copy.15
  198.1 0.8 all_to_all.19
  198.9 5.5 %all-to-all-start.1 = ((bf16[64,4,576]{2,1,0:T(4,128)(2,1)}), bf16[64,4,576]{2,1,0:T(4,128)(2,1)S(1)}, u32[]{:S(2)}, u32[]{:S(2)}) async-start(bf16[64,4,576]{2,1,0:T(4,128)(2,1)} %all_to_all.19), calls=%async_computation.2 | async-start | bytes 655360 | tf_op jit(solution)/shard_map/all_to_all | solution.py:70
  204.5 11.8 %all-to-all-done.1 = bf16[64,4,576]{2,1,0:T(4,128)(2,1)S(1)} async-done(((bf16[64,4,576]{2,1,0:T(4,128)(2,1)}), bf16[64,4,576]{2,1,0:T(4,128)(2,1)S(1)}, u32[]{:S(2)}, u32[]{:S(2)}) %all-to-all-start.1) | async-done | bytes 294944 | tf_op jit(solution)/shard_map/all_to_all | solution.py:70
  216.2 0.2 all_to_all.21
  216.4 1.0 gather_fusion
  217.4 0.8 broadcast_select_fusion
  218.2 182.7 %reduce-scatter.2.cloned.1.call-done = f32[128,576]{0,1:T(8,128)} async-done(((f32[8192,576]{0,1:T(8,128)}), f32[128,576]{0,1:T(8,128)}) %reduce-scatter.2.cloned.1.call-update) | async-done | bytes 294928 | tf_op jit(solution)/shard_map/reduce_scatter | solution.py:69
  401.0 1.6 convert_element_type.28
  (3 shorter events, 0.0 us)
Async XLA Ops:
  7.2 9.8 %copy-start = (bf16[192,576]{1,0:T(8,128)(2,1)S(1)}, bf16[192,576]{1,0:T(8,128)(2,1)}, u32[]{:S(2)}) copy-start(bf16[192,576]{1,0:T(8,128)(2,1)} %param.6) | copy-start | bytes 663556
  7.2 160.1 %all-gather.2.cloned.1.call-start = ((), (), s32[]{:S(2)}) async-start(), calls=%async_computation.3 | async-start | bytes 19169280 | tf_op jit(solution)/shard_map/all_gather | solution.py:58
  18.3 24.7 %all-to-all-start = ((bf16[64,4,576]{2,1,0:T(4,128)(2,1)}), bf16[64,4,576]{2,1,0:T(4,128)(2,1)S(1)}, u32[]{:S(2)}, u32[]{:S(2)}) async-start(bf16[64,4,576]{2,1,0:T(4,128)(2,1)} %all_to_all.16), calls=%async_computation | async-start | bytes 655360 | tf_op jit(solution)/shard_map/all_to_all | solution.py:48
  29.4 371.5 %reduce-scatter.2.cloned.1.call-start = ((), (), s32[]{:S(2)}) async-start(), calls=%async_computation.4 | async-start | bytes 19169280 | tf_op jit(solution)/shard_map/reduce_scatter | solution.py:69
  180.4 2.0 copy-start.1
  198.9 17.3 %all-to-all-start.1 = ((bf16[64,4,576]{2,1,0:T(4,128)(2,1)}), bf16[64,4,576]{2,1,0:T(4,128)(2,1)S(1)}, u32[]{:S(2)}, u32[]{:S(2)}) async-start(bf16[64,4,576]{2,1,0:T(4,128)(2,1)} %all_to_all.19), calls=%async_computation.2 | async-start | bytes 655360 | tf_op jit(solution)/shard_map/all_to_all | solution.py:70
Sparse Core Ops, SparseCore 0:
  15.5 151.7 all-gather.1
  190.4 210.4 reduce-scatter.1
where the time goes:
time: 410 us; the launch traced here: 409 us
  waiting for transfers between devices  320 us (78%)
  matrix products  28.9 us (7%)
  blocking collectives  17.8 us (4%)
  starting transfers between devices  16.7 us (4%)
  between operations  14.1 us (3%)
  other arithmetic  6.2 us (2%)
  local copies, waits for them, and re-layouts  5.5 us (1%)
    reduce_scatter x1, waiting for transfers between devices, body(): lax.psum_scatter(image_terms, 'dp', scatter_dimension=0, tiled=True)  183 us
    all_gather x1, waiting for transfers between devices, body(): piece = lax.all_gather(images_wide, 'dp', axis=0, tiled=True)  114 us
    dot_general x1, matrix products, cross_rows(): lax.dot_general(left, right, (((1,), (1,)), ((), ())), preferred_element_...  13.1 us
    all_to_all x1, waiting for transfers between devices, body(): lax.all_to_all(text_total.astype(jnp.bfloat16), 'dp', split_axis=0, conca...  11.8 us
    all_to_all x1, waiting for transfers between devices, body(): lax.all_to_all(outgoing, 'dp', split_axis=0, concat_axis=0, tiled=True)  11.4 us
    all_to_all x1, starting transfers between devices, body(): lax.all_to_all(outgoing, 'dp', split_axis=0, concat_axis=0, tiled=True)  11.1 us
    all_gather x1, blocking collectives, body(): lax.all_gather(owned_rows, 'mp', axis=1, tiled=True)  9.74 us
  transfers between devices with their start and end apart: 4, of which 4 were waited for; matrix products, arithmetic and copies ran while one was open for 3% of the time, Pallas kernels for 0%

commit v1 on v0

v1 whole, which is shorter than its diff:
```python
import jax
import jax.numpy as jnp
from jax import lax
from jax.experimental import pallas as pl
from jax.experimental.pallas import tpu as pltpu
from jax.sharding import PartitionSpec as P


F = 576
W = 640
IMG = 128
ROWS = F + 16
HALF = 96
CAPS = 8 * HALF
IMGS = 8 * IMG
VMEM_LIMIT = 56 * 1024 * 1024


def exchange(value, move):
    pairs = []
    for source in range(128):
        xl, c, z, y, xh = source & 1, source >> 1 & 1, source >> 2 & 3, source >> 4 & 3, source >> 6
        jx, jy, jz, jc = move(c)
        x = (xh * 2 + xl) ^ jx
        target = ((((x >> 1) * 4 + (y ^ jy)) * 4 + (z ^ jz)) * 2 + (c ^ jc)) * 2 + (x & 1)
        pairs.append((source, target))
    return lax.ppermute(value, ("dp", "mp"), pairs)


def first_axis(j):
    return lambda c: (j, 0, 0, 0) if c == 0 else (0, j, 0, 0)


def second_axis(j):
    return lambda c: (0, j, 0, 0) if c == 0 else (j, 0, 0, 0)


def caption_kernel(near_ref, far_ref, rows_ref, turned_ref):
    for e, ref in enumerate((near_ref, far_ref)):
        for j in range(4):
            for h in range(2):
                rows_ref[pl.ds((e * 4 + j) * HALF, HALF), h * W : (h + 1) * W] = ref[j, h]
    for block in range(2 * W // 128):
        columns = slice(block * 128, (block + 1) * 128)
        turned_ref[columns, :] = rows_ref[:, columns].T


def main_kernel(
    place_ref, captions_ref, turned_ref, p0_ref, p1_ref, p2_ref, p3_ref,
    image_out, caption_out, images, tables, coefficient, sems,
):
    me = place_ref[0]
    c = me & 1
    copies = []
    for p2, ref in enumerate((p0_ref, p1_ref, p2_ref, p3_ref)):
        for p1 in range(4):
            jx = jnp.where(c == 0, p1, p2)
            jy = jnp.where(c == 0, p2, p1)
            h, column = jx & 1, jy * 2 + (jx >> 1)
            copies.append(
                pltpu.make_async_copy(
                    ref.at[p1, pl.ds(0, F)],
                    images.at[h, pl.ds(0, F), pl.ds(pl.multiple_of(column * IMG, IMG), IMG)],
                    sems.at[0, p2 * 4 + p1],
                )
            )
            copies.append(
                pltpu.make_async_copy(
                    ref.at[p1, pl.ds(F, 16)], tables.at[h, column], sems.at[1, p2 * 4 + p1]
                )
            )
    for copy in copies:
        copy.start()
    images[:, F:W, :] = jnp.zeros((2, W - F, IMGS), jnp.bfloat16)
    marks = captions_ref[:, 512:640].astype(jnp.float32).astype(jnp.int32)
    owner, slot = marks[:, 64:65], marks[:, 65:66]
    relative = owner ^ me
    for copy in copies:
        copy.wait()

    table = tables[0].astype(jnp.float32)
    inverse = 1.0 / table[:, 0, :]
    slots = jnp.concatenate([table[:, 1, :], table[:, 2, :]], axis=1)
    slots = jnp.concatenate([slots, jnp.zeros((120, 256), jnp.float32)], axis=0)
    picked = (lax.broadcasted_iota(jnp.int32, (CAPS, 256), 1) == slot).astype(jnp.float32)
    named = lax.dot_general(
        picked.astype(jnp.bfloat16), slots.astype(jnp.bfloat16), (((1,), (1,)), ((), ())),
        preferred_element_type=jnp.float32,
    )
    block = (relative >> 3 & 3) * 2 + (relative >> 5)
    lanes = lax.broadcasted_iota(jnp.int32, (CAPS, 128), 1)
    named = jnp.sum(jnp.where(lanes == block, named, 0.0), axis=1, keepdims=True)
    target = jnp.where((relative & 7) == 0, block * IMG + named.astype(jnp.int32), -1)

    for jy in range(4):
        columns = slice(jy * 256, (jy + 1) * 256)
        products = jnp.dot(
            captions_ref[:, :W], images[0, :, columns], preferred_element_type=jnp.float32
        ) + jnp.dot(captions_ref[:, W:], images[1, :, columns], preferred_element_type=jnp.float32)
        negative = 5.0 * jnp.tanh(5.0 * products - 1.0) + 5.0
        weight = jnp.concatenate([inverse[2 * jy : 2 * jy + 1], inverse[2 * jy + 1 : 2 * jy + 2]], axis=1)
        here = lax.broadcasted_iota(jnp.int32, (CAPS, 256), 1) + jy * 256 == target
        part = jnp.where(here, weight * (negative - 10.0), negative).astype(jnp.bfloat16)
        coefficient[:, columns] = part
        for h in range(2):
            grads = jnp.dot(
                turned_ref[h * W : h * W + F, :], part, preferred_element_type=jnp.float32
            )
            for g in range(2):
                jx = g * 2 + h
                p2 = jnp.where(c == 0, jy, jx)
                p1 = jnp.where(c == 0, jx, jy)
                image_out[p2, p1] = grads[:, g * IMG : (g + 1) * IMG]
    for h in range(2):
        for start, size in ((0, 256), (256, 256), (512, 128)):
            caption_out[:, h * W + start : h * W + start + size] = lax.dot_general(
                coefficient[...], images[h, start : start + size, :], (((1,), (1,)), ((), ())),
                preferred_element_type=jnp.float32,
            )


def body(image_emb, caption_emb, caption_count, caption_owner, pair_image):
    me = lax.axis_index("dp")
    xl = lax.axis_index("mp")

    positions = jnp.arange(192, dtype=jnp.int32)
    earlier = positions[None, :] < positions[:, None]
    same_owner = caption_owner[:, None] == caption_owner[None, :]
    rank = jnp.sum((same_owner & earlier).astype(jnp.int32), axis=1)
    slot = me * 4 + rank
    marks = jnp.stack([caption_owner, slot], axis=1).astype(jnp.bfloat16)
    rows = jnp.concatenate([caption_emb, marks, jnp.zeros((192, W - F - 2), jnp.bfloat16)], axis=1)
    kept = lax.dynamic_slice_in_dim(rows, xl * HALF, HALF, 0)
    given = lax.dynamic_slice_in_dim(rows, (1 - xl) * HALF, HALF, 0)

    extra = jnp.concatenate(
        [caption_count[None], pair_image.reshape(2, IMG), jnp.zeros((13, IMG), jnp.int32)], axis=0
    ).astype(jnp.bfloat16)
    piece = jnp.concatenate([image_emb.T, extra], axis=0)

    pieces = [piece] + [exchange(piece, first_axis(j)) for j in (1, 2, 3)]
    gained = exchange(given, lambda c: (1, 0, 0, 0))
    pieces = jnp.stack(pieces)
    groups = [pieces] + [exchange(pieces, second_axis(j)) for j in (1, 2, 3)]

    pair = jnp.stack([kept, gained])
    near = jnp.stack([pair] + [exchange(pair, lambda c, j=j: (0, 0, j, 0)) for j in (1, 2, 3)])
    far = exchange(near, lambda c: (0, 0, 0, 1))

    vmem = pl.BlockSpec(memory_space=pltpu.VMEM)
    anywhere = pl.BlockSpec(memory_space=pl.ANY)
    captions, turned = pl.pallas_call(
        caption_kernel,
        out_shape=(
            jax.ShapeDtypeStruct((CAPS, 2 * W), jnp.bfloat16),
            jax.ShapeDtypeStruct((2 * W, CAPS), jnp.bfloat16),
        ),
        in_specs=[vmem] * 2,
        out_specs=(vmem, vmem),
        compiler_params=pltpu.CompilerParams(vmem_limit_bytes=VMEM_LIMIT),
        cost_estimate=pl.CostEstimate(flops=0, bytes_accessed=8_000_000, transcendentals=0),
    )(near, far)

    image_part, caption_part = pl.pallas_call(
        main_kernel,
        out_shape=(
            jax.ShapeDtypeStruct((4, 4, F, IMG), jnp.float32),
            jax.ShapeDtypeStruct((CAPS, 2 * W), jnp.float32),
        ),
        in_specs=[pl.BlockSpec(memory_space=pltpu.SMEM), vmem, vmem] + [anywhere] * 4,
        out_specs=(vmem, vmem),
        scratch_shapes=[
            pltpu.VMEM((2, W, IMGS), jnp.bfloat16),
            pltpu.VMEM((2, 8, 16, IMG), jnp.bfloat16),
            pltpu.VMEM((CAPS, IMGS), jnp.bfloat16),
            pltpu.SemaphoreType.DMA((2, 16)),
        ],
        compiler_params=pltpu.CompilerParams(vmem_limit_bytes=VMEM_LIMIT),
        cost_estimate=pl.CostEstimate(
            flops=6 * CAPS * IMGS * 2 * W, bytes_accessed=16_000_000, transcendentals=CAPS * IMGS
        ),
    )(me[None], captions, turned, *groups)

    half = jnp.float16
    caption_part = caption_part.reshape(2, 4, HALF, 2 * W)
    crossed = exchange(caption_part[1].astype(half), lambda c: (0, 0, 0, 1))
    group_total = caption_part[0] + crossed.astype(jnp.float32)
    image_received = [
        exchange(image_part[j].astype(half), second_axis(j)) for j in (2, 1, 3)
    ]
    caption_received = [
        exchange(group_total[j].astype(half), lambda c, j=j: (0, 0, j, 0)) for j in (2, 1, 3)
    ]
    line = image_part[0]
    for value in image_received:
        line = line + value.astype(jnp.float32)
    line_received = [exchange(line[j].astype(half), first_axis(j)) for j in (2, 1, 3)]
    total = line[0]
    for value in line_received:
        total = total + value.astype(jnp.float32)
    image_grad = total.astype(jnp.bfloat16).T

    both = group_total[0]
    for value in caption_received:
        both = both + value.astype(jnp.float32)
    both = both.astype(jnp.bfloat16)
    mine, theirs = both[:, :F], both[:, W : W + F]
    returned = exchange(theirs, lambda c: (1, 0, 0, 0))
    caption_grad = jnp.where(
        xl == 0,
        jnp.concatenate([mine, returned], axis=0),
        jnp.concatenate([returned, mine], axis=0),
    )
    return image_grad, caption_grad


def solution(mesh):
    in_specs = (P("dp", "mp"), P("dp", "mp"), P("dp"), P("dp"), P("dp"))
    out_specs = (P("dp", "mp"), P("dp", "mp"))
    return jax.shard_map(body, mesh=mesh, in_specs=in_specs, out_specs=out_specs, check_vma=False)
```

time: 410 us -> 109 us (0.27)
  waiting for transfers between devices: 320 us -> 41.6 us
  matrix products: 28.9 us -> 0 us
  Pallas kernels: 0 us -> 21.4 us
  blocking collectives: 17.8 us -> 0 us
  between operations: 14.1 us -> 0.86 us
  starting transfers between devices: 16.7 us -> 29.6 us
  other arithmetic: 6.2 us -> 12.8 us
    reduce_scatter x1 -> x0, waiting for transfers between devices: 183 us -> none  [body(): lax.psum_scatter(image_terms, 'dp', scatter_dimension=0, tiled=True)]
    all_gather x1 -> x0, waiting for transfers between devices: 114 us -> none  [body(): piece = lax.all_gather(images_wide, 'dp', axis=0, tiled=True)]
    ppermute x0 -> x22, waiting for transfers between devices: none -> 41.6 us  [exchange(): return lax.ppermute(value, ('dp', 'mp'), pairs)]
    ppermute x0 -> x22, starting transfers between devices: none -> 29.6 us  [exchange(): return lax.ppermute(value, ('dp', 'mp'), pairs)]
    dot_general x4 -> x0, matrix products: 28.9 us -> none  [the longest x1 13.1 us: cross_rows(): lax.dot_general(left, right, (((1,), (1,)), ((), ())), preferred_element_...]
    all_to_all x2 -> x0, waiting for transfers between devices: 23.2 us -> none  [the longest x1 11.8 us: body(): lax.all_to_all(text_total.astype(jnp.bfloat16), 'dp', split_axis=0, conca...]
    pallas_call x0 -> x2, Pallas kernels: none -> 21.4 us  [the longest x1 17.5 us: body(): pl.pallas_call(main_kernel, out_shape=(jax.ShapeDtypeStruct((4, 4, F, IMG...]
    all_gather x2 -> x0, blocking collectives: 17.8 us -> none  [the longest x1 9.74 us: body(): lax.all_gather(owned_rows, 'mp', axis=1, tiled=True)]
  transfers between devices with their start and end apart: 4 -> 22, of which waited for: 4 -> 15; matrix products, arithmetic and copies ran while one was open for 3% -> 6% of each run, Pallas kernels for 0% -> 4%
where the time goes in v1:
time: 109 us
  waiting for transfers between devices  41.6 us (38%)
  starting transfers between devices  29.6 us (27%)
  Pallas kernels  21.4 us (20%)
  other arithmetic  12.8 us (12%)
  local copies, waits for them, and re-layouts  2.77 us (3%)
    ppermute x22, waiting for transfers between devices, exchange(): return lax.ppermute(value, ('dp', 'mp'), pairs)  41.6 us
    ppermute x22, starting transfers between devices, exchange(): return lax.ppermute(value, ('dp', 'mp'), pairs)  29.6 us
    pallas_call x1, Pallas kernels, body(): pl.pallas_call(main_kernel, out_shape=(jax.ShapeDtypeStruct((4, 4, F, IMG...  17.5 us
    another operation x6, other arithmetic  8.71 us
    pallas_call x1, Pallas kernels, body(): pl.pallas_call(caption_kernel, out_shape=(jax.ShapeDtypeStruct((CAPS, 2 *...  3.86 us
  transfers between devices with their start and end apart: 22, of which 15 were waited for; matrix products, arithmetic and copies ran while one was open for 6% of the time, Pallas kernels for 4%

profile of v1, /device:TPU:0, one launch (start us, length us, event | category | flops | bytes accessed | tf_op | source)
XLA Modules:
  0.0 109.0 jit_solution(7295514478087576327)
XLA Ops:
  0.7 0.7 convert.36
  1.3 0.9 convert_reduce_fusion
  2.6 1.0 maximum_maximum_fusion
  3.7 1.7 %collective-permute-start = (bf16[96,640]{1,0:T(8,128)(2,1)S(1)}, bf16[96,640]{1,0:T(8,128)(2,1)S(1)}, u32[]{:S(2)}, u32[]{:S(2)}) collective-permute-start(bf16[96,640]{1,0:T(8,128)(2,1)S(1)} %get-tuple-element.30), channel_id=1, source_target_pairs={{0,1},{1,0},{2,3},{3,2},{4,5},{5,4},{6,7},{7,6},{8,9},{9,8},{10,11... | collective-permute-start | bytes 368648 | tf_op jit(solution)/shard_map/ppermute | solution.py:27
  5.3 3.3 %collective-permute-done = bf16[96,640]{1,0:T(8,128)(2,1)S(1)} collective-permute-done((bf16[96,640]{1,0:T(8,128)(2,1)S(1)}, bf16[96,640]{1,0:T(8,128)(2,1)S(1)}, u32[]{:S(2)}, u32[]{:S(2)}) %collective-permute-start) | collective-permute-done | bytes 122912 | tf_op jit(solution)/shard_map/ppermute | solution.py:27
  8.7 4.2 %collective-permute-start.2 = (bf16[2,96,640]{2,1,0:T(8,128)(2,1)S(1)}, bf16[2,96,640]{2,1,0:T(8,128)(2,1)S(1)}, u32[]{:S(2)}, u32[]{:S(2)}) collective-permute-start(bf16[2,96,640]{2,1,0:T(8,128)(2,1)S(1)} %get-tuple-element.28), channel_id=1, source_target_pairs={{0,8},{1,9},{2,10},{3,11},{4,12},{5,13},{6,14},{7,15},{8,0},{9,1},... | collective-permute-start | bytes 737288 | tf_op jit(solution)/shard_map/ppermute | solution.py:27
  12.9 1.0 collective-permute-start.1
  14.0 5.7 %collective-permute-done.2 = bf16[2,96,640]{2,1,0:T(8,128)(2,1)S(1)} collective-permute-done((bf16[2,96,640]{2,1,0:T(8,128)(2,1)S(1)}, bf16[2,96,640]{2,1,0:T(8,128)(2,1)S(1)}, u32[]{:S(2)}, u32[]{:S(2)}) %collective-permute-start.2) | collective-permute-done | bytes 245792 | tf_op jit(solution)/shard_map/ppermute | solution.py:27
  19.8 4.3 %collective-permute-done.1 = bf16[2,96,640]{2,1,0:T(8,128)(2,1)S(1)} collective-permute-done((bf16[2,96,640]{2,1,0:T(8,128)(2,1)S(1)}, bf16[2,96,640]{2,1,0:T(8,128)(2,1)S(1)}, u32[]{:S(2)}, u32[]{:S(2)}) %collective-permute-start.1) | collective-permute-done | bytes 245792 | tf_op jit(solution)/shard_map/ppermute | solution.py:27
  24.0 0.1 pad_maximum_fusion.near_ref
  24.4 3.1 %collective-permute-start.6 = (bf16[592,128]{1,0:T(8,128)(2,1)S(1)}, bf16[592,128]{1,0:T(8,128)(2,1)S(1)}, u32[]{:S(2)}, u32[]{:S(2)}) collective-permute-start(bf16[592,128]{1,0:T(8,128)(2,1)S(1)} %maximum_maximum_fusion.1), channel_id=1, source_target_pairs={{0,64},{1,65},{2,34},{3,35},{4,68},{5,69},{6,38},{7,39},{8,72},{9,... | collective-permute-start | bytes 454664 | tf_op jit(solution)/shard_map/ppermute | solution.py:27
  27.6 0.6 collective-permute-start.5
  28.1 0.6 collective-permute-start.7
  28.8 2.4 %collective-permute-done.6 = bf16[592,128]{1,0:T(8,128)(2,1)S(1)} collective-permute-done((bf16[592,128]{1,0:T(8,128)(2,1)S(1)}, bf16[592,128]{1,0:T(8,128)(2,1)S(1)}, u32[]{:S(2)}, u32[]{:S(2)}) %collective-permute-start.6) | collective-permute-done | bytes 151584 | tf_op jit(solution)/shard_map/ppermute | solution.py:27
  31.2 1.7 %collective-permute-done.5 = bf16[592,128]{1,0:T(8,128)(2,1)S(1)} collective-permute-done((bf16[592,128]{1,0:T(8,128)(2,1)S(1)}, bf16[592,128]{1,0:T(8,128)(2,1)S(1)}, u32[]{:S(2)}, u32[]{:S(2)}) %collective-permute-start.5) | collective-permute-done | bytes 151584 | tf_op jit(solution)/shard_map/ppermute | solution.py:27
  32.9 1.6 %collective-permute-done.7 = bf16[592,128]{1,0:T(8,128)(2,1)S(1)} collective-permute-done((bf16[592,128]{1,0:T(8,128)(2,1)S(1)}, bf16[592,128]{1,0:T(8,128)(2,1)S(1)}, u32[]{:S(2)}, u32[]{:S(2)}) %collective-permute-start.7) | collective-permute-done | bytes 151584 | tf_op jit(solution)/shard_map/ppermute | solution.py:27
  34.6 3.1 %collective-permute-start.10 = (bf16[4,592,128]{2,1,0:T(8,128)(2,1)S(1)}, bf16[4,592,128]{2,1,0:T(8,128)(2,1)S(1)}, u32[]{:S(2)}, u32[]{:S(2)}) collective-permute-start(bf16[4,592,128]{2,1,0:T(8,128)(2,1)S(1)} %pad_maximum_fusion.1.p0_ref), channel_id=1, source_target_pairs={{0,48},{1,49},{2,67},{3,66},{4,52},{5,53},{6,71},{7,70},{8,56},{9,... | collective-permute-start | bytes 1818632 | tf_op jit(solution)/shard_map/ppermute | solution.py:27
  37.7 0.6 collective-permute-start.9
  38.4 0.5 collective-permute-start.8
  38.8 0.9 copy-done.1
  39.8 3.9 %shard_map.68 = (bf16[768,1280]{1,0:T(8,128)(2,1)}, bf16[1280,768]{1,0:T(8,128)(2,1)}) custom-call(bf16[4,2,96,640]{3,2,1,0:T(8,128)(2,1)} %copy-done, bf16[4,2,96,640]{3,2,1,0:T(8,128)(2,1)} %copy-done.1), custom_call_target="tpu_custom_call" | custom-call | bytes 8000000 | tf_op jit(solution)/shard_map/pallas_call | solution.py:152
  43.6 8.9 %collective-permute-done.10.p3_ref = bf16[4,592,128]{2,1,0:T(8,128)(2,1)S(1)} collective-permute-done((bf16[4,592,128]{2,1,0:T(8,128)(2,1)S(1)}, bf16[4,592,128]{2,1,0:T(8,128)(2,1)S(1)}, u32[]{:S(2)}, u32[]{:S(2)}) %collective-permute-start.10) | collective-permute-done | bytes 606240 | tf_op jit(solution)/shard_map/ppermute | solution.py:27
  52.5 0.9 collective-permute-done.8.p1_ref
  53.5 0.7 copy-done.6
  54.2 17.5 %shard_map.69 = (f32[4,4,576,128]{3,2,1,0:T(8,128)}, f32[768,1280]{1,0:T(8,128)}) custom-call(s32[1]{0:T(128)} %bitcast.place_ref, bf16[768,1280]{1,0:T(8,128)(2,1)} %get-tuple-element.6.captions_ref, bf16[1280,768]{1,0:T(8,128)(2,1)} %get-tuple-element.7.turned_ref, bf16[4,592,128]{2,1,0:T(8,128)(2,1)} %copy-done.2, bf16[4,592,128]{2,1,0:T(8,128)(2,1)} %copy-done.6, ...), custom_call_target="tpu_custom_call" | custom-call | flops 6039797760 | bytes 16000000 | tf_op jit(solution)/shard_map/pallas_call | solution.py:164
  71.7 3.3 %slice_convert_fusion = (f16[384,1280]{1,0:T(8,128)(2,1)}, f32[384,1280]{1,0:T(8,128)S(1)}) fusion(f32[768,1280]{1,0:T(8,128)} %get-tuple-element.9), kind=kLoop, calls=%fused_computation | loop fusion | flops 491520 | bytes 6881280 | tf_op jit(solution)/shard_map/convert.3
  75.0 2.8 %convert.40 = f16[4,4,576,128]{3,2,1,0:T(8,128)(2,1)S(1)} convert(f32[4,4,576,128]{3,2,1,0:T(8,128)} %get-tuple-element.8) | non-fusion elementwise | flops 1179648 | bytes 7077888 | tf_op jit(solution)/shard_map/convert.9
  77.9 0.3 slice_bitcast_fusion.2
  78.2 3.3 %collective-permute-start.11 = (f16[4,576,128]{2,1,0:T(8,128)(2,1)S(1)}, f16[4,576,128]{2,1,0:T(8,128)(2,1)S(1)}, u32[]{:S(2)}, u32[]{:S(2)}) collective-permute-start(f16[4,576,128]{2,1,0:T(8,128)(2,1)S(1)} %get-tuple-element.16), channel_id=1, source_target_pairs={{0,32},{1,33},{2,66},{3,67},{4,36},{5,37},{6,70},{7,71},{8,40},{9,... | collective-permute-start | bytes 1769480 | tf_op jit(solution)/shard_map/ppermute | solution.py:27
  81.5 1.1 collective-permute-start.13
  82.6 0.3 fusion.13
  83.0 2.5 %collective-permute-start.18 = (f16[96,1280]{1,0:T(8,128)(2,1)S(1)}, f16[96,1280]{1,0:T(8,128)(2,1)S(1)}, u32[]{:S(2)}, u32[]{:S(2)}) collective-permute-start(f16[96,1280]{1,0:T(8,128)(2,1)S(1)} %get-tuple-element.19), channel_id=1, source_target_pairs={{0,8},{1,9},{2,10},{3,11},{4,12},{5,13},{6,14},{7,15},{8,0},{9,1},... | collective-permute-start | bytes 737288 | tf_op jit(solution)/shard_map/ppermute | solution.py:27
  85.5 1.2 %collective-permute-start.20 = (f16[96,1280]{1,0:T(8,128)(2,1)S(1)}, f16[96,1280]{1,0:T(8,128)(2,1)S(1)}, u32[]{:S(2)}, u32[]{:S(2)}) collective-permute-start(f16[96,1280]{1,0:T(8,128)(2,1)S(1)} %get-tuple-element.20), channel_id=1, source_target_pairs={{0,12},{1,13},{2,14},{3,15},{4,8},{5,9},{6,10},{7,11},{8,4},{9,5},... | collective-permute-start | bytes 737288 | tf_op jit(solution)/shard_map/ppermute | solution.py:27
  86.7 3.1 %collective-permute-done.11 = f16[4,576,128]{2,1,0:T(8,128)(2,1)S(1)} collective-permute-done((f16[4,576,128]{2,1,0:T(8,128)(2,1)S(1)}, f16[4,576,128]{2,1,0:T(8,128)(2,1)S(1)}, u32[]{:S(2)}, u32[]{:S(2)}) %collective-permute-start.11) | collective-permute-done | bytes 589856 | tf_op jit(solution)/shard_map/ppermute | solution.py:27
  89.8 1.0 collective-permute-start.19
  90.8 5.2 %collective-permute-done.13 = f16[4,576,128]{2,1,0:T(8,128)(2,1)S(1)} collective-permute-done((f16[4,576,128]{2,1,0:T(8,128)(2,1)S(1)}, f16[4,576,128]{2,1,0:T(8,128)(2,1)S(1)}, u32[]{:S(2)}, u32[]{:S(2)}) %collective-permute-start.13) | collective-permute-done | bytes 589856 | tf_op jit(solution)/shard_map/ppermute | solution.py:27
  96.0 0.4 collective-permute-done.12
  96.4 1.6 %fusion.14 = (f16[4,576,128]{2,1,0:T(8,128)(2,1)S(1)}, f32[4,576,128]{2,1,0:T(8,128)S(1)}) fusion(f16[4,576,128]{2,1,0:T(8,128)(2,1)S(1)} %collective-permute-done.13, f16[4,576,128]{2,1,0:T(8,128)(2,1)S(1)} %collective-permute-done.12, f16[4,576,128]{2,1,0:T(8,128)(2,1)S(1)} %collective-permute-done.11, f32[4,4,576,128]{3,2,1,0:T(8,128)} %get-tuple-element.8), kind=kLoop, calls=%fused_computation.41 | loop fusion | flops 2064384 | bytes 4718592 | tf_op jit(solution)/shard_map/convert.6
  98.1 1.4 %collective-permute-start.14 = (f16[576,128]{1,0:T(8,128)(2,1)S(1)}, f16[576,128]{1,0:T(8,128)(2,1)S(1)}, u32[]{:S(2)}, u32[]{:S(2)}) collective-permute-start(f16[576,128]{1,0:T(8,128)(2,1)S(1)} %get-tuple-element.22), channel_id=1, source_target_pairs={{0,64},{1,65},{2,34},{3,35},{4,68},{5,69},{6,38},{7,39},{8,72},{9,... | collective-permute-start | bytes 442376 | tf_op jit(solution)/shard_map/ppermute | solution.py:27
  99.5 1.6 %collective-permute-start.16 = (f16[576,128]{1,0:T(8,128)(2,1)S(1)}, f16[576,128]{1,0:T(8,128)(2,1)S(1)}, u32[]{:S(2)}, u32[]{:S(2)}) collective-permute-start(f16[576,128]{1,0:T(8,128)(2,1)S(1)} %get-tuple-element.23), channel_id=1, source_target_pairs={{0,65},{1,64},{2,50},{3,51},{4,69},{5,68},{6,54},{7,55},{8,73},{9,... | collective-permute-start | bytes 442376 | tf_op jit(solution)/shard_map/ppermute | solution.py:27
  101.1 0.6 collective-permute-start.15
  101.9 1.5 %collective-permute-start.21 = (bf16[96,576]{1,0:T(8,128)(2,1)S(1)}, bf16[96,576]{1,0:T(8,128)(2,1)S(1)}, u32[]{:S(2)}, u32[]{:S(2)}) collective-permute-start(bf16[96,576]{1,0:T(8,128)(2,1)S(1)} %get-tuple-element.26), channel_id=1, source_target_pairs={{0,1},{1,0},{2,3},{3,2},{4,5},{5,4},{6,7},{7,6},{8,9},{9,8},{10,11... | collective-permute-start | bytes 331784 | tf_op jit(solution)/shard_map/ppermute | solution.py:27
  103.4 1.8 %collective-permute-done.14 = f16[576,128]{1,0:T(8,128)(2,1)S(1)} collective-permute-done((f16[576,128]{1,0:T(8,128)(2,1)S(1)}, f16[576,128]{1,0:T(8,128)(2,1)S(1)}, u32[]{:S(2)}, u32[]{:S(2)}) %collective-permute-start.14) | collective-permute-done | bytes 147488 | tf_op jit(solution)/shard_map/ppermute | solution.py:27
  105.2 1.3 %collective-permute-done.16 = f16[576,128]{1,0:T(8,128)(2,1)S(1)} collective-permute-done((f16[576,128]{1,0:T(8,128)(2,1)S(1)}, f16[576,128]{1,0:T(8,128)(2,1)S(1)}, u32[]{:S(2)}, u32[]{:S(2)}) %collective-permute-start.16) | collective-permute-done | bytes 147488 | tf_op jit(solution)/shard_map/ppermute | solution.py:27
  106.4 0.5 collective-permute-done.15
  106.9 0.7 fusion.11
  107.6 0.6 collective-permute-done.21
  108.2 0.7 maximum_select_fusion
  (45 shorter events, 1.4 us)
Async XLA Ops:
  0.6 13.3 %copy-start.8 = (s32[128]{0:T(128)S(1)}, s32[128]{0:T(128)}, u32[]{:S(2)}) copy-start(s32[128]{0:T(128)} %param.7) | copy-start | bytes 1540
  0.6 13.4 %copy-start.7 = (s32[256]{0:T(256)S(1)}, s32[256]{0:T(256)}, u32[]{:S(2)}) copy-start(s32[256]{0:T(256)} %param.9) | copy-start | bytes 3076
  1.3 22.9 %copy-start.3 = (bf16[128,576]{0,1:T(8,128)(2,1)S(1)}, bf16[128,576]{0,1:T(8,128)(2,1)}, u32[]{:S(2)}) copy-start(bf16[128,576]{0,1:T(8,128)(2,1)} %param.5) | copy-start | bytes 442372
  3.7 5.0 %collective-permute-start = (bf16[96,640]{1,0:T(8,128)(2,1)S(1)}, bf16[96,640]{1,0:T(8,128)(2,1)S(1)}, u32[]{:S(2)}, u32[]{:S(2)}) collective-permute-start(bf16[96,640]{1,0:T(8,128)(2,1)S(1)} %get-tuple-element.30), channel_id=1, source_target_pairs={{0,1},{1,0},{2,3},{3,2},{4,5},{5,4},{6,7},{7,6},{8,9},{9,8},{10,11... | collective-permute-start | bytes 368648 | tf_op jit(solution)/shard_map/ppermute | solution.py:27
  8.7 11.1 %collective-permute-start.2 = (bf16[2,96,640]{2,1,0:T(8,128)(2,1)S(1)}, bf16[2,96,640]{2,1,0:T(8,128)(2,1)S(1)}, u32[]{:S(2)}, u32[]{:S(2)}) collective-permute-start(bf16[2,96,640]{2,1,0:T(8,128)(2,1)S(1)} %get-tuple-element.28), channel_id=1, source_target_pairs={{0,8},{1,9},{2,10},{3,11},{4,12},{5,13},{6,14},{7,15},{8,0},{9,1},... | collective-permute-start | bytes 737288 | tf_op jit(solution)/shard_map/ppermute | solution.py:27
  12.9 11.1 %collective-permute-start.1 = (bf16[2,96,640]{2,1,0:T(8,128)(2,1)S(1)}, bf16[2,96,640]{2,1,0:T(8,128)(2,1)S(1)}, u32[]{:S(2)}, u32[]{:S(2)}) collective-permute-start(bf16[2,96,640]{2,1,0:T(8,128)(2,1)S(1)} %get-tuple-element.28), channel_id=1, source_target_pairs={{0,4},{1,5},{2,6},{3,7},{4,0},{5,1},{6,2},{7,3},{8,12},{9,13},{10,... | collective-permute-start | bytes 737288 | tf_op jit(solution)/shard_map/ppermute | solution.py:27
  13.9 10.1 %collective-permute-start.3 = (bf16[2,96,640]{2,1,0:T(8,128)(2,1)S(1)}, bf16[2,96,640]{2,1,0:T(8,128)(2,1)S(1)}, u32[]{:S(2)}, u32[]{:S(2)}) collective-permute-start(bf16[2,96,640]{2,1,0:T(8,128)(2,1)S(1)} %get-tuple-element.28), channel_id=1, source_target_pairs={{0,12},{1,13},{2,14},{3,15},{4,8},{5,9},{6,10},{7,11},{8,4},{9,5},... | collective-permute-start | bytes 737288 | tf_op jit(solution)/shard_map/ppermute | solution.py:27
  24.2 14.6 %copy-start = (bf16[4,2,96,640]{3,2,1,0:T(8,128)(2,1)}, bf16[4,2,96,640]{3,2,1,0:T(8,128)(2,1)S(1)}, u32[]{:S(2)}) copy-start(bf16[4,2,96,640]{3,2,1,0:T(8,128)(2,1)S(1)} %pad_maximum_fusion.near_ref) | copy-start | bytes 2949124
  24.2 14.6 %collective-permute-start.4 = (bf16[4,2,96,640]{3,2,1,0:T(8,128)(2,1)S(1)}, bf16[4,2,96,640]{3,2,1,0:T(8,128)(2,1)S(1)}, u32[]{:S(2)}, u32[]{:S(2)}) collective-permute-start(bf16[4,2,96,640]{3,2,1,0:T(8,128)(2,1)S(1)} %pad_maximum_fusion.near_ref), channel_id=1, source_target_pairs={{0,2},{1,3},{2,0},{3,1},{4,6},{5,7},{6,4},{7,5},{8,10},{9,11},{10,... | collective-permute-start | bytes 2949128 | tf_op jit(solution)/shard_map/ppermute | solution.py:27
  24.4 6.8 %collective-permute-start.6 = (bf16[592,128]{1,0:T(8,128)(2,1)S(1)}, bf16[592,128]{1,0:T(8,128)(2,1)S(1)}, u32[]{:S(2)}, u32[]{:S(2)}) collective-permute-start(bf16[592,128]{1,0:T(8,128)(2,1)S(1)} %maximum_maximum_fusion.1), channel_id=1, source_target_pairs={{0,64},{1,65},{2,34},{3,35},{4,68},{5,69},{6,38},{7,39},{8,72},{9,... | collective-permute-start | bytes 454664 | tf_op jit(solution)/shard_map/ppermute | solution.py:27
  27.6 5.4 %collective-permute-start.5 = (bf16[592,128]{1,0:T(8,128)(2,1)S(1)}, bf16[592,128]{1,0:T(8,128)(2,1)S(1)}, u32[]{:S(2)}, u32[]{:S(2)}) collective-permute-start(bf16[592,128]{1,0:T(8,128)(2,1)S(1)} %maximum_maximum_fusion.1), channel_id=1, source_target_pairs={{0,1},{1,0},{2,18},{3,19},{4,5},{5,4},{6,22},{7,23},{8,9},{9,8},{1... | collective-permute-start | bytes 454664 | tf_op jit(solution)/shard_map/ppermute | solution.py:27
  28.1 6.4 %collective-permute-start.7 = (bf16[592,128]{1,0:T(8,128)(2,1)S(1)}, bf16[592,128]{1,0:T(8,128)(2,1)S(1)}, u32[]{:S(2)}, u32[]{:S(2)}) collective-permute-start(bf16[592,128]{1,0:T(8,128)(2,1)S(1)} %maximum_maximum_fusion.1), channel_id=1, source_target_pairs={{0,65},{1,64},{2,50},{3,51},{4,69},{5,68},{6,54},{7,55},{8,73},{9,... | collective-permute-start | bytes 454664 | tf_op jit(solution)/shard_map/ppermute | solution.py:27
  34.6 18.8 %copy-start.2 = (bf16[4,592,128]{2,1,0:T(8,128)(2,1)}, bf16[4,592,128]{2,1,0:T(8,128)(2,1)S(1)}, u32[]{:S(2)}) copy-start(bf16[4,592,128]{2,1,0:T(8,128)(2,1)S(1)} %pad_maximum_fusion.1.p0_ref) | copy-start | bytes 1818628
  34.6 17.8 %collective-permute-start.10 = (bf16[4,592,128]{2,1,0:T(8,128)(2,1)S(1)}, bf16[4,592,128]{2,1,0:T(8,128)(2,1)S(1)}, u32[]{:S(2)}, u32[]{:S(2)}) collective-permute-start(bf16[4,592,128]{2,1,0:T(8,128)(2,1)S(1)} %pad_maximum_fusion.1.p0_ref), channel_id=1, source_target_pairs={{0,48},{1,49},{2,67},{3,66},{4,52},{5,53},{6,71},{7,70},{8,56},{9,... | collective-permute-start | bytes 1818632 | tf_op jit(solution)/shard_map/ppermute | solution.py:27
  37.7 14.8 %collective-permute-start.9 = (bf16[4,592,128]{2,1,0:T(8,128)(2,1)S(1)}, bf16[4,592,128]{2,1,0:T(8,128)(2,1)S(1)}, u32[]{:S(2)}, u32[]{:S(2)}) collective-permute-start(bf16[4,592,128]{2,1,0:T(8,128)(2,1)S(1)} %pad_maximum_fusion.1.p0_ref), channel_id=1, source_target_pairs={{0,32},{1,33},{2,66},{3,67},{4,36},{5,37},{6,70},{7,71},{8,40},{9,... | collective-permute-start | bytes 1818632 | tf_op jit(solution)/shard_map/ppermute | solution.py:27
  38.4 15.0 %collective-permute-start.8 = (bf16[4,592,128]{2,1,0:T(8,128)(2,1)S(1)}, bf16[4,592,128]{2,1,0:T(8,128)(2,1)S(1)}, u32[]{:S(2)}, u32[]{:S(2)}) collective-permute-start(bf16[4,592,128]{2,1,0:T(8,128)(2,1)S(1)} %pad_maximum_fusion.1.p0_ref), channel_id=1, source_target_pairs={{0,16},{1,17},{2,3},{3,2},{4,20},{5,21},{6,7},{7,6},{8,24},{9,25},... | collective-permute-start | bytes 1818632 | tf_op jit(solution)/shard_map/ppermute | solution.py:27
  38.8 0.9 copy-start.1
  52.5 0.9 copy-start.4
  52.5 1.0 copy-start.5
  53.4 0.8 copy-start.6
  75.0 7.5 %collective-permute-start.17 = (f16[4,96,1280]{2,1,0:T(8,128)(2,1)}, f16[4,96,1280]{2,1,0:T(8,128)(2,1)S(1)}, u32[]{:S(2)}, u32[]{:S(2)}) collective-permute-start(f16[4,96,1280]{2,1,0:T(8,128)(2,1)} %bitcast.24), channel_id=1, source_target_pairs={{0,2},{1,3},{2,0},{3,1},{4,6},{5,7},{6,4},{7,5},{8,10},{9,11},{10,... | collective-permute-start | bytes 2949128 | tf_op jit(solution)/shard_map/ppermute | solution.py:27
  78.2 11.6 %collective-permute-start.11 = (f16[4,576,128]{2,1,0:T(8,128)(2,1)S(1)}, f16[4,576,128]{2,1,0:T(8,128)(2,1)S(1)}, u32[]{:S(2)}, u32[]{:S(2)}) collective-permute-start(f16[4,576,128]{2,1,0:T(8,128)(2,1)S(1)} %get-tuple-element.16), channel_id=1, source_target_pairs={{0,32},{1,33},{2,66},{3,67},{4,36},{5,37},{6,70},{7,71},{8,40},{9,... | collective-permute-start | bytes 1769480 | tf_op jit(solution)/shard_map/ppermute | solution.py:27
  81.5 14.5 %collective-permute-start.13 = (f16[4,576,128]{2,1,0:T(8,128)(2,1)S(1)}, f16[4,576,128]{2,1,0:T(8,128)(2,1)S(1)}, u32[]{:S(2)}, u32[]{:S(2)}) collective-permute-start(f16[4,576,128]{2,1,0:T(8,128)(2,1)S(1)} %get-tuple-element.17), channel_id=1, source_target_pairs={{0,48},{1,49},{2,67},{3,66},{4,52},{5,53},{6,71},{7,70},{8,56},{9,... | collective-permute-start | bytes 1769480 | tf_op jit(solution)/shard_map/ppermute | solution.py:27
  82.6 13.8 %collective-permute-start.12 = (f16[4,576,128]{2,1,0:T(8,128)(2,1)S(1)}, f16[4,576,128]{2,1,0:T(8,128)(2,1)S(1)}, u32[]{:S(2)}, u32[]{:S(2)}) collective-permute-start(f16[4,576,128]{2,1,0:T(8,128)(2,1)S(1)} %get-tuple-element.18), channel_id=1, source_target_pairs={{0,16},{1,17},{2,3},{3,2},{4,20},{5,21},{6,7},{7,6},{8,24},{9,25},... | collective-permute-start | bytes 1769480 | tf_op jit(solution)/shard_map/ppermute | solution.py:27
  83.0 18.1 %collective-permute-start.18 = (f16[96,1280]{1,0:T(8,128)(2,1)S(1)}, f16[96,1280]{1,0:T(8,128)(2,1)S(1)}, u32[]{:S(2)}, u32[]{:S(2)}) collective-permute-start(f16[96,1280]{1,0:T(8,128)(2,1)S(1)} %get-tuple-element.19), channel_id=1, source_target_pairs={{0,8},{1,9},{2,10},{3,11},{4,12},{5,13},{6,14},{7,15},{8,0},{9,1},... | collective-permute-start | bytes 737288 | tf_op jit(solution)/shard_map/ppermute | solution.py:27
  85.5 16.2 %collective-permute-start.20 = (f16[96,1280]{1,0:T(8,128)(2,1)S(1)}, f16[96,1280]{1,0:T(8,128)(2,1)S(1)}, u32[]{:S(2)}, u32[]{:S(2)}) collective-permute-start(f16[96,1280]{1,0:T(8,128)(2,1)S(1)} %get-tuple-element.20), channel_id=1, source_target_pairs={{0,12},{1,13},{2,14},{3,15},{4,8},{5,9},{6,10},{7,11},{8,4},{9,5},... | collective-permute-start | bytes 737288 | tf_op jit(solution)/shard_map/ppermute | solution.py:27
  89.8 11.9 %collective-permute-start.19 = (f16[96,1280]{1,0:T(8,128)(2,1)S(1)}, f16[96,1280]{1,0:T(8,128)(2,1)S(1)}, u32[]{:S(2)}, u32[]{:S(2)}) collective-permute-start(f16[96,1280]{1,0:T(8,128)(2,1)S(1)} %get-tuple-element.21), channel_id=1, source_target_pairs={{0,4},{1,5},{2,6},{3,7},{4,0},{5,1},{6,2},{7,3},{8,12},{9,13},{10,... | collective-permute-start | bytes 737288 | tf_op jit(solution)/shard_map/ppermute | solution.py:27
  98.1 7.0 %collective-permute-start.14 = (f16[576,128]{1,0:T(8,128)(2,1)S(1)}, f16[576,128]{1,0:T(8,128)(2,1)S(1)}, u32[]{:S(2)}, u32[]{:S(2)}) collective-permute-start(f16[576,128]{1,0:T(8,128)(2,1)S(1)} %get-tuple-element.22), channel_id=1, source_target_pairs={{0,64},{1,65},{2,34},{3,35},{4,68},{5,69},{6,38},{7,39},{8,72},{9,... | collective-permute-start | bytes 442376 | tf_op jit(solution)/shard_map/ppermute | solution.py:27
  99.5 6.9 %collective-permute-start.16 = (f16[576,128]{1,0:T(8,128)(2,1)S(1)}, f16[576,128]{1,0:T(8,128)(2,1)S(1)}, u32[]{:S(2)}, u32[]{:S(2)}) collective-permute-start(f16[576,128]{1,0:T(8,128)(2,1)S(1)} %get-tuple-element.23), channel_id=1, source_target_pairs={{0,65},{1,64},{2,50},{3,51},{4,69},{5,68},{6,54},{7,55},{8,73},{9,... | collective-permute-start | bytes 442376 | tf_op jit(solution)/shard_map/ppermute | solution.py:27
  101.1 5.8 %collective-permute-start.15 = (f16[576,128]{1,0:T(8,128)(2,1)S(1)}, f16[576,128]{1,0:T(8,128)(2,1)S(1)}, u32[]{:S(2)}, u32[]{:S(2)}) collective-permute-start(f16[576,128]{1,0:T(8,128)(2,1)S(1)} %get-tuple-element.24), channel_id=1, source_target_pairs={{0,1},{1,0},{2,18},{3,19},{4,5},{5,4},{6,22},{7,23},{8,9},{9,8},{1... | collective-permute-start | bytes 442376 | tf_op jit(solution)/shard_map/ppermute | solution.py:27
  101.9 6.4 %collective-permute-start.21 = (bf16[96,576]{1,0:T(8,128)(2,1)S(1)}, bf16[96,576]{1,0:T(8,128)(2,1)S(1)}, u32[]{:S(2)}, u32[]{:S(2)}) collective-permute-start(bf16[96,576]{1,0:T(8,128)(2,1)S(1)} %get-tuple-element.26), channel_id=1, source_target_pairs={{0,1},{1,0},{2,3},{3,2},{4,5},{5,4},{6,7},{7,6},{8,9},{9,8},{10,11... | collective-permute-start | bytes 331784 | tf_op jit(solution)/shard_map/ppermute | solution.py:27

commit v2 on v1

v2 whole, which is shorter than its diff:
```python
import functools

import jax
import jax.numpy as jnp
from jax import lax
from jax.experimental import pallas as pl
from jax.experimental.pallas import tpu as pltpu
from jax.sharding import PartitionSpec as P


F = 576
W = 640
IMG = 128
ROWS = F + 16
LOAD = 192
HALF = 96
CAPS = 8 * HALF
COLS = 4 * IMG


def exchange(value, move):
    pairs = []
    for source in range(128):
        xl, c, z, y, xh = source & 1, source >> 1 & 1, source >> 2 & 3, source >> 4 & 3, source >> 6
        jx, jy, jz, jc = move(c)
        x = (xh * 2 + xl) ^ jx
        target = ((((x >> 1) * 4 + (y ^ jy)) * 4 + (z ^ jz)) * 2 + (c ^ jc)) * 2 + (x & 1)
        pairs.append((source, target))
    return lax.ppermute(value, ("dp", "mp"), pairs)


def first_axis(j):
    return lambda c: (j, 0, 0, 0) if c == 0 else (0, j, 0, 0)


def second_axis(j):
    return lambda c: (0, j, 0, 0) if c == 0 else (j, 0, 0, 0)


def along_z(j):
    return lambda c: (0, 0, j, 0)


def other_half(c):
    return (1, 0, 0, 0)


def other_core(c):
    return (0, 0, 0, 1)


def join_kernel(piece_ref, r1_ref, r2_ref, r3_ref, kept_ref, gained_ref, pieces_ref, pair_ref):
    for i, ref in enumerate((piece_ref, r1_ref, r2_ref, r3_ref)):
        pieces_ref[i] = ref[...]
    pair_ref[0] = kept_ref[...]
    pair_ref[1] = gained_ref[...]


def near_kernel(pair_ref, r1_ref, r2_ref, r3_ref, _a, _b, near_ref):
    for i, ref in enumerate((pair_ref, r1_ref, r2_ref, r3_ref)):
        near_ref[i] = ref[...]


def load_images(c, refs, images, tables, sems):
    copies = []
    for low, ref in enumerate(refs):
        for p1 in range(4):
            h = jnp.where(c == 0, p1 & 1, low)
            q = jnp.where(c == 0, low * 2 + (p1 >> 1), p1)
            copies.append(
                pltpu.make_async_copy(
                    ref.at[p1, pl.ds(0, F)],
                    images.at[pl.ds(pl.multiple_of(h * W, W), F), pl.ds(pl.multiple_of(q * IMG, IMG), IMG)],
                    sems.at[0, low * 4 + p1],
                )
            )
            copies.append(
                pltpu.make_async_copy(
                    ref.at[p1, pl.ds(F, 16)], tables.at[h, q], sems.at[1, low * 4 + p1]
                )
            )
    for copy in copies:
        copy.start()
    return copies


def make_coefficients(stage, me, captions_ref, images, tables, coefficient, copies):
    c = me & 1
    for h in range(2):
        images[h * W + F : (h + 1) * W, :] = jnp.zeros((W - F, COLS), jnp.bfloat16)
    marks = captions_ref[:, 512:640].astype(jnp.float32).astype(jnp.int32)
    owner, slot = marks[:, 64:65], marks[:, 65:66]
    relative = owner ^ me
    near_y, near_x = relative >> 3 & 3, relative >> 5
    column = jnp.where(c == 0, near_y * 2 + near_x, near_x * 4 + near_y) - 4 * stage
    picked = (lax.broadcasted_iota(jnp.int32, (CAPS, 256), 1) == slot).astype(jnp.float32)
    for copy in copies:
        copy.wait()

    table = tables[0].astype(jnp.float32)
    inverse = 1.0 / table[:, 0, :]
    slots = jnp.concatenate([table[:, 1, :], table[:, 2, :]], axis=1)
    slots = jnp.concatenate([slots, jnp.zeros((124, 256), jnp.float32)], axis=0)
    named = lax.dot_general(
        picked.astype(jnp.bfloat16), slots.astype(jnp.bfloat16), (((1,), (1,)), ((), ())),
        preferred_element_type=jnp.float32,
    )
    lanes = lax.broadcasted_iota(jnp.int32, (CAPS, 128), 1)
    named = jnp.sum(jnp.where(lanes == column, named, 0.0), axis=1, keepdims=True)
    inside = ((relative & 7) == 0) & (column >= 0) & (column < 4)
    target = jnp.where(inside, column * IMG + named.astype(jnp.int32), -1)

    for u in range(2):
        columns = slice(u * 256, (u + 1) * 256)
        products = jnp.dot(
            captions_ref[...], images[:, columns], preferred_element_type=jnp.float32
        )
        negative = 5.0 * jnp.tanh(5.0 * products - 1.0) + 5.0
        weight = jnp.concatenate([inverse[2 * u : 2 * u + 1], inverse[2 * u + 1 : 2 * u + 2]], axis=1)
        here = lax.broadcasted_iota(jnp.int32, (CAPS, 256), 1) + u * 256 == target
        part = jnp.where(here, weight * (negative - 10.0), negative)
        coefficient[:, columns] = part.astype(jnp.bfloat16)


def image_grads(c, turned_ref, coefficient, a_out, b_out):
    for low, out in enumerate((a_out, b_out)):
        for t in range(2):
            u = jnp.where(c == 0, low, t)
            h = jnp.where(c == 0, t, low)
            grads = jnp.dot(
                turned_ref[pl.ds(pl.multiple_of(h * W, W), F), :],
                coefficient[:, pl.ds(pl.multiple_of(u * 256, 256), 256)],
                preferred_element_type=jnp.float32,
            )
            for g in range(2):
                p1 = jnp.where(c == 0, g * 2 + t, t * 2 + g)
                out[p1] = grads[:, g * IMG : (g + 1) * IMG]


def caption_grads(coefficient, images, outs, before_ref=None):
    for start in range(0, 2 * W, 256):
        columns = slice(start, start + 256)
        part = lax.dot_general(
            coefficient[...], images[columns, :], (((1,), (1,)), ((), ())),
            preferred_element_type=jnp.float32,
        )
        if before_ref is not None:
            part = part + before_ref[:, columns]
        rows = CAPS // len(outs)
        for i, out in enumerate(outs):
            out[:, columns] = part[i * rows : (i + 1) * rows]


def near_stage_kernel(
    place_ref, near_ref, far_ref, a_ref, b_ref,
    a_out, b_out, caption_out, captions_ref, turned_ref, images, tables, coefficient, sems,
):
    me = place_ref[0]
    copies = load_images(me & 1, (a_ref, b_ref), images, tables, sems)
    for e, ref in enumerate((near_ref, far_ref)):
        for j in range(4):
            for h in range(2):
                captions_ref[pl.ds((e * 4 + j) * HALF, HALF), h * W : (h + 1) * W] = ref[j, h]
    for block in range(2 * W // 128):
        columns = slice(block * 128, (block + 1) * 128)
        turned_ref[columns, :] = captions_ref[:, columns].T
    make_coefficients(0, me, captions_ref, images, tables, coefficient, copies)
    image_grads(me & 1, turned_ref, coefficient, a_out, b_out)
    caption_grads(coefficient, images, (caption_out,))


def far_stage_kernel(
    place_ref, captions_ref, turned_ref, a_ref, b_ref, before_ref,
    a_out, b_out, near_out, far_out, images, tables, coefficient, sems,
):
    me = place_ref[0]
    copies = load_images(me & 1, (a_ref, b_ref), images, tables, sems)
    make_coefficients(1, me, captions_ref, images, tables, coefficient, copies)
    image_grads(me & 1, turned_ref, coefficient, a_out, b_out)
    caption_grads(coefficient, images, (near_out, far_out), before_ref)


VMEM = pl.BlockSpec(memory_space=pltpu.VMEM)
SMEM = pl.BlockSpec(memory_space=pltpu.SMEM)
ANY = pl.BlockSpec(memory_space=pl.ANY)


def bf16(*shape):
    return jax.ShapeDtypeStruct(shape, jnp.bfloat16)


def f32(*shape):
    return jax.ShapeDtypeStruct(shape, jnp.float32)


def call(kernel, outs, ins, scratch=(), megabytes=8, flops=0, nbytes=1_000_000, **kwargs):
    return pl.pallas_call(
        kernel,
        out_shape=outs,
        in_specs=ins,
        out_specs=tuple(VMEM for _ in outs),
        scratch_shapes=list(scratch),
        compiler_params=pltpu.CompilerParams(vmem_limit_bytes=megabytes * 1024 * 1024),
        cost_estimate=pl.CostEstimate(flops=flops, bytes_accessed=nbytes, transcendentals=0),
        **kwargs,
    )


STAGE_SCRATCH = [
    pltpu.VMEM((2 * W, COLS), jnp.bfloat16),
    pltpu.VMEM((2, 4, 16, IMG), jnp.bfloat16),
    pltpu.VMEM((CAPS, COLS), jnp.bfloat16),
    pltpu.SemaphoreType.DMA((2, 8)),
]
DOT_FLOPS = 2 * CAPS * COLS * 2 * W


def body(image_emb, caption_emb, caption_count, caption_owner, pair_image):
    me = lax.axis_index("dp")
    xl = lax.axis_index("mp")
    place = me[None]

    extra = jnp.concatenate(
        [caption_count[None], pair_image.reshape(2, IMG), jnp.zeros((13, IMG), jnp.int32)], axis=0
    ).astype(jnp.bfloat16)
    piece = jnp.concatenate([image_emb.T, extra], axis=0)

    positions = jnp.arange(LOAD, dtype=jnp.int32)
    earlier = positions[None, :] < positions[:, None]
    same_owner = caption_owner[:, None] == caption_owner[None, :]
    rank = jnp.sum((same_owner & earlier).astype(jnp.int32), axis=1)
    marks = jnp.stack([caption_owner, me * 4 + rank], axis=1).astype(jnp.bfloat16)
    rows = jnp.concatenate([caption_emb, marks, jnp.zeros((LOAD, W - F - 2), jnp.bfloat16)], axis=1)
    kept = lax.dynamic_slice_in_dim(rows, xl * HALF, HALF, 0)
    given = lax.dynamic_slice_in_dim(rows, (1 - xl) * HALF, HALF, 0)

    received = [exchange(piece, first_axis(j)) for j in (1, 2, 3)]
    gained = exchange(given, other_half)
    pieces, pair = call(
        join_kernel, (bf16(4, ROWS, IMG), bf16(2, HALF, W)), [VMEM] * 6
    )(piece, *received, kept, gained)

    groups = [pieces] + [exchange(pieces, second_axis(j)) for j in (1, 2, 3)]
    (near,) = call(near_kernel, (bf16(4, 2, HALF, W),), [VMEM] * 4 + [ANY] * 2)(
        pair, *[exchange(pair, along_z(j)) for j in (1, 2, 3)], groups[1], groups[3]
    )
    far = exchange(near, other_core)
    half = jnp.float16
    image_own, image_1, caption_near, captions, turned = call(
        near_stage_kernel,
        (f32(4, F, IMG), f32(4, F, IMG), f32(CAPS, 2 * W), bf16(CAPS, 2 * W), bf16(2 * W, CAPS)),
        [SMEM, VMEM, VMEM, ANY, ANY],
        scratch=STAGE_SCRATCH, megabytes=10, flops=3 * DOT_FLOPS, nbytes=8_000_000,
    )(place, near, far, groups[0], groups[1])
    image_2, image_3, caption_own, caption_far = call(
        far_stage_kernel,
        (f32(4, F, IMG), f32(4, F, IMG), f32(CAPS // 2, 2 * W), f32(CAPS // 2, 2 * W)),
        [SMEM, VMEM, VMEM, ANY, ANY, VMEM],
        scratch=STAGE_SCRATCH, megabytes=10, flops=3 * DOT_FLOPS, nbytes=8_000_000,
    )(place, captions, turned, groups[2], groups[3], caption_near)
    crossed = exchange(caption_far, other_core)
    image_received = [
        exchange(image_1.astype(half), second_axis(1)),
        exchange(image_2.astype(half), second_axis(2)),
        exchange(image_3.astype(half), second_axis(3)),
    ]
    group_total = (caption_own + crossed).reshape(4, HALF, 2 * W)
    caption_received = [
        exchange(group_total[j].astype(half), along_z(j)) for j in (2, 1, 3)
    ]
    line = image_own
    for value in image_received:
        line = line + value.astype(jnp.float32)
    line_received = [exchange(line[j].astype(half), first_axis(j)) for j in (2, 1, 3)]
    total = line[0]
    for value in line_received:
        total = total + value.astype(jnp.float32)
    image_grad = total.astype(jnp.bfloat16).T

    both = group_total[0]
    for value in caption_received:
        both = both + value.astype(jnp.float32)
    both = both.astype(jnp.bfloat16)
    mine, theirs = both[:, :F], both[:, W : W + F]
    returned = exchange(theirs, other_half)
    caption_grad = jnp.where(
        xl == 0,
        jnp.concatenate([mine, returned], axis=0),
        jnp.concatenate([returned, mine], axis=0),
    )
    return image_grad, caption_grad


def solution(mesh):
    in_specs = (P("dp", "mp"), P("dp", "mp"), P("dp"), P("dp"), P("dp"))
    out_specs = (P("dp", "mp"), P("dp", "mp"))
    return jax.shard_map(body, mesh=mesh, in_specs=in_specs, out_specs=out_specs, check_vma=False)
```

time: 109 us -> 83.4 us (0.77)
  waiting for transfers between devices: 41.6 us -> 26.3 us
  Pallas kernels: 21.4 us -> 10 us
  other arithmetic: 12.8 us -> 9.05 us
  starting transfers between devices: 29.6 us -> 33.2 us
    ppermute x22, waiting for transfers between devices: 41.6 us -> 26.3 us  [exchange(): return lax.ppermute(value, ('dp', 'mp'), pairs)]
    pallas_call x2 -> x4, Pallas kernels: 21.4 us -> 10 us  [the longest x1 5.41 us: body(): call(far_stage_kernel, (f32(4, F, IMG), f32(4, F, IMG), f32(CAPS // 2, 2...]
    another operation x10 -> x4, other arithmetic: 9.12 us -> 2.84 us
    ppermute x22, starting transfers between devices: 29.6 us -> 33.2 us  [exchange(): return lax.ppermute(value, ('dp', 'mp'), pairs)]
    unnamed x18 -> x12, local copies, waits for them, and re-layouts: 1.81 us -> 3.09 us
  transfers between devices with their start and end apart: 22 -> 22, of which waited for: 15 -> 9; matrix products, arithmetic and copies ran while one was open for 6% -> 8% of each run, Pallas kernels for 4% -> 5%
where the time goes in v2:
time: 83.4 us; the launch traced here: 83.1 us
  starting transfers between devices  33.2 us (40%)
  waiting for transfers between devices  26.3 us (32%)
  Pallas kernels  10 us (12%)
  other arithmetic  9.05 us (11%)
  local copies, waits for them, and re-layouts  3.72 us (4%)
  between operations  0.85 us (1%)
    ppermute x22, starting transfers between devices, exchange(): return lax.ppermute(value, ('dp', 'mp'), pairs)  33.2 us
    ppermute x22, waiting for transfers between devices, exchange(): return lax.ppermute(value, ('dp', 'mp'), pairs)  26.3 us
    pallas_call x1, Pallas kernels, body(): call(far_stage_kernel, (f32(4, F, IMG), f32(4, F, IMG), f32(CAPS // 2, 2...  5.41 us
    pallas_call x1, Pallas kernels, body(): call(near_stage_kernel, (f32(4, F, IMG), f32(4, F, IMG), f32(CAPS, 2 * W)...  4.5 us
    unnamed x12, local copies, waits for them, and re-layouts  3.09 us
    another operation x4, other arithmetic  2.84 us
  transfers between devices with their start and end apart: 22, of which 9 were waited for; matrix products, arithmetic and copies ran while one was open for 8% of the time, Pallas kernels for 5%

profile of v2, /device:TPU:0, one launch (start us, length us, event | category | flops | bytes accessed | tf_op | source)
XLA Modules:
  0.0 83.1 jit_solution(428509582438402398)
XLA Ops:
  0.6 0.7 convert_bitcast_fusion.1
  1.3 0.7 convert_bitcast_fusion
  2.1 1.1 %maximum_maximum_fusion.1.piece_ref = bf16[592,128]{1,0:T(8,128)(2,1)S(1)} fusion(bf16[2,128]{1,0:T(2,128)(2,1)S(1)} %convert_bitcast_fusion, bf16[1,128]{1,0:T(2,128)(2,1)S(1)} %convert_bitcast_fusion.1, bf16[576,128]{1,0:T(8,128)(2,1)} %bitcast.26, bf16[592]{0:T(1024)(128)(2,1)S(1)} %pad.11.clone), kind=kLoop, calls=%fused_computation.15 | loop fusion | flops 606208 | bytes 300960 | tf_op jit(solution)/shard_map/concatenate | solution.py:226
  3.1 2.9 %collective-permute-start.2 = (bf16[592,128]{1,0:T(8,128)(2,1)S(1)}, bf16[592,128]{1,0:T(8,128)(2,1)S(1)}, u32[]{:S(2)}, u32[]{:S(2)}) collective-permute-start(bf16[592,128]{1,0:T(8,128)(2,1)S(1)} %maximum_maximum_fusion.1.piece_ref), channel_id=1, source_target_pairs={{0,65},{1,64},{2,50},{3,51},{4,69},{5,68},{6,54},{7,55},{8,73},{9,... | collective-permute-start | bytes 454664 | tf_op jit(solution)/shard_map/ppermute | solution.py:29
  6.0 0.8 collective-permute-start.1
  6.8 0.5 collective-permute-start
  7.3 0.7 convert.30
  8.0 0.9 %convert_reduce_fusion = s32[192]{0:T(256)S(1)} fusion(s32[192]{0:T(256)} %param.8), kind=kLoop, calls=%fused_computation.12 | loop fusion | flops 184128 | bytes 1536 | tf_op jit(solution)/shard_map/reduce_sum | solution.py:231
  9.0 0.1 add.67
  9.1 0.1 stack.8
  9.2 1.0 %maximum_maximum_fusion = bf16[192,640]{1,0:T(8,128)(2,1)S(1)} fusion(bf16[192,1]{1,0:T(8,128)(2,1)S(1)} %add.67, bf16[192,1]{1,0:T(8,128)(2,1)S(1)} %stack.8, bf16[192,576]{1,0:T(8,128)(2,1)} %param.6, bf16[640]{0:T(1024)(128)(2,1)S(1)} %pad.7.clone), kind=kLoop, calls=%fused_computation.10 | loop fusion | flops 983040 | bytes 468992 | tf_op jit(solution)/shard_map/concatenate | solution.py:233
  10.3 1.7 %collective-permute-start.3 = (bf16[96,640]{1,0:T(8,128)(2,1)S(1)}, bf16[96,640]{1,0:T(8,128)(2,1)S(1)}, u32[]{:S(2)}, u32[]{:S(2)}) collective-permute-start(bf16[96,640]{1,0:T(8,128)(2,1)S(1)} %get-tuple-element.36), channel_id=1, source_target_pairs={{0,1},{1,0},{2,3},{3,2},{4,5},{5,4},{6,7},{7,6},{8,9},{9,8},{10,11... | collective-permute-start | bytes 368648 | tf_op jit(solution)/shard_map/ppermute | solution.py:29
  12.0 3.3 %collective-permute-done.3.gained_ref = bf16[96,640]{1,0:T(8,128)(2,1)S(1)} collective-permute-done((bf16[96,640]{1,0:T(8,128)(2,1)S(1)}, bf16[96,640]{1,0:T(8,128)(2,1)S(1)}, u32[]{:S(2)}, u32[]{:S(2)}) %collective-permute-start.3) | collective-permute-done | bytes 122912 | tf_op jit(solution)/shard_map/ppermute | solution.py:29
  15.3 3.2 %collective-permute-start.8 = (bf16[4,592,128]{2,1,0:T(8,128)(2,1)S(1)}, bf16[4,592,128]{2,1,0:T(8,128)(2,1)S(1)}, u32[]{:S(2)}, u32[]{:S(2)}) collective-permute-start(bf16[4,592,128]{2,1,0:T(8,128)(2,1)S(1)} %get-tuple-element.14.a_ref), channel_id=1, source_target_pairs={{0,48},{1,49},{2,67},{3,66},{4,52},{5,53},{6,71},{7,70},{8,56},{9,... | collective-permute-start | bytes 1818632 | tf_op jit(solution)/shard_map/ppermute | solution.py:29
  18.5 0.1 collective-permute-start.7
  18.7 4.0 %collective-permute-start.6 = (bf16[2,96,640]{2,1,0:T(8,128)(2,1)S(1)}, bf16[2,96,640]{2,1,0:T(8,128)(2,1)S(1)}, u32[]{:S(2)}, u32[]{:S(2)}) collective-permute-start(bf16[2,96,640]{2,1,0:T(8,128)(2,1)S(1)} %get-tuple-element.13.pair_ref), channel_id=1, source_target_pairs={{0,12},{1,13},{2,14},{3,15},{4,8},{5,9},{6,10},{7,11},{8,4},{9,5},... | collective-permute-start | bytes 737288 | tf_op jit(solution)/shard_map/ppermute | solution.py:29
  22.7 0.9 %collective-permute-start.4 = (bf16[2,96,640]{2,1,0:T(8,128)(2,1)S(1)}, bf16[2,96,640]{2,1,0:T(8,128)(2,1)S(1)}, u32[]{:S(2)}, u32[]{:S(2)}) collective-permute-start(bf16[2,96,640]{2,1,0:T(8,128)(2,1)S(1)} %get-tuple-element.13.pair_ref), channel_id=1, source_target_pairs={{0,4},{1,5},{2,6},{3,7},{4,0},{5,1},{6,2},{7,3},{8,12},{9,13},{10,... | collective-permute-start | bytes 737288 | tf_op jit(solution)/shard_map/ppermute | solution.py:29
  23.6 7.1 %collective-permute-done.6.r3_ref = bf16[2,96,640]{2,1,0:T(8,128)(2,1)S(1)} collective-permute-done((bf16[2,96,640]{2,1,0:T(8,128)(2,1)S(1)}, bf16[2,96,640]{2,1,0:T(8,128)(2,1)S(1)}, u32[]{:S(2)}, u32[]{:S(2)}) %collective-permute-start.6) | collective-permute-done | bytes 245792 | tf_op jit(solution)/shard_map/ppermute | solution.py:29
  30.7 1.1 %collective-permute-done.5.r2_ref = bf16[2,96,640]{2,1,0:T(8,128)(2,1)S(1)} collective-permute-done((bf16[2,96,640]{2,1,0:T(8,128)(2,1)S(1)}, bf16[2,96,640]{2,1,0:T(8,128)(2,1)S(1)}, u32[]{:S(2)}, u32[]{:S(2)}) %collective-permute-start.5) | collective-permute-done | bytes 245792 | tf_op jit(solution)/shard_map/ppermute | solution.py:29
  31.8 0.2 collective-permute-done.4.r1_ref
  32.1 0.1 collective-permute-start.9
  32.2 3.2 %collective-permute-start.11 = (bf16[4,592,128]{2,1,0:T(8,128)(2,1)S(1)}, bf16[4,592,128]{2,1,0:T(8,128)(2,1)S(1)}, u32[]{:S(2)}, u32[]{:S(2)}) collective-permute-start(bf16[4,592,128]{2,1,0:T(8,128)(2,1)S(1)} %get-tuple-element.14.a_ref), channel_id=1, source_target_pairs={{0,32},{1,33},{2,66},{3,67},{4,36},{5,37},{6,70},{7,71},{8,40},{9,... | collective-permute-start | bytes 1818632 | tf_op jit(solution)/shard_map/ppermute | solution.py:29
  35.4 4.5 %shard_map.70 = (f32[4,576,128]{2,1,0:T(8,128)S(1)}, f32[4,576,128]{2,1,0:T(8,128)S(1)}, f32[768,1280]{1,0:T(8,128)S(1)}, bf16[768,1280]{1,0:T(8,128)(2,1)S(1)}, bf16[1280,768]{1,0:T(8,128)(2,1)S(1)}) custom-call(s32[1]{0:T(128)} %bitcast.place_ref, bf16[4,2,96,640]{3,2,1,0:T(8,128)(2,1)S(1)} %shard_map.69.near_ref, ...), custom_call_target="tpu_custom_call" | custom-call | flops 3019898880 | bytes 8000000 | tf_op jit(solution)/shard_map/pallas_call | solution.py:249
  40.0 1.0 %copy-done.4 = f32[4,576,128]{2,1,0:T(8,128)} copy-done((f32[4,576,128]{2,1,0:T(8,128)}, f32[4,576,128]{2,1,0:T(8,128)S(1)}, u32[]{:S(2)}) %copy-start.4) | copy-done | bytes 1179672
  41.0 2.9 %collective-permute-done.11.a_ref = bf16[4,592,128]{2,1,0:T(8,128)(2,1)S(1)} collective-permute-done((bf16[4,592,128]{2,1,0:T(8,128)(2,1)S(1)}, bf16[4,592,128]{2,1,0:T(8,128)(2,1)S(1)}, u32[]{:S(2)}, u32[]{:S(2)}) %collective-permute-start.11) | collective-permute-done | bytes 606240 | tf_op jit(solution)/shard_map/ppermute | solution.py:29
  43.9 5.4 %shard_map.71 = (f32[4,576,128]{2,1,0:T(8,128)S(1)}, f32[4,576,128]{2,1,0:T(8,128)S(1)}, f32[384,1280]{1,0:T(8,128)S(1)}, f32[384,1280]{1,0:T(8,128)}) custom-call(s32[1]{0:T(128)} %bitcast.place_ref, bf16[768,1280]{1,0:T(8,128)(2,1)S(1)} %get-tuple-element.17.captions_ref, bf16[1280,768]{1,0:T(8,128)(2,1)S(1)} %get-tuple-element.18.turned_ref, ...), custom_call_target="tpu_custom_call" | custom-call | flops 3019898880 | bytes 8000000 | tf_op jit(solution)/shard_map/pallas_call | solution.py:255
  49.3 1.0 %copy-done = f32[4,576,128]{2,1,0:T(8,128)} copy-done((f32[4,576,128]{2,1,0:T(8,128)}, f32[4,576,128]{2,1,0:T(8,128)S(1)}, u32[]{:S(2)}) %copy-start) | copy-done | bytes 1179672
  50.3 1.0 %copy-done.2 = f32[4,576,128]{2,1,0:T(8,128)} copy-done((f32[4,576,128]{2,1,0:T(8,128)}, f32[4,576,128]{2,1,0:T(8,128)S(1)}, u32[]{:S(2)}) %copy-start.2) | copy-done | bytes 1179672
  51.4 1.8 %collective-permute-start.10 = (f16[4,576,128]{2,1,0:T(8,128)(2,1)S(1)}, f16[4,576,128]{2,1,0:T(8,128)(2,1)S(1)}, u32[]{:S(2)}, u32[]{:S(2)}) collective-permute-start(f16[4,576,128]{2,1,0:T(8,128)(2,1)S(1)} %convert_element_type.63), channel_id=1, source_target_pairs={{0,16},{1,17},{2,3},{3,2},{4,20},{5,21},{6,7},{7,6},{8,24},{9,25},... | collective-permute-start | bytes 1769480 | tf_op jit(solution)/shard_map/ppermute | solution.py:29
  53.4 2.7 %collective-permute-start.13 = (f16[4,576,128]{2,1,0:T(8,128)(2,1)S(1)}, f16[4,576,128]{2,1,0:T(8,128)(2,1)S(1)}, u32[]{:S(2)}, u32[]{:S(2)}) collective-permute-start(f16[4,576,128]{2,1,0:T(8,128)(2,1)S(1)} %convert_element_type.67), channel_id=1, source_target_pairs={{0,48},{1,49},{2,67},{3,66},{4,52},{5,53},{6,71},{7,70},{8,56},{9,... | collective-permute-start | bytes 1769480 | tf_op jit(solution)/shard_map/ppermute | solution.py:29
  56.1 0.7 collective-permute-start.12
  56.8 1.8 %fusion.9 = (f16[384,1280]{1,0:T(8,128)(2,1)S(1)}, f32[384,1280]{1,0:T(8,128)S(1)}) fusion(f32[384,1280]{1,0:T(8,128)S(1)} %get-tuple-element.22, f32[384,1280]{1,0:T(8,128)} %collective-permute-done.17), kind=kLoop, calls=%fused_computation.25 | loop fusion | flops 983040 | bytes 6881280 | tf_op jit(solution)/shard_map/convert.2
  58.6 0.1 fusion.11
  58.7 2.8 %collective-permute-start.18 = (f16[96,1280]{1,0:T(8,128)(2,1)S(1)}, f16[96,1280]{1,0:T(8,128)(2,1)S(1)}, u32[]{:S(2)}, u32[]{:S(2)}) collective-permute-start(f16[96,1280]{1,0:T(8,128)(2,1)S(1)} %get-tuple-element.28), channel_id=1, source_target_pairs={{0,8},{1,9},{2,10},{3,11},{4,12},{5,13},{6,14},{7,15},{8,0},{9,1},... | collective-permute-start | bytes 737288 | tf_op jit(solution)/shard_map/ppermute | solution.py:29
  61.5 1.1 %collective-permute-start.20 = (f16[96,1280]{1,0:T(8,128)(2,1)S(1)}, f16[96,1280]{1,0:T(8,128)(2,1)S(1)}, u32[]{:S(2)}, u32[]{:S(2)}) collective-permute-start(f16[96,1280]{1,0:T(8,128)(2,1)S(1)} %get-tuple-element.29), channel_id=1, source_target_pairs={{0,12},{1,13},{2,14},{3,15},{4,8},{5,9},{6,10},{7,11},{8,4},{9,5},... | collective-permute-start | bytes 737288 | tf_op jit(solution)/shard_map/ppermute | solution.py:29
  62.6 0.1 collective-permute-start.19
  62.8 8.2 %collective-permute-done.13 = f16[4,576,128]{2,1,0:T(8,128)(2,1)S(1)} collective-permute-done((f16[4,576,128]{2,1,0:T(8,128)(2,1)S(1)}, f16[4,576,128]{2,1,0:T(8,128)(2,1)S(1)}, u32[]{:S(2)}, u32[]{:S(2)}) %collective-permute-start.13) | collective-permute-done | bytes 589856 | tf_op jit(solution)/shard_map/ppermute | solution.py:29
  70.9 0.4 fusion.10
  71.3 0.1 slice_bitcast_fusion.3
  71.4 1.8 %collective-permute-start.14 = (f16[576,128]{1,0:T(8,128)(2,1)S(1)}, f16[576,128]{1,0:T(8,128)(2,1)S(1)}, u32[]{:S(2)}, u32[]{:S(2)}) collective-permute-start(f16[576,128]{1,0:T(8,128)(2,1)S(1)} %get-tuple-element.31), channel_id=1, source_target_pairs={{0,64},{1,65},{2,34},{3,35},{4,68},{5,69},{6,38},{7,39},{8,72},{9,... | collective-permute-start | bytes 442376 | tf_op jit(solution)/shard_map/ppermute | solution.py:29
  73.2 2.7 %collective-permute-start.16 = (f16[576,128]{1,0:T(8,128)(2,1)S(1)}, f16[576,128]{1,0:T(8,128)(2,1)S(1)}, u32[]{:S(2)}, u32[]{:S(2)}) collective-permute-start(f16[576,128]{1,0:T(8,128)(2,1)S(1)} %get-tuple-element.32), channel_id=1, source_target_pairs={{0,65},{1,64},{2,50},{3,51},{4,69},{5,68},{6,54},{7,55},{8,73},{9,... | collective-permute-start | bytes 442376 | tf_op jit(solution)/shard_map/ppermute | solution.py:29
  75.9 0.1 fusion.2
  76.1 2.1 %collective-permute-start.21 = (bf16[96,576]{1,0:T(8,128)(2,1)S(1)}, bf16[96,576]{1,0:T(8,128)(2,1)S(1)}, u32[]{:S(2)}, u32[]{:S(2)}) collective-permute-start(bf16[96,576]{1,0:T(8,128)(2,1)S(1)} %get-tuple-element.35), channel_id=1, source_target_pairs={{0,1},{1,0},{2,3},{3,2},{4,5},{5,4},{6,7},{7,6},{8,9},{9,8},{10,11... | collective-permute-start | bytes 331784 | tf_op jit(solution)/shard_map/ppermute | solution.py:29
  78.2 1.5 %collective-permute-done.16 = f16[576,128]{1,0:T(8,128)(2,1)S(1)} collective-permute-done((f16[576,128]{1,0:T(8,128)(2,1)S(1)}, f16[576,128]{1,0:T(8,128)(2,1)S(1)}, u32[]{:S(2)}, u32[]{:S(2)}) %collective-permute-start.16) | collective-permute-done | bytes 147488 | tf_op jit(solution)/shard_map/ppermute | solution.py:29
  79.7 1.3 %collective-permute-done.15 = f16[576,128]{1,0:T(8,128)(2,1)S(1)} collective-permute-done((f16[576,128]{1,0:T(8,128)(2,1)S(1)}, f16[576,128]{1,0:T(8,128)(2,1)S(1)}, u32[]{:S(2)}, u32[]{:S(2)}) %collective-permute-start.15) | collective-permute-done | bytes 147488 | tf_op jit(solution)/shard_map/ppermute | solution.py:29
  81.0 0.7 fusion.8
  81.8 0.6 collective-permute-done.21
  82.4 0.7 maximum_select_fusion
  (37 shorter events, 0.7 us)
Async XLA Ops:
  3.1 12.1 %collective-permute-start.2 = (bf16[592,128]{1,0:T(8,128)(2,1)S(1)}, bf16[592,128]{1,0:T(8,128)(2,1)S(1)}, u32[]{:S(2)}, u32[]{:S(2)}) collective-permute-start(bf16[592,128]{1,0:T(8,128)(2,1)S(1)} %maximum_maximum_fusion.1.piece_ref), channel_id=1, source_target_pairs={{0,65},{1,64},{2,50},{3,51},{4,69},{5,68},{6,54},{7,55},{8,73},{9,... | collective-permute-start | bytes 454664 | tf_op jit(solution)/shard_map/ppermute | solution.py:29
  6.0 9.2 %collective-permute-start.1 = (bf16[592,128]{1,0:T(8,128)(2,1)S(1)}, bf16[592,128]{1,0:T(8,128)(2,1)S(1)}, u32[]{:S(2)}, u32[]{:S(2)}) collective-permute-start(bf16[592,128]{1,0:T(8,128)(2,1)S(1)} %maximum_maximum_fusion.1.piece_ref), channel_id=1, source_target_pairs={{0,64},{1,65},{2,34},{3,35},{4,68},{5,69},{6,38},{7,39},{8,72},{9,... | collective-permute-start | bytes 454664 | tf_op jit(solution)/shard_map/ppermute | solution.py:29
  6.8 8.4 %collective-permute-start = (bf16[592,128]{1,0:T(8,128)(2,1)S(1)}, bf16[592,128]{1,0:T(8,128)(2,1)S(1)}, u32[]{:S(2)}, u32[]{:S(2)}) collective-permute-start(bf16[592,128]{1,0:T(8,128)(2,1)S(1)} %maximum_maximum_fusion.1.piece_ref), channel_id=1, source_target_pairs={{0,1},{1,0},{2,18},{3,19},{4,5},{5,4},{6,22},{7,23},{8,9},{9,8},{1... | collective-permute-start | bytes 454664 | tf_op jit(solution)/shard_map/ppermute | solution.py:29
  10.3 5.0 %collective-permute-start.3 = (bf16[96,640]{1,0:T(8,128)(2,1)S(1)}, bf16[96,640]{1,0:T(8,128)(2,1)S(1)}, u32[]{:S(2)}, u32[]{:S(2)}) collective-permute-start(bf16[96,640]{1,0:T(8,128)(2,1)S(1)} %get-tuple-element.36), channel_id=1, source_target_pairs={{0,1},{1,0},{2,3},{3,2},{4,5},{5,4},{6,7},{7,6},{8,9},{9,8},{10,11... | collective-permute-start | bytes 368648 | tf_op jit(solution)/shard_map/ppermute | solution.py:29
  15.3 16.7 %collective-permute-start.8 = (bf16[4,592,128]{2,1,0:T(8,128)(2,1)S(1)}, bf16[4,592,128]{2,1,0:T(8,128)(2,1)S(1)}, u32[]{:S(2)}, u32[]{:S(2)}) collective-permute-start(bf16[4,592,128]{2,1,0:T(8,128)(2,1)S(1)} %get-tuple-element.14.a_ref), channel_id=1, source_target_pairs={{0,48},{1,49},{2,67},{3,66},{4,52},{5,53},{6,71},{7,70},{8,56},{9,... | collective-permute-start | bytes 1818632 | tf_op jit(solution)/shard_map/ppermute | solution.py:29
  18.5 13.5 %collective-permute-start.7 = (bf16[4,592,128]{2,1,0:T(8,128)(2,1)S(1)}, bf16[4,592,128]{2,1,0:T(8,128)(2,1)S(1)}, u32[]{:S(2)}, u32[]{:S(2)}) collective-permute-start(bf16[4,592,128]{2,1,0:T(8,128)(2,1)S(1)} %get-tuple-element.14.a_ref), channel_id=1, source_target_pairs={{0,16},{1,17},{2,3},{3,2},{4,20},{5,21},{6,7},{7,6},{8,24},{9,25},... | collective-permute-start | bytes 1818632 | tf_op jit(solution)/shard_map/ppermute | solution.py:29
  18.7 12.0 %collective-permute-start.6 = (bf16[2,96,640]{2,1,0:T(8,128)(2,1)S(1)}, bf16[2,96,640]{2,1,0:T(8,128)(2,1)S(1)}, u32[]{:S(2)}, u32[]{:S(2)}) collective-permute-start(bf16[2,96,640]{2,1,0:T(8,128)(2,1)S(1)} %get-tuple-element.13.pair_ref), channel_id=1, source_target_pairs={{0,12},{1,13},{2,14},{3,15},{4,8},{5,9},{6,10},{7,11},{8,4},{9,5},... | collective-permute-start | bytes 737288 | tf_op jit(solution)/shard_map/ppermute | solution.py:29
  22.7 9.1 %collective-permute-start.5 = (bf16[2,96,640]{2,1,0:T(8,128)(2,1)S(1)}, bf16[2,96,640]{2,1,0:T(8,128)(2,1)S(1)}, u32[]{:S(2)}, u32[]{:S(2)}) collective-permute-start(bf16[2,96,640]{2,1,0:T(8,128)(2,1)S(1)} %get-tuple-element.13.pair_ref), channel_id=1, source_target_pairs={{0,8},{1,9},{2,10},{3,11},{4,12},{5,13},{6,14},{7,15},{8,0},{9,1},... | collective-permute-start | bytes 737288 | tf_op jit(solution)/shard_map/ppermute | solution.py:29
  22.7 9.3 %collective-permute-start.4 = (bf16[2,96,640]{2,1,0:T(8,128)(2,1)S(1)}, bf16[2,96,640]{2,1,0:T(8,128)(2,1)S(1)}, u32[]{:S(2)}, u32[]{:S(2)}) collective-permute-start(bf16[2,96,640]{2,1,0:T(8,128)(2,1)S(1)} %get-tuple-element.13.pair_ref), channel_id=1, source_target_pairs={{0,4},{1,5},{2,6},{3,7},{4,0},{5,1},{6,2},{7,3},{8,12},{9,13},{10,... | collective-permute-start | bytes 737288 | tf_op jit(solution)/shard_map/ppermute | solution.py:29
  32.1 3.3 %collective-permute-start.9 = (bf16[4,2,96,640]{3,2,1,0:T(8,128)(2,1)S(1)}, bf16[4,2,96,640]{3,2,1,0:T(8,128)(2,1)S(1)}, u32[]{:S(2)}, u32[]{:S(2)}) collective-permute-start(bf16[4,2,96,640]{3,2,1,0:T(8,128)(2,1)S(1)} %shard_map.69.near_ref), channel_id=1, source_target_pairs={{0,2},{1,3},{2,0},{3,1},{4,6},{5,7},{6,4},{7,5},{8,10},{9,11},{10,... | collective-permute-start | bytes 2949128 | tf_op jit(solution)/shard_map/ppermute | solution.py:29
  32.2 11.6 %collective-permute-start.11 = (bf16[4,592,128]{2,1,0:T(8,128)(2,1)S(1)}, bf16[4,592,128]{2,1,0:T(8,128)(2,1)S(1)}, u32[]{:S(2)}, u32[]{:S(2)}) collective-permute-start(bf16[4,592,128]{2,1,0:T(8,128)(2,1)S(1)} %get-tuple-element.14.a_ref), channel_id=1, source_target_pairs={{0,32},{1,33},{2,66},{3,67},{4,36},{5,37},{6,70},{7,71},{8,40},{9,... | collective-permute-start | bytes 1818632 | tf_op jit(solution)/shard_map/ppermute | solution.py:29
  39.9 1.0 %copy-start.4 = (f32[4,576,128]{2,1,0:T(8,128)}, f32[4,576,128]{2,1,0:T(8,128)S(1)}, u32[]{:S(2)}) copy-start(f32[4,576,128]{2,1,0:T(8,128)S(1)} %get-tuple-element.15) | copy-start | bytes 3538948
  49.3 1.0 %copy-start = (f32[4,576,128]{2,1,0:T(8,128)}, f32[4,576,128]{2,1,0:T(8,128)S(1)}, u32[]{:S(2)}) copy-start(f32[4,576,128]{2,1,0:T(8,128)S(1)} %get-tuple-element.21) | copy-start | bytes 3538948
  50.3 1.0 %copy-start.2 = (f32[4,576,128]{2,1,0:T(8,128)}, f32[4,576,128]{2,1,0:T(8,128)S(1)}, u32[]{:S(2)}) copy-start(f32[4,576,128]{2,1,0:T(8,128)S(1)} %get-tuple-element.20) | copy-start | bytes 3538948
  51.3 5.5 %collective-permute-start.17 = (f32[384,1280]{1,0:T(8,128)}, f32[384,1280]{1,0:T(8,128)}, u32[]{:S(2)}, u32[]{:S(2)}) collective-permute-start(f32[384,1280]{1,0:T(8,128)} %get-tuple-element.23), channel_id=1, source_target_pairs={{0,2},{1,3},{2,0},{3,1},{4,6},{5,7},{6,4},{7,5},{8,10},{9,11},{10,... | collective-permute-start | bytes 5898248 | tf_op jit(solution)/shard_map/ppermute | solution.py:29
  51.3 1.9 %copy-start.3 = (f32[4,576,128]{2,1,0:T(8,128)S(1)}, f32[4,576,128]{2,1,0:T(8,128)}, u32[]{:S(2)}) copy-start(f32[4,576,128]{2,1,0:T(8,128)} %copy-done.2) | copy-start | bytes 3538948
  51.4 1.9 %copy-start.1 = (f32[4,576,128]{2,1,0:T(8,128)S(1)}, f32[4,576,128]{2,1,0:T(8,128)}, u32[]{:S(2)}) copy-start(f32[4,576,128]{2,1,0:T(8,128)} %copy-done) | copy-start | bytes 3538948
  51.4 11.2 %collective-permute-start.10 = (f16[4,576,128]{2,1,0:T(8,128)(2,1)S(1)}, f16[4,576,128]{2,1,0:T(8,128)(2,1)S(1)}, u32[]{:S(2)}, u32[]{:S(2)}) collective-permute-start(f16[4,576,128]{2,1,0:T(8,128)(2,1)S(1)} %convert_element_type.63), channel_id=1, source_target_pairs={{0,16},{1,17},{2,3},{3,2},{4,20},{5,21},{6,7},{7,6},{8,24},{9,25},... | collective-permute-start | bytes 1769480 | tf_op jit(solution)/shard_map/ppermute | solution.py:29
  53.4 17.5 %collective-permute-start.13 = (f16[4,576,128]{2,1,0:T(8,128)(2,1)S(1)}, f16[4,576,128]{2,1,0:T(8,128)(2,1)S(1)}, u32[]{:S(2)}, u32[]{:S(2)}) collective-permute-start(f16[4,576,128]{2,1,0:T(8,128)(2,1)S(1)} %convert_element_type.67), channel_id=1, source_target_pairs={{0,48},{1,49},{2,67},{3,66},{4,52},{5,53},{6,71},{7,70},{8,56},{9,... | collective-permute-start | bytes 1769480 | tf_op jit(solution)/shard_map/ppermute | solution.py:29
  56.1 14.8 %collective-permute-start.12 = (f16[4,576,128]{2,1,0:T(8,128)(2,1)S(1)}, f16[4,576,128]{2,1,0:T(8,128)(2,1)S(1)}, u32[]{:S(2)}, u32[]{:S(2)}) collective-permute-start(f16[4,576,128]{2,1,0:T(8,128)(2,1)S(1)} %convert_element_type.65), channel_id=1, source_target_pairs={{0,32},{1,33},{2,66},{3,67},{4,36},{5,37},{6,70},{7,71},{8,40},{9,... | collective-permute-start | bytes 1769480 | tf_op jit(solution)/shard_map/ppermute | solution.py:29
  58.6 12.4 %copy-start.5 = (f32[4,576,128]{2,1,0:T(8,128)S(1)}, f32[4,576,128]{2,1,0:T(8,128)}, u32[]{:S(2)}) copy-start(f32[4,576,128]{2,1,0:T(8,128)} %copy-done.4) | copy-start | bytes 3538948
  58.7 17.2 %collective-permute-start.18 = (f16[96,1280]{1,0:T(8,128)(2,1)S(1)}, f16[96,1280]{1,0:T(8,128)(2,1)S(1)}, u32[]{:S(2)}, u32[]{:S(2)}) collective-permute-start(f16[96,1280]{1,0:T(8,128)(2,1)S(1)} %get-tuple-element.28), channel_id=1, source_target_pairs={{0,8},{1,9},{2,10},{3,11},{4,12},{5,13},{6,14},{7,15},{8,0},{9,1},... | collective-permute-start | bytes 737288 | tf_op jit(solution)/shard_map/ppermute | solution.py:29
  61.5 14.4 %collective-permute-start.20 = (f16[96,1280]{1,0:T(8,128)(2,1)S(1)}, f16[96,1280]{1,0:T(8,128)(2,1)S(1)}, u32[]{:S(2)}, u32[]{:S(2)}) collective-permute-start(f16[96,1280]{1,0:T(8,128)(2,1)S(1)} %get-tuple-element.29), channel_id=1, source_target_pairs={{0,12},{1,13},{2,14},{3,15},{4,8},{5,9},{6,10},{7,11},{8,4},{9,5},... | collective-permute-start | bytes 737288 | tf_op jit(solution)/shard_map/ppermute | solution.py:29
  62.6 13.3 %collective-permute-start.19 = (f16[96,1280]{1,0:T(8,128)(2,1)S(1)}, f16[96,1280]{1,0:T(8,128)(2,1)S(1)}, u32[]{:S(2)}, u32[]{:S(2)}) collective-permute-start(f16[96,1280]{1,0:T(8,128)(2,1)S(1)} %get-tuple-element.30), channel_id=1, source_target_pairs={{0,4},{1,5},{2,6},{3,7},{4,0},{5,1},{6,2},{7,3},{8,12},{9,13},{10,... | collective-permute-start | bytes 737288 | tf_op jit(solution)/shard_map/ppermute | solution.py:29
  71.4 6.8 %collective-permute-start.14 = (f16[576,128]{1,0:T(8,128)(2,1)S(1)}, f16[576,128]{1,0:T(8,128)(2,1)S(1)}, u32[]{:S(2)}, u32[]{:S(2)}) collective-permute-start(f16[576,128]{1,0:T(8,128)(2,1)S(1)} %get-tuple-element.31), channel_id=1, source_target_pairs={{0,64},{1,65},{2,34},{3,35},{4,68},{5,69},{6,38},{7,39},{8,72},{9,... | collective-permute-start | bytes 442376 | tf_op jit(solution)/shard_map/ppermute | solution.py:29
  73.2 6.5 %collective-permute-start.16 = (f16[576,128]{1,0:T(8,128)(2,1)S(1)}, f16[576,128]{1,0:T(8,128)(2,1)S(1)}, u32[]{:S(2)}, u32[]{:S(2)}) collective-permute-start(f16[576,128]{1,0:T(8,128)(2,1)S(1)} %get-tuple-element.32), channel_id=1, source_target_pairs={{0,65},{1,64},{2,50},{3,51},{4,69},{5,68},{6,54},{7,55},{8,73},{9,... | collective-permute-start | bytes 442376 | tf_op jit(solution)/shard_map/ppermute | solution.py:29
  75.9 5.1 %collective-permute-start.15 = (f16[576,128]{1,0:T(8,128)(2,1)S(1)}, f16[576,128]{1,0:T(8,128)(2,1)S(1)}, u32[]{:S(2)}, u32[]{:S(2)}) collective-permute-start(f16[576,128]{1,0:T(8,128)(2,1)S(1)} %get-tuple-element.33), channel_id=1, source_target_pairs={{0,1},{1,0},{2,18},{3,19},{4,5},{5,4},{6,22},{7,23},{8,9},{9,8},{1... | collective-permute-start | bytes 442376 | tf_op jit(solution)/shard_map/ppermute | solution.py:29
  76.1 6.3 %collective-permute-start.21 = (bf16[96,576]{1,0:T(8,128)(2,1)S(1)}, bf16[96,576]{1,0:T(8,128)(2,1)S(1)}, u32[]{:S(2)}, u32[]{:S(2)}) collective-permute-start(bf16[96,576]{1,0:T(8,128)(2,1)S(1)} %get-tuple-element.35), channel_id=1, source_target_pairs={{0,1},{1,0},{2,3},{3,2},{4,5},{5,4},{6,7},{7,6},{8,9},{9,8},{10,11... | collective-permute-start | bytes 331784 | tf_op jit(solution)/shard_map/ppermute | solution.py:29

commit v3 on v2

--- a/solution.py
+++ b/solution.py
@@ -53,7 +53,8 @@
     for i, ref in enumerate((piece_ref, r1_ref, r2_ref, r3_ref)):
         pieces_ref[i] = ref[...]
     pair_ref[0] = kept_ref[...]
-    pair_ref[1] = gained_ref[...]
+    pair_ref[1, :, :F] = gained_ref[...]
+    pair_ref[1, :, F:] = jnp.zeros((HALF, W - F), jnp.bfloat16)
 
 
 def near_kernel(pair_ref, r1_ref, r2_ref, r3_ref, _a, _b, near_ref):
@@ -70,7 +71,7 @@
             copies.append(
                 pltpu.make_async_copy(
                     ref.at[p1, pl.ds(0, F)],
-                    images.at[pl.ds(pl.multiple_of(h * W, W), F), pl.ds(pl.multiple_of(q * IMG, IMG), IMG)],
+                    images.at[pl.ds(pl.multiple_of(h * F, F), F), pl.ds(pl.multiple_of(q * IMG, IMG), IMG)],
                     sems.at[0, low * 4 + p1],
                 )
             )
@@ -84,11 +85,9 @@
     return copies
 
 
-def make_coefficients(stage, me, captions_ref, images, tables, coefficient, copies):
+def make_coefficients(stage, me, captions_ref, marks_ref, images, tables, coefficient, copies):
     c = me & 1
-    for h in range(2):
-        images[h * W + F : (h + 1) * W, :] = jnp.zeros((W - F, COLS), jnp.bfloat16)
-    marks = captions_ref[:, 512:640].astype(jnp.float32).astype(jnp.int32)
+    marks = marks_ref[...].astype(jnp.float32).astype(jnp.int32)
     owner, slot = marks[:, 64:65], marks[:, 65:66]
     relative = owner ^ me
     near_y, near_x = relative >> 3 & 3, relative >> 5
@@ -128,7 +127,7 @@
             u = jnp.where(c == 0, low, t)
             h = jnp.where(c == 0, t, low)
             grads = jnp.dot(
-                turned_ref[pl.ds(pl.multiple_of(h * W, W), F), :],
+                turned_ref[pl.ds(pl.multiple_of(h * F, F), F), :],
                 coefficient[:, pl.ds(pl.multiple_of(u * 256, 256), 256)],
                 preferred_element_type=jnp.float32,
             )
@@ -138,8 +137,8 @@
 
 
 def caption_grads(coefficient, images, outs, before_ref=None):
-    for start in range(0, 2 * W, 256):
-        columns = slice(start, start + 256)
+    for start in range(0, 2 * F, 256):
+        columns = slice(start, min(start + 256, 2 * F))
         part = lax.dot_general(
             coefficient[...], images[columns, :], (((1,), (1,)), ((), ())),
             preferred_element_type=jnp.float32,
@@ -153,29 +152,32 @@
 
 def near_stage_kernel(
     place_ref, near_ref, far_ref, a_ref, b_ref,
-    a_out, b_out, caption_out, captions_ref, turned_ref, images, tables, coefficient, sems,
+    a_out, b_out, caption_out, captions_ref, turned_ref, marks_ref, images, tables, coefficient, sems,
 ):
     me = place_ref[0]
     copies = load_images(me & 1, (a_ref, b_ref), images, tables, sems)
     for e, ref in enumerate((near_ref, far_ref)):
         for j in range(4):
             for h in range(2):
-                captions_ref[pl.ds((e * 4 + j) * HALF, HALF), h * W : (h + 1) * W] = ref[j, h]
-    for block in range(2 * W // 128):
+                rows = pl.ds((e * 4 + j) * HALF, HALF)
+                captions_ref[rows, h * F : (h + 1) * F] = ref[j, h, :, :F]
+                if h == 0:
+                    marks_ref[rows, :] = ref[j, 0, :, 512:640]
+    for block in range(2 * F // 128):
         columns = slice(block * 128, (block + 1) * 128)
         turned_ref[columns, :] = captions_ref[:, columns].T
-    make_coefficients(0, me, captions_ref, images, tables, coefficient, copies)
+    make_coefficients(0, me, captions_ref, marks_ref, images, tables, coefficient, copies)
     image_grads(me & 1, turned_ref, coefficient, a_out, b_out)
     caption_grads(coefficient, images, (caption_out,))
 
 
 def far_stage_kernel(
-    place_ref, captions_ref, turned_ref, a_ref, b_ref, before_ref,
+    place_ref, captions_ref, turned_ref, marks_ref, a_ref, b_ref, before_ref,
     a_out, b_out, near_out, far_out, images, tables, coefficient, sems,
 ):
     me = place_ref[0]
     copies = load_images(me & 1, (a_ref, b_ref), images, tables, sems)
-    make_coefficients(1, me, captions_ref, images, tables, coefficient, copies)
+    make_coefficients(1, me, captions_ref, marks_ref, images, tables, coefficient, copies)
     image_grads(me & 1, turned_ref, coefficient, a_out, b_out)
     caption_grads(coefficient, images, (near_out, far_out), before_ref)
 
@@ -207,12 +209,16 @@
 
 
 STAGE_SCRATCH = [
-    pltpu.VMEM((2 * W, COLS), jnp.bfloat16),
+    pltpu.VMEM((2 * F, COLS), jnp.bfloat16),
     pltpu.VMEM((2, 4, 16, IMG), jnp.bfloat16),
     pltpu.VMEM((CAPS, COLS), jnp.bfloat16),
     pltpu.SemaphoreType.DMA((2, 8)),
 ]
-DOT_FLOPS = 2 * CAPS * COLS * 2 * W
+DOT_FLOPS = 2 * CAPS * COLS * 2 * F
+
+
+def after(values, earlier):
+    return lax.optimization_barrier((values, earlier))[0]
 
 
 def body(image_emb, caption_emb, caption_count, caption_owner, pair_image):
@@ -220,11 +226,16 @@
     xl = lax.axis_index("mp")
     place = me[None]
 
-    extra = jnp.concatenate(
-        [caption_count[None], pair_image.reshape(2, IMG), jnp.zeros((13, IMG), jnp.int32)], axis=0
-    ).astype(jnp.bfloat16)
-    piece = jnp.concatenate([image_emb.T, extra], axis=0)
-
+    given = lax.dynamic_slice_in_dim(caption_emb, (1 - xl) * HALF, HALF, 0)
+    gained = exchange(given, other_half)
+    extra = lax.optimization_barrier(
+        jnp.concatenate(
+            [caption_count[None], pair_image.reshape(2, IMG), jnp.zeros((13, IMG), jnp.int32)], axis=0
+        )
+    )
+    piece = jnp.concatenate([image_emb.T, extra.astype(jnp.bfloat16)], axis=0)
+
+    received = [exchange(piece, first_axis(j)) for j in (1, 2, 3)]
     positions = jnp.arange(LOAD, dtype=jnp.int32)
     earlier = positions[None, :] < positions[:, None]
     same_owner = caption_owner[:, None] == caption_owner[None, :]
@@ -232,10 +243,6 @@
     marks = jnp.stack([caption_owner, me * 4 + rank], axis=1).astype(jnp.bfloat16)
     rows = jnp.concatenate([caption_emb, marks, jnp.zeros((LOAD, W - F - 2), jnp.bfloat16)], axis=1)
     kept = lax.dynamic_slice_in_dim(rows, xl * HALF, HALF, 0)
-    given = lax.dynamic_slice_in_dim(rows, (1 - xl) * HALF, HALF, 0)
-
-    received = [exchange(piece, first_axis(j)) for j in (1, 2, 3)]
-    gained = exchange(given, other_half)
     pieces, pair = call(
         join_kernel, (bf16(4, ROWS, IMG), bf16(2, HALF, W)), [VMEM] * 6
     )(piece, *received, kept, gained)
@@ -246,28 +253,36 @@
     )
     far = exchange(near, other_core)
     half = jnp.float16
-    image_own, image_1, caption_near, captions, turned = call(
+    image_own, image_1, caption_near, captions, turned, marks = call(
         near_stage_kernel,
-        (f32(4, F, IMG), f32(4, F, IMG), f32(CAPS, 2 * W), bf16(CAPS, 2 * W), bf16(2 * W, CAPS)),
+        (
+            f32(4, F, IMG), f32(4, F, IMG), f32(CAPS, 2 * F),
+            bf16(CAPS, 2 * F), bf16(2 * F, CAPS), bf16(CAPS, 128),
+        ),
         [SMEM, VMEM, VMEM, ANY, ANY],
         scratch=STAGE_SCRATCH, megabytes=10, flops=3 * DOT_FLOPS, nbytes=8_000_000,
     )(place, near, far, groups[0], groups[1])
+    image_1 = image_1.astype(half)
+    received_1 = exchange(image_1, second_axis(1))
+    caption_near = after(caption_near, image_1)
     image_2, image_3, caption_own, caption_far = call(
         far_stage_kernel,
-        (f32(4, F, IMG), f32(4, F, IMG), f32(CAPS // 2, 2 * W), f32(CAPS // 2, 2 * W)),
-        [SMEM, VMEM, VMEM, ANY, ANY, VMEM],
+        (f32(4, F, IMG), f32(4, F, IMG), f32(CAPS // 2, 2 * F), f32(CAPS // 2, 2 * F)),
+        [SMEM, VMEM, VMEM, VMEM, ANY, ANY, VMEM],
         scratch=STAGE_SCRATCH, megabytes=10, flops=3 * DOT_FLOPS, nbytes=8_000_000,
-    )(place, captions, turned, groups[2], groups[3], caption_near)
+    )(place, captions, turned, marks, groups[2], groups[3], caption_near)
+    image_2, image_3 = image_2.astype(half), image_3.astype(half)
+    caption_far = after(caption_far, (received_1, image_2, image_3)).astype(half)
     crossed = exchange(caption_far, other_core)
     image_received = [
-        exchange(image_1.astype(half), second_axis(1)),
-        exchange(image_2.astype(half), second_axis(2)),
-        exchange(image_3.astype(half), second_axis(3)),
+        received_1,
+        exchange(image_2, second_axis(2)),
+        exchange(image_3, second_axis(3)),
     ]
-    group_total = (caption_own + crossed).reshape(4, HALF, 2 * W)
-    caption_received = [
-        exchange(group_total[j].astype(half), along_z(j)) for j in (2, 1, 3)
-    ]
+    group_total = (caption_own + crossed.astype(jnp.float32)).reshape(4, HALF, 2 * F)
+    messages = [group_total[j].astype(half) for j in (2, 1, 3)]
+    caption_received = [exchange(m, along_z(j)) for m, j in zip(messages, (2, 1, 3))]
+    image_received = after(image_received, messages)
     line = image_own
     for value in image_received:
         line = line + value.astype(jnp.float32)
@@ -281,7 +296,7 @@
     for value in caption_received:
         both = both + value.astype(jnp.float32)
     both = both.astype(jnp.bfloat16)
-    mine, theirs = both[:, :F], both[:, W : W + F]
+    mine, theirs = both[:, :F], both[:, F:]
     returned = exchange(theirs, other_half)
     caption_grad = jnp.where(
         xl == 0,

time: 83.4 us -> 80.3 us (0.963)
  local copies, waits for them, and re-layouts: 3.72 us -> 1.55 us
  other arithmetic: 9.05 us -> 10.6 us
  waiting for transfers between devices: 26.3 us -> 25.2 us
  Pallas kernels: 10 us -> 8.91 us
    unnamed x12 -> x0, local copies, waits for them, and re-layouts: 3.09 us -> none
    convert_element_type x3 -> x5, other arithmetic: 0.24 us -> 2.93 us  [the longest x2 1.81 us: body(): image_2, image_3 = (image_2.astype(half), image_3.astype(half))]
    pallas_call x1, Pallas kernels: 5.41 us -> 4.02 us  [body(): call(far_stage_kernel, (f32(4, F, IMG), f32(4, F, IMG), f32(CAPS // 2, 2...]
    ppermute x22, waiting for transfers between devices: 26.3 us -> 25.2 us  [exchange(): return lax.ppermute(value, ('dp', 'mp'), pairs)]
    dynamic_slice x1, local copies, waits for them, and re-layouts: 0.04 us -> 0.91 us  [body(): given = lax.dynamic_slice_in_dim(caption_emb, (1 - xl) * HALF, HALF, 0)]
    concatenate x1 -> x2, other arithmetic: 1.05 us -> 1.67 us  [the longest x1 0.92 us: body(): piece = jnp.concatenate([image_emb.T, extra.astype(jnp.bfloat16)], axis=0)]
  transfers between devices with their start and end apart: 22 -> 22, of which waited for: 9 -> 10; matrix products, arithmetic and copies ran while one was open for 8% -> 11% of each run, Pallas kernels for 5% -> 11%
where the time goes in v3:
time: 80.3 us; the launch traced here: 80 us
  starting transfers between devices  33 us (41%)
  waiting for transfers between devices  25.2 us (31%)
  other arithmetic  10.6 us (13%)
  Pallas kernels  8.91 us (11%)
  local copies, waits for them, and re-layouts  1.55 us (2%)
  between operations  0.81 us (1%)
    ppermute x22, starting transfers between devices, exchange(): return lax.ppermute(value, ('dp', 'mp'), pairs)  33 us
    ppermute x22, waiting for transfers between devices, exchange(): return lax.ppermute(value, ('dp', 'mp'), pairs)  25.2 us
    pallas_call x1, Pallas kernels, body(): call(near_stage_kernel, (f32(4, F, IMG), f32(4, F, IMG), f32(CAPS, 2 * F)...  4.75 us
    pallas_call x1, Pallas kernels, body(): call(far_stage_kernel, (f32(4, F, IMG), f32(4, F, IMG), f32(CAPS // 2, 2...  4.02 us
    another operation x4, other arithmetic  2.41 us
    convert_element_type x2, other arithmetic, body(): image_2, image_3 = (image_2.astype(half), image_3.astype(half))  1.81 us
  transfers between devices with their start and end apart: 22, of which 10 were waited for; matrix products, arithmetic and copies ran while one was open for 11% of the time, Pallas kernels for 11%

profile of v3, /device:TPU:0, one launch (start us, length us, event | category | flops | bytes accessed | tf_op | source)
XLA Modules:
  0.0 80.0 jit_solution(8071693398070502674)
XLA Ops:
  0.7 0.8 add_add_fusion
  1.5 0.9 %pad_maximum_fusion.piece_ref = bf16[592,128]{1,0:T(8,128)(2,1)S(1)} fusion(bf16[16,128]{1,0:T(8,128)(2,1)S(1)} %convert_element_type.70, bf16[576,128]{1,0:T(8,128)(2,1)} %bitcast.24), kind=kLoop, calls=%fused_computation.18 | loop fusion | flops 303104 | bytes 303104 | tf_op jit(solution)/shard_map/concatenate | solution.py:236
  2.4 2.9 %collective-permute-start.2 = (bf16[592,128]{1,0:T(8,128)(2,1)S(1)}, bf16[592,128]{1,0:T(8,128)(2,1)S(1)}, u32[]{:S(2)}, u32[]{:S(2)}) collective-permute-start(bf16[592,128]{1,0:T(8,128)(2,1)S(1)} %pad_maximum_fusion.piece_ref), channel_id=1, source_target_pairs={{0,65},{1,64},{2,50},{3,51},{4,69},{5,68},{6,54},{7,55},{8,73},{9,... | collective-permute-start | bytes 454664 | tf_op jit(solution)/shard_map/ppermute | solution.py:29
  5.3 0.8 %collective-permute-start.1 = (bf16[592,128]{1,0:T(8,128)(2,1)S(1)}, bf16[592,128]{1,0:T(8,128)(2,1)S(1)}, u32[]{:S(2)}, u32[]{:S(2)}) collective-permute-start(bf16[592,128]{1,0:T(8,128)(2,1)S(1)} %pad_maximum_fusion.piece_ref), channel_id=1, source_target_pairs={{0,64},{1,65},{2,34},{3,35},{4,68},{5,69},{6,38},{7,39},{8,72},{9,... | collective-permute-start | bytes 454664 | tf_op jit(solution)/shard_map/ppermute | solution.py:29
  6.1 0.5 collective-permute-start
  6.6 0.9 %constant_dynamic-slice_fusion = bf16[96,576]{1,0:T(8,128)(2,1)S(1)} fusion(bf16[192,576]{1,0:T(8,128)(2,1)} %param.6, s32[]{:T(128)S(6)} %select_n.15), kind=kLoop, calls=%fused_computation.28 | loop fusion | bytes 221188 | tf_op jit(solution)/shard_map/dynamic_slice | solution.py:229
  7.5 1.7 %collective-permute-start.3 = (bf16[96,576]{1,0:T(8,128)(2,1)S(1)}, bf16[96,576]{1,0:T(8,128)(2,1)S(1)}, u32[]{:S(2)}, u32[]{:S(2)}) collective-permute-start(bf16[96,576]{1,0:T(8,128)(2,1)S(1)} %constant_dynamic-slice_fusion), channel_id=1, source_target_pairs={{0,1},{1,0},{2,3},{3,2},{4,5},{5,4},{6,7},{7,6},{8,9},{9,8},{10,11... | collective-permute-start | bytes 331784 | tf_op jit(solution)/shard_map/ppermute | solution.py:29
  9.1 0.7 convert.18
  9.8 0.9 %convert_reduce_fusion = s32[192]{0:T(256)S(1)} fusion(s32[192]{0:T(256)} %param.8), kind=kLoop, calls=%fused_computation.15 | loop fusion | flops 184128 | bytes 1536 | tf_op jit(solution)/shard_map/reduce_sum | solution.py:242
  10.8 0.1 add.67
  10.9 0.1 stack.8
  11.1 1.0 %fusion.11.kept_ref = bf16[96,640]{1,0:T(8,128)(2,1)S(1)} fusion(s32[]{:T(128)S(6)} %select_n.14, bf16[192,576]{1,0:T(8,128)(2,1)} %param.6, bf16[192,1]{1,0:T(8,128)(2,1)S(1)} %stack.8, bf16[192,1]{1,0:T(8,128)(2,1)S(1)} %add.67, bf16[640]{0:T(1024)(128)(2,1)S(1)} %pad.7.clone), kind=kLoop, calls=%fused_computation.25 | loop fusion | flops 491520 | bytes 346116 | tf_op jit(solution)/shard_map/concatenate | solution.py:244
  12.1 2.0 %collective-permute-done.3.gained_ref = bf16[96,576]{1,0:T(8,128)(2,1)S(1)} collective-permute-done((bf16[96,576]{1,0:T(8,128)(2,1)S(1)}, bf16[96,576]{1,0:T(8,128)(2,1)S(1)}, u32[]{:S(2)}, u32[]{:S(2)}) %collective-permute-start.3) | collective-permute-done | bytes 110624 | tf_op jit(solution)/shard_map/ppermute | solution.py:29
  14.1 3.2 %collective-permute-start.8 = (bf16[4,592,128]{2,1,0:T(8,128)(2,1)S(1)}, bf16[4,592,128]{2,1,0:T(8,128)(2,1)S(1)}, u32[]{:S(2)}, u32[]{:S(2)}) collective-permute-start(bf16[4,592,128]{2,1,0:T(8,128)(2,1)S(1)} %get-tuple-element.20.a_ref), channel_id=1, source_target_pairs={{0,48},{1,49},{2,67},{3,66},{4,52},{5,53},{6,71},{7,70},{8,56},{9,... | collective-permute-start | bytes 1818632 | tf_op jit(solution)/shard_map/ppermute | solution.py:29
  17.3 0.1 collective-permute-start.7
  17.4 4.0 %collective-permute-start.6 = (bf16[2,96,640]{2,1,0:T(8,128)(2,1)S(1)}, bf16[2,96,640]{2,1,0:T(8,128)(2,1)S(1)}, u32[]{:S(2)}, u32[]{:S(2)}) collective-permute-start(bf16[2,96,640]{2,1,0:T(8,128)(2,1)S(1)} %get-tuple-element.19.pair_ref), channel_id=1, source_target_pairs={{0,12},{1,13},{2,14},{3,15},{4,8},{5,9},{6,10},{7,11},{8,4},{9,5},... | collective-permute-start | bytes 737288 | tf_op jit(solution)/shard_map/ppermute | solution.py:29
  21.5 0.9 %collective-permute-start.4 = (bf16[2,96,640]{2,1,0:T(8,128)(2,1)S(1)}, bf16[2,96,640]{2,1,0:T(8,128)(2,1)S(1)}, u32[]{:S(2)}, u32[]{:S(2)}) collective-permute-start(bf16[2,96,640]{2,1,0:T(8,128)(2,1)S(1)} %get-tuple-element.19.pair_ref), channel_id=1, source_target_pairs={{0,4},{1,5},{2,6},{3,7},{4,0},{5,1},{6,2},{7,3},{8,12},{9,13},{10,... | collective-permute-start | bytes 737288 | tf_op jit(solution)/shard_map/ppermute | solution.py:29
  22.3 7.2 %collective-permute-done.6.r3_ref = bf16[2,96,640]{2,1,0:T(8,128)(2,1)S(1)} collective-permute-done((bf16[2,96,640]{2,1,0:T(8,128)(2,1)S(1)}, bf16[2,96,640]{2,1,0:T(8,128)(2,1)S(1)}, u32[]{:S(2)}, u32[]{:S(2)}) %collective-permute-start.6) | collective-permute-done | bytes 245792 | tf_op jit(solution)/shard_map/ppermute | solution.py:29
  29.5 1.1 %collective-permute-done.5.r2_ref = bf16[2,96,640]{2,1,0:T(8,128)(2,1)S(1)} collective-permute-done((bf16[2,96,640]{2,1,0:T(8,128)(2,1)S(1)}, bf16[2,96,640]{2,1,0:T(8,128)(2,1)S(1)}, u32[]{:S(2)}, u32[]{:S(2)}) %collective-permute-start.5) | collective-permute-done | bytes 245792 | tf_op jit(solution)/shard_map/ppermute | solution.py:29
  30.6 0.2 collective-permute-done.4.r1_ref
  31.0 3.1 %collective-permute-start.11 = (bf16[4,592,128]{2,1,0:T(8,128)(2,1)S(1)}, bf16[4,592,128]{2,1,0:T(8,128)(2,1)S(1)}, u32[]{:S(2)}, u32[]{:S(2)}) collective-permute-start(bf16[4,592,128]{2,1,0:T(8,128)(2,1)S(1)} %get-tuple-element.20.a_ref), channel_id=1, source_target_pairs={{0,32},{1,33},{2,66},{3,67},{4,36},{5,37},{6,70},{7,71},{8,40},{9,... | collective-permute-start | bytes 1818632 | tf_op jit(solution)/shard_map/ppermute | solution.py:29
  34.1 4.7 %shard_map.70 = (f32[4,576,128]{2,1,0:T(8,128)S(1)}, f32[4,576,128]{2,1,0:T(8,128)S(1)}, f32[768,1152]{1,0:T(8,128)S(1)}, bf16[768,1152]{1,0:T(8,128)(2,1)S(1)},...) custom-call(s32[1]{0:T(128)} %bitcast.place_ref, bf16[4,2,96,640]{3,2,1,0:T(8,128)(2,1)S(1)} %shard_map.69.near_ref, ...), custom_call_target="tpu_custom_call" | custom-call | flops 2717908992 | bytes 8000000 | tf_op jit(solution)/shard_map/pallas_call | solution.py:256
  39.0 1.0 %collective-permute-start.10 = (f16[4,576,128]{2,1,0:T(8,128)(2,1)S(1)}, f16[4,576,128]{2,1,0:T(8,128)(2,1)S(1)}, u32[]{:S(2)}, u32[]{:S(2)}) collective-permute-start(f16[4,576,128]{2,1,0:T(8,128)(2,1)S(1)} %convert_element_type.72), channel_id=1, source_target_pairs={{0,16},{1,17},{2,3},{3,2},{4,20},{5,21},{6,7},{7,6},{8,24},{9,25},... | collective-permute-start | bytes 1769480 | tf_op jit(solution)/shard_map/ppermute | solution.py:29
  40.0 2.7 %collective-permute-done.11.a_ref = bf16[4,592,128]{2,1,0:T(8,128)(2,1)S(1)} collective-permute-done((bf16[4,592,128]{2,1,0:T(8,128)(2,1)S(1)}, bf16[4,592,128]{2,1,0:T(8,128)(2,1)S(1)}, u32[]{:S(2)}, u32[]{:S(2)}) %collective-permute-start.11) | collective-permute-done | bytes 606240 | tf_op jit(solution)/shard_map/ppermute | solution.py:29
  42.7 4.0 %shard_map.71 = (f32[4,576,128]{2,1,0:T(8,128)S(1)}, f32[4,576,128]{2,1,0:T(8,128)S(1)}, f32[384,1152]{1,0:T(8,128)S(1)}, f32[384,1152]{1,0:T(8,128)S(1)}) custom-call(s32[1]{0:T(128)} %bitcast.place_ref, bf16[768,1152]{1,0:T(8,128)(2,1)S(1)} %get-tuple-element.23.captions_ref, bf16[1152,768]{1,0:T(8,128)(2,1)S(1)} %get-tuple-element.24.turned_ref, ...), custom_call_target="tpu_custom_call" | custom-call | flops 2717908992 | bytes 8000000 | tf_op jit(solution)/shard_map/pallas_call | solution.py:268
  46.7 0.9 %convert_element_type.73 = f16[4,576,128]{2,1,0:T(8,128)(2,1)} convert(f32[4,576,128]{2,1,0:T(8,128)S(1)} %get-tuple-element.28) | non-fusion elementwise | flops 294912 | bytes 1769472 | tf_op jit(solution)/shard_map/convert_element_type | solution.py:274
  47.6 0.9 %convert_element_type.74 = f16[4,576,128]{2,1,0:T(8,128)(2,1)} convert(f32[4,576,128]{2,1,0:T(8,128)S(1)} %get-tuple-element.29) | non-fusion elementwise | flops 294912 | bytes 1769472 | tf_op jit(solution)/shard_map/convert_element_type | solution.py:274
  48.5 0.6 collective-permute-done.10
  49.2 1.0 %convert_element_type.75 = f16[384,1152]{1,0:T(8,128)(2,1)} convert(f32[384,1152]{1,0:T(8,128)S(1)} %get-tuple-element.32) | non-fusion elementwise | flops 442368 | bytes 2654208 | tf_op jit(solution)/shard_map/convert_element_type | solution.py:275
  50.2 2.2 %collective-permute-start.13 = (f16[4,576,128]{2,1,0:T(8,128)(2,1)}, f16[4,576,128]{2,1,0:T(8,128)(2,1)S(1)}, u32[]{:S(2)}, u32[]{:S(2)}) collective-permute-start(f16[4,576,128]{2,1,0:T(8,128)(2,1)} %convert_element_type.74), channel_id=1, source_target_pairs={{0,48},{1,49},{2,67},{3,66},{4,52},{5,53},{6,71},{7,70},{8,56},{9,... | collective-permute-start | bytes 1769480 | tf_op jit(solution)/shard_map/ppermute | solution.py:29
  52.4 1.2 %collective-permute-start.12 = (f16[4,576,128]{2,1,0:T(8,128)(2,1)}, f16[4,576,128]{2,1,0:T(8,128)(2,1)S(1)}, u32[]{:S(2)}, u32[]{:S(2)}) collective-permute-start(f16[4,576,128]{2,1,0:T(8,128)(2,1)} %convert_element_type.73), channel_id=1, source_target_pairs={{0,32},{1,33},{2,66},{3,67},{4,36},{5,37},{6,70},{7,71},{8,40},{9,... | collective-permute-start | bytes 1769480 | tf_op jit(solution)/shard_map/ppermute | solution.py:29
  53.6 1.4 %fusion.13 = (f16[384,1152]{1,0:T(8,128)(2,1)S(1)}, f32[384,1152]{1,0:T(8,128)S(1)}) fusion(f32[384,1152]{1,0:T(8,128)S(1)} %get-tuple-element.30, f16[384,1152]{1,0:T(8,128)(2,1)} %collective-permute-done.14), kind=kLoop, calls=%fused_computation.30 | loop fusion | flops 1327104 | bytes 5308416 | tf_op jit(solution)/shard_map/convert.5
  55.0 0.1 fusion.14
  55.1 3.0 %collective-permute-start.20 = (f16[96,1152]{1,0:T(8,128)(2,1)S(1)}, f16[96,1152]{1,0:T(8,128)(2,1)S(1)}, u32[]{:S(2)}, u32[]{:S(2)}) collective-permute-start(f16[96,1152]{1,0:T(8,128)(2,1)S(1)} %get-tuple-element.40), channel_id=1, source_target_pairs={{0,12},{1,13},{2,14},{3,15},{4,8},{5,9},{6,10},{7,11},{8,4},{9,5},... | collective-permute-start | bytes 663560 | tf_op jit(solution)/shard_map/ppermute | solution.py:29
  58.2 1.7 %collective-permute-start.18 = (f16[96,1152]{1,0:T(8,128)(2,1)S(1)}, f16[96,1152]{1,0:T(8,128)(2,1)S(1)}, u32[]{:S(2)}, u32[]{:S(2)}) collective-permute-start(f16[96,1152]{1,0:T(8,128)(2,1)S(1)} %get-tuple-element.42), channel_id=1, source_target_pairs={{0,8},{1,9},{2,10},{3,11},{4,12},{5,13},{6,14},{7,15},{8,0},{9,1},... | collective-permute-start | bytes 663560 | tf_op jit(solution)/shard_map/ppermute | solution.py:29
  59.9 7.9 %collective-permute-done.13 = f16[4,576,128]{2,1,0:T(8,128)(2,1)S(1)} collective-permute-done((f16[4,576,128]{2,1,0:T(8,128)(2,1)}, f16[4,576,128]{2,1,0:T(8,128)(2,1)S(1)}, u32[]{:S(2)}, u32[]{:S(2)}) %collective-permute-start.13) | collective-permute-done | bytes 589856 | tf_op jit(solution)/shard_map/ppermute | solution.py:29
  67.8 0.3 fusion.12
  68.2 0.1 slice_bitcast_fusion.3
  68.3 1.8 %collective-permute-start.15 = (f16[576,128]{1,0:T(8,128)(2,1)S(1)}, f16[576,128]{1,0:T(8,128)(2,1)S(1)}, u32[]{:S(2)}, u32[]{:S(2)}) collective-permute-start(f16[576,128]{1,0:T(8,128)(2,1)S(1)} %get-tuple-element.43), channel_id=1, source_target_pairs={{0,64},{1,65},{2,34},{3,35},{4,68},{5,69},{6,38},{7,39},{8,72},{9,... | collective-permute-start | bytes 442376 | tf_op jit(solution)/shard_map/ppermute | solution.py:29
  70.1 2.7 %collective-permute-start.17 = (f16[576,128]{1,0:T(8,128)(2,1)S(1)}, f16[576,128]{1,0:T(8,128)(2,1)S(1)}, u32[]{:S(2)}, u32[]{:S(2)}) collective-permute-start(f16[576,128]{1,0:T(8,128)(2,1)S(1)} %get-tuple-element.44), channel_id=1, source_target_pairs={{0,65},{1,64},{2,50},{3,51},{4,69},{5,68},{6,54},{7,55},{8,73},{9,... | collective-permute-start | bytes 442376 | tf_op jit(solution)/shard_map/ppermute | solution.py:29
  72.8 0.1 fusion.2
  72.9 0.1 fusion.15
  73.0 2.1 %collective-permute-start.21 = (bf16[96,576]{1,0:T(8,128)(2,1)S(1)}, bf16[96,576]{1,0:T(8,128)(2,1)S(1)}, u32[]{:S(2)}, u32[]{:S(2)}) collective-permute-start(bf16[96,576]{1,0:T(8,128)(2,1)S(1)} %get-tuple-element.47), channel_id=1, source_target_pairs={{0,1},{1,0},{2,3},{3,2},{4,5},{5,4},{6,7},{7,6},{8,9},{9,8},{10,11... | collective-permute-start | bytes 331784 | tf_op jit(solution)/shard_map/ppermute | solution.py:29
  75.1 1.5 %collective-permute-done.17 = f16[576,128]{1,0:T(8,128)(2,1)S(1)} collective-permute-done((f16[576,128]{1,0:T(8,128)(2,1)S(1)}, f16[576,128]{1,0:T(8,128)(2,1)S(1)}, u32[]{:S(2)}, u32[]{:S(2)}) %collective-permute-start.17) | collective-permute-done | bytes 147488 | tf_op jit(solution)/shard_map/ppermute | solution.py:29
  76.6 1.3 %collective-permute-done.16 = f16[576,128]{1,0:T(8,128)(2,1)S(1)} collective-permute-done((f16[576,128]{1,0:T(8,128)(2,1)S(1)}, f16[576,128]{1,0:T(8,128)(2,1)S(1)}, u32[]{:S(2)}, u32[]{:S(2)}) %collective-permute-start.16) | collective-permute-done | bytes 147488 | tf_op jit(solution)/shard_map/ppermute | solution.py:29
  77.9 0.8 fusion.8
  78.7 0.6 collective-permute-done.21
  79.2 0.7 maximum_select_fusion
  (26 shorter events, 0.5 us)
Async XLA Ops:
  2.4 11.6 %collective-permute-start.2 = (bf16[592,128]{1,0:T(8,128)(2,1)S(1)}, bf16[592,128]{1,0:T(8,128)(2,1)S(1)}, u32[]{:S(2)}, u32[]{:S(2)}) collective-permute-start(bf16[592,128]{1,0:T(8,128)(2,1)S(1)} %pad_maximum_fusion.piece_ref), channel_id=1, source_target_pairs={{0,65},{1,64},{2,50},{3,51},{4,69},{5,68},{6,54},{7,55},{8,73},{9,... | collective-permute-start | bytes 454664 | tf_op jit(solution)/shard_map/ppermute | solution.py:29
  5.3 8.7 %collective-permute-start.1 = (bf16[592,128]{1,0:T(8,128)(2,1)S(1)}, bf16[592,128]{1,0:T(8,128)(2,1)S(1)}, u32[]{:S(2)}, u32[]{:S(2)}) collective-permute-start(bf16[592,128]{1,0:T(8,128)(2,1)S(1)} %pad_maximum_fusion.piece_ref), channel_id=1, source_target_pairs={{0,64},{1,65},{2,34},{3,35},{4,68},{5,69},{6,38},{7,39},{8,72},{9,... | collective-permute-start | bytes 454664 | tf_op jit(solution)/shard_map/ppermute | solution.py:29
  6.1 7.9 %collective-permute-start = (bf16[592,128]{1,0:T(8,128)(2,1)S(1)}, bf16[592,128]{1,0:T(8,128)(2,1)S(1)}, u32[]{:S(2)}, u32[]{:S(2)}) collective-permute-start(bf16[592,128]{1,0:T(8,128)(2,1)S(1)} %pad_maximum_fusion.piece_ref), channel_id=1, source_target_pairs={{0,1},{1,0},{2,18},{3,19},{4,5},{5,4},{6,22},{7,23},{8,9},{9,8},{1... | collective-permute-start | bytes 454664 | tf_op jit(solution)/shard_map/ppermute | solution.py:29
  7.5 6.5 %collective-permute-start.3 = (bf16[96,576]{1,0:T(8,128)(2,1)S(1)}, bf16[96,576]{1,0:T(8,128)(2,1)S(1)}, u32[]{:S(2)}, u32[]{:S(2)}) collective-permute-start(bf16[96,576]{1,0:T(8,128)(2,1)S(1)} %constant_dynamic-slice_fusion), channel_id=1, source_target_pairs={{0,1},{1,0},{2,3},{3,2},{4,5},{5,4},{6,7},{7,6},{8,9},{9,8},{10,11... | collective-permute-start | bytes 331784 | tf_op jit(solution)/shard_map/ppermute | solution.py:29
  14.1 16.7 %collective-permute-start.8 = (bf16[4,592,128]{2,1,0:T(8,128)(2,1)S(1)}, bf16[4,592,128]{2,1,0:T(8,128)(2,1)S(1)}, u32[]{:S(2)}, u32[]{:S(2)}) collective-permute-start(bf16[4,592,128]{2,1,0:T(8,128)(2,1)S(1)} %get-tuple-element.20.a_ref), channel_id=1, source_target_pairs={{0,48},{1,49},{2,67},{3,66},{4,52},{5,53},{6,71},{7,70},{8,56},{9,... | collective-permute-start | bytes 1818632 | tf_op jit(solution)/shard_map/ppermute | solution.py:29
  17.3 13.6 %collective-permute-start.7 = (bf16[4,592,128]{2,1,0:T(8,128)(2,1)S(1)}, bf16[4,592,128]{2,1,0:T(8,128)(2,1)S(1)}, u32[]{:S(2)}, u32[]{:S(2)}) collective-permute-start(bf16[4,592,128]{2,1,0:T(8,128)(2,1)S(1)} %get-tuple-element.20.a_ref), channel_id=1, source_target_pairs={{0,16},{1,17},{2,3},{3,2},{4,20},{5,21},{6,7},{7,6},{8,24},{9,25},... | collective-permute-start | bytes 1818632 | tf_op jit(solution)/shard_map/ppermute | solution.py:29
  17.4 12.1 %collective-permute-start.6 = (bf16[2,96,640]{2,1,0:T(8,128)(2,1)S(1)}, bf16[2,96,640]{2,1,0:T(8,128)(2,1)S(1)}, u32[]{:S(2)}, u32[]{:S(2)}) collective-permute-start(bf16[2,96,640]{2,1,0:T(8,128)(2,1)S(1)} %get-tuple-element.19.pair_ref), channel_id=1, source_target_pairs={{0,12},{1,13},{2,14},{3,15},{4,8},{5,9},{6,10},{7,11},{8,4},{9,5},... | collective-permute-start | bytes 737288 | tf_op jit(solution)/shard_map/ppermute | solution.py:29
  21.5 9.1 %collective-permute-start.5 = (bf16[2,96,640]{2,1,0:T(8,128)(2,1)S(1)}, bf16[2,96,640]{2,1,0:T(8,128)(2,1)S(1)}, u32[]{:S(2)}, u32[]{:S(2)}) collective-permute-start(bf16[2,96,640]{2,1,0:T(8,128)(2,1)S(1)} %get-tuple-element.19.pair_ref), channel_id=1, source_target_pairs={{0,8},{1,9},{2,10},{3,11},{4,12},{5,13},{6,14},{7,15},{8,0},{9,1},... | collective-permute-start | bytes 737288 | tf_op jit(solution)/shard_map/ppermute | solution.py:29
  21.5 9.4 %collective-permute-start.4 = (bf16[2,96,640]{2,1,0:T(8,128)(2,1)S(1)}, bf16[2,96,640]{2,1,0:T(8,128)(2,1)S(1)}, u32[]{:S(2)}, u32[]{:S(2)}) collective-permute-start(bf16[2,96,640]{2,1,0:T(8,128)(2,1)S(1)} %get-tuple-element.19.pair_ref), channel_id=1, source_target_pairs={{0,4},{1,5},{2,6},{3,7},{4,0},{5,1},{6,2},{7,3},{8,12},{9,13},{10,... | collective-permute-start | bytes 737288 | tf_op jit(solution)/shard_map/ppermute | solution.py:29
  30.9 3.2 %collective-permute-start.9 = (bf16[4,2,96,640]{3,2,1,0:T(8,128)(2,1)S(1)}, bf16[4,2,96,640]{3,2,1,0:T(8,128)(2,1)S(1)}, u32[]{:S(2)}, u32[]{:S(2)}) collective-permute-start(bf16[4,2,96,640]{3,2,1,0:T(8,128)(2,1)S(1)} %shard_map.69.near_ref), channel_id=1, source_target_pairs={{0,2},{1,3},{2,0},{3,1},{4,6},{5,7},{6,4},{7,5},{8,10},{9,11},{10,... | collective-permute-start | bytes 2949128 | tf_op jit(solution)/shard_map/ppermute | solution.py:29
  31.0 11.6 %collective-permute-start.11 = (bf16[4,592,128]{2,1,0:T(8,128)(2,1)S(1)}, bf16[4,592,128]{2,1,0:T(8,128)(2,1)S(1)}, u32[]{:S(2)}, u32[]{:S(2)}) collective-permute-start(bf16[4,592,128]{2,1,0:T(8,128)(2,1)S(1)} %get-tuple-element.20.a_ref), channel_id=1, source_target_pairs={{0,32},{1,33},{2,66},{3,67},{4,36},{5,37},{6,70},{7,71},{8,40},{9,... | collective-permute-start | bytes 1818632 | tf_op jit(solution)/shard_map/ppermute | solution.py:29
  39.0 10.2 %collective-permute-start.10 = (f16[4,576,128]{2,1,0:T(8,128)(2,1)S(1)}, f16[4,576,128]{2,1,0:T(8,128)(2,1)S(1)}, u32[]{:S(2)}, u32[]{:S(2)}) collective-permute-start(f16[4,576,128]{2,1,0:T(8,128)(2,1)S(1)} %convert_element_type.72), channel_id=1, source_target_pairs={{0,16},{1,17},{2,3},{3,2},{4,20},{5,21},{6,7},{7,6},{8,24},{9,25},... | collective-permute-start | bytes 1769480 | tf_op jit(solution)/shard_map/ppermute | solution.py:29
  50.2 3.4 %collective-permute-start.14 = (f16[384,1152]{1,0:T(8,128)(2,1)}, f16[384,1152]{1,0:T(8,128)(2,1)}, u32[]{:S(2)}, u32[]{:S(2)}) collective-permute-start(f16[384,1152]{1,0:T(8,128)(2,1)} %convert_element_type.75), channel_id=1, source_target_pairs={{0,2},{1,3},{2,0},{3,1},{4,6},{5,7},{6,4},{7,5},{8,10},{9,11},{10,... | collective-permute-start | bytes 2654216 | tf_op jit(solution)/shard_map/ppermute | solution.py:29
  50.2 17.6 %collective-permute-start.13 = (f16[4,576,128]{2,1,0:T(8,128)(2,1)}, f16[4,576,128]{2,1,0:T(8,128)(2,1)S(1)}, u32[]{:S(2)}, u32[]{:S(2)}) collective-permute-start(f16[4,576,128]{2,1,0:T(8,128)(2,1)} %convert_element_type.74), channel_id=1, source_target_pairs={{0,48},{1,49},{2,67},{3,66},{4,52},{5,53},{6,71},{7,70},{8,56},{9,... | collective-permute-start | bytes 1769480 | tf_op jit(solution)/shard_map/ppermute | solution.py:29
  52.4 15.4 %collective-permute-start.12 = (f16[4,576,128]{2,1,0:T(8,128)(2,1)}, f16[4,576,128]{2,1,0:T(8,128)(2,1)S(1)}, u32[]{:S(2)}, u32[]{:S(2)}) collective-permute-start(f16[4,576,128]{2,1,0:T(8,128)(2,1)} %convert_element_type.73), channel_id=1, source_target_pairs={{0,32},{1,33},{2,66},{3,67},{4,36},{5,37},{6,70},{7,71},{8,40},{9,... | collective-permute-start | bytes 1769480 | tf_op jit(solution)/shard_map/ppermute | solution.py:29
  55.1 17.7 %collective-permute-start.20 = (f16[96,1152]{1,0:T(8,128)(2,1)S(1)}, f16[96,1152]{1,0:T(8,128)(2,1)S(1)}, u32[]{:S(2)}, u32[]{:S(2)}) collective-permute-start(f16[96,1152]{1,0:T(8,128)(2,1)S(1)} %get-tuple-element.40), channel_id=1, source_target_pairs={{0,12},{1,13},{2,14},{3,15},{4,8},{5,9},{6,10},{7,11},{8,4},{9,5},... | collective-permute-start | bytes 663560 | tf_op jit(solution)/shard_map/ppermute | solution.py:29
  58.2 14.6 %collective-permute-start.19 = (f16[96,1152]{1,0:T(8,128)(2,1)S(1)}, f16[96,1152]{1,0:T(8,128)(2,1)S(1)}, u32[]{:S(2)}, u32[]{:S(2)}) collective-permute-start(f16[96,1152]{1,0:T(8,128)(2,1)S(1)} %get-tuple-element.41), channel_id=1, source_target_pairs={{0,4},{1,5},{2,6},{3,7},{4,0},{5,1},{6,2},{7,3},{8,12},{9,13},{10,... | collective-permute-start | bytes 663560 | tf_op jit(solution)/shard_map/ppermute | solution.py:29
  58.2 14.6 %collective-permute-start.18 = (f16[96,1152]{1,0:T(8,128)(2,1)S(1)}, f16[96,1152]{1,0:T(8,128)(2,1)S(1)}, u32[]{:S(2)}, u32[]{:S(2)}) collective-permute-start(f16[96,1152]{1,0:T(8,128)(2,1)S(1)} %get-tuple-element.42), channel_id=1, source_target_pairs={{0,8},{1,9},{2,10},{3,11},{4,12},{5,13},{6,14},{7,15},{8,0},{9,1},... | collective-permute-start | bytes 663560 | tf_op jit(solution)/shard_map/ppermute | solution.py:29
  68.3 6.8 %collective-permute-start.15 = (f16[576,128]{1,0:T(8,128)(2,1)S(1)}, f16[576,128]{1,0:T(8,128)(2,1)S(1)}, u32[]{:S(2)}, u32[]{:S(2)}) collective-permute-start(f16[576,128]{1,0:T(8,128)(2,1)S(1)} %get-tuple-element.43), channel_id=1, source_target_pairs={{0,64},{1,65},{2,34},{3,35},{4,68},{5,69},{6,38},{7,39},{8,72},{9,... | collective-permute-start | bytes 442376 | tf_op jit(solution)/shard_map/ppermute | solution.py:29
  70.1 6.5 %collective-permute-start.17 = (f16[576,128]{1,0:T(8,128)(2,1)S(1)}, f16[576,128]{1,0:T(8,128)(2,1)S(1)}, u32[]{:S(2)}, u32[]{:S(2)}) collective-permute-start(f16[576,128]{1,0:T(8,128)(2,1)S(1)} %get-tuple-element.44), channel_id=1, source_target_pairs={{0,65},{1,64},{2,50},{3,51},{4,69},{5,68},{6,54},{7,55},{8,73},{9,... | collective-permute-start | bytes 442376 | tf_op jit(solution)/shard_map/ppermute | solution.py:29
  72.8 5.1 %collective-permute-start.16 = (f16[576,128]{1,0:T(8,128)(2,1)S(1)}, f16[576,128]{1,0:T(8,128)(2,1)S(1)}, u32[]{:S(2)}, u32[]{:S(2)}) collective-permute-start(f16[576,128]{1,0:T(8,128)(2,1)S(1)} %get-tuple-element.45), channel_id=1, source_target_pairs={{0,1},{1,0},{2,18},{3,19},{4,5},{5,4},{6,22},{7,23},{8,9},{9,8},{1... | collective-permute-start | bytes 442376 | tf_op jit(solution)/shard_map/ppermute | solution.py:29
  73.0 6.2 %collective-permute-start.21 = (bf16[96,576]{1,0:T(8,128)(2,1)S(1)}, bf16[96,576]{1,0:T(8,128)(2,1)S(1)}, u32[]{:S(2)}, u32[]{:S(2)}) collective-permute-start(bf16[96,576]{1,0:T(8,128)(2,1)S(1)} %get-tuple-element.47), channel_id=1, source_target_pairs={{0,1},{1,0},{2,3},{3,2},{4,5},{5,4},{6,7},{7,6},{8,9},{9,8},{10,11... | collective-permute-start | bytes 331784 | tf_op jit(solution)/shard_map/ppermute | solution.py:29

commit v4 on v3

--- a/solution.py
+++ b/solution.py
@@ -286,18 +286,19 @@
     line = image_own
     for value in image_received:
         line = line + value.astype(jnp.float32)
-    line_received = [exchange(line[j].astype(half), first_axis(j)) for j in (2, 1, 3)]
-    total = line[0]
-    for value in line_received:
-        total = total + value.astype(jnp.float32)
-    image_grad = total.astype(jnp.bfloat16).T
-
     both = group_total[0]
     for value in caption_received:
         both = both + value.astype(jnp.float32)
     both = both.astype(jnp.bfloat16)
     mine, theirs = both[:, :F], both[:, F:]
     returned = exchange(theirs, other_half)
+    line = after(line, theirs)
+    line_received = [exchange(line[j].astype(half), first_axis(j)) for j in (2, 1, 3)]
+    total = line[0]
+    for value in line_received:
+        total = total + value.astype(jnp.float32)
+    image_grad = total.astype(jnp.bfloat16).T
+
     caption_grad = jnp.where(
         xl == 0,
         jnp.concatenate([mine, returned], axis=0),

time: 80.3 us -> 79.6 us (level)
  waiting for transfers between devices: 25.2 us -> 29.6 us
  other arithmetic: 10.6 us -> 6.77 us
  starting transfers between devices: 33 us -> 31.6 us
    ppermute x22, waiting for transfers between devices: 25.2 us -> 29.6 us  [exchange(): return lax.ppermute(value, ('dp', 'mp'), pairs)]
    convert_element_type x2, other arithmetic: 1.81 us -> 0.16 us  [body(): image_2, image_3 = (image_2.astype(half), image_3.astype(half))]
    another operation x4, other arithmetic: 2.41 us -> 0.98 us
    ppermute x22, starting transfers between devices: 33 us -> 31.6 us  [exchange(): return lax.ppermute(value, ('dp', 'mp'), pairs)]
    convert_element_type x1, other arithmetic: 1.03 us -> 0.1 us  [body(): after(caption_far, (received_1, image_2, image_3)).astype(half)]
  transfers between devices with their start and end apart: 22 -> 22, of which waited for: 10 -> 11; matrix products, arithmetic and copies ran while one was open for 11% -> 7% of each run, Pallas kernels for 11% -> 11%
where the time goes in v4:
time: 79.6 us; the launch traced here: 79.4 us
  starting transfers between devices  31.6 us (40%)
  waiting for transfers between devices  29.6 us (37%)
  Pallas kernels  9.05 us (11%)
  other arithmetic  6.77 us (9%)
  local copies, waits for them, and re-layouts  1.55 us (2%)
  between operations  0.84 us (1%)
    ppermute x22, starting transfers between devices, exchange(): return lax.ppermute(value, ('dp', 'mp'), pairs)  31.6 us
    ppermute x22, waiting for transfers between devices, exchange(): return lax.ppermute(value, ('dp', 'mp'), pairs)  29.6 us
    pallas_call x1, Pallas kernels, body(): call(near_stage_kernel, (f32(4, F, IMG), f32(4, F, IMG), f32(CAPS, 2 * F)...  4.79 us
    pallas_call x1, Pallas kernels, body(): call(far_stage_kernel, (f32(4, F, IMG), f32(4, F, IMG), f32(CAPS // 2, 2...  4.12 us
  transfers between devices with their start and end apart: 22, of which 11 were waited for; matrix products, arithmetic and copies ran while one was open for 7% of the time, Pallas kernels for 11%

profile of v4, /device:TPU:0, one launch (start us, length us, event | category | flops | bytes accessed | tf_op | source)
XLA Modules:
  0.0 79.4 jit_solution(415569369617311192)
XLA Ops:
  0.7 0.8 add_add_fusion
  1.5 0.9 %pad_maximum_fusion.piece_ref = bf16[592,128]{1,0:T(8,128)(2,1)S(1)} fusion(bf16[16,128]{1,0:T(8,128)(2,1)S(1)} %convert_element_type.70, bf16[576,128]{1,0:T(8,128)(2,1)} %bitcast.22), kind=kLoop, calls=%fused_computation.17 | loop fusion | flops 303104 | bytes 303104 | tf_op jit(solution)/shard_map/concatenate | solution.py:236
  2.4 2.9 %collective-permute-start.2 = (bf16[592,128]{1,0:T(8,128)(2,1)S(1)}, bf16[592,128]{1,0:T(8,128)(2,1)S(1)}, u32[]{:S(2)}, u32[]{:S(2)}) collective-permute-start(bf16[592,128]{1,0:T(8,128)(2,1)S(1)} %pad_maximum_fusion.piece_ref), channel_id=1, source_target_pairs={{0,65},{1,64},{2,50},{3,51},{4,69},{5,68},{6,54},{7,55},{8,73},{9,... | collective-permute-start | bytes 454664 | tf_op jit(solution)/shard_map/ppermute | solution.py:29
  5.3 0.8 %collective-permute-start.1 = (bf16[592,128]{1,0:T(8,128)(2,1)S(1)}, bf16[592,128]{1,0:T(8,128)(2,1)S(1)}, u32[]{:S(2)}, u32[]{:S(2)}) collective-permute-start(bf16[592,128]{1,0:T(8,128)(2,1)S(1)} %pad_maximum_fusion.piece_ref), channel_id=1, source_target_pairs={{0,64},{1,65},{2,34},{3,35},{4,68},{5,69},{6,38},{7,39},{8,72},{9,... | collective-permute-start | bytes 454664 | tf_op jit(solution)/shard_map/ppermute | solution.py:29
  6.1 0.5 collective-permute-start
  6.6 0.9 %constant_dynamic-slice_fusion = bf16[96,576]{1,0:T(8,128)(2,1)S(1)} fusion(bf16[192,576]{1,0:T(8,128)(2,1)} %param.6, s32[]{:T(128)S(6)} %select_n.15), kind=kLoop, calls=%fused_computation.27 | loop fusion | bytes 221188 | tf_op jit(solution)/shard_map/dynamic_slice | solution.py:229
  7.5 1.7 %collective-permute-start.3 = (bf16[96,576]{1,0:T(8,128)(2,1)S(1)}, bf16[96,576]{1,0:T(8,128)(2,1)S(1)}, u32[]{:S(2)}, u32[]{:S(2)}) collective-permute-start(bf16[96,576]{1,0:T(8,128)(2,1)S(1)} %constant_dynamic-slice_fusion), channel_id=1, source_target_pairs={{0,1},{1,0},{2,3},{3,2},{4,5},{5,4},{6,7},{7,6},{8,9},{9,8},{10,11... | collective-permute-start | bytes 331784 | tf_op jit(solution)/shard_map/ppermute | solution.py:29
  9.1 0.7 convert.18
  9.8 0.9 %convert_reduce_fusion = s32[192]{0:T(256)S(1)} fusion(s32[192]{0:T(256)} %param.8), kind=kLoop, calls=%fused_computation.14 | loop fusion | flops 184128 | bytes 1536 | tf_op jit(solution)/shard_map/reduce_sum | solution.py:242
  10.8 0.1 add.67
  10.9 0.1 stack.8
  11.1 1.0 %fusion.10.kept_ref = bf16[96,640]{1,0:T(8,128)(2,1)S(1)} fusion(s32[]{:T(128)S(6)} %select_n.14, bf16[192,576]{1,0:T(8,128)(2,1)} %param.6, bf16[192,1]{1,0:T(8,128)(2,1)S(1)} %stack.8, bf16[192,1]{1,0:T(8,128)(2,1)S(1)} %add.67, bf16[640]{0:T(1024)(128)(2,1)S(1)} %pad.7.clone), kind=kLoop, calls=%fused_computation.24 | loop fusion | flops 491520 | bytes 346116 | tf_op jit(solution)/shard_map/concatenate | solution.py:244
  12.1 2.0 %collective-permute-done.3.gained_ref = bf16[96,576]{1,0:T(8,128)(2,1)S(1)} collective-permute-done((bf16[96,576]{1,0:T(8,128)(2,1)S(1)}, bf16[96,576]{1,0:T(8,128)(2,1)S(1)}, u32[]{:S(2)}, u32[]{:S(2)}) %collective-permute-start.3) | collective-permute-done | bytes 110624 | tf_op jit(solution)/shard_map/ppermute | solution.py:29
  14.1 3.2 %collective-permute-start.8 = (bf16[4,592,128]{2,1,0:T(8,128)(2,1)S(1)}, bf16[4,592,128]{2,1,0:T(8,128)(2,1)S(1)}, u32[]{:S(2)}, u32[]{:S(2)}) collective-permute-start(bf16[4,592,128]{2,1,0:T(8,128)(2,1)S(1)} %get-tuple-element.21.a_ref), channel_id=1, source_target_pairs={{0,48},{1,49},{2,67},{3,66},{4,52},{5,53},{6,71},{7,70},{8,56},{9,... | collective-permute-start | bytes 1818632 | tf_op jit(solution)/shard_map/ppermute | solution.py:29
  17.3 0.1 collective-permute-start.7
  17.4 4.0 %collective-permute-start.6 = (bf16[2,96,640]{2,1,0:T(8,128)(2,1)S(1)}, bf16[2,96,640]{2,1,0:T(8,128)(2,1)S(1)}, u32[]{:S(2)}, u32[]{:S(2)}) collective-permute-start(bf16[2,96,640]{2,1,0:T(8,128)(2,1)S(1)} %get-tuple-element.20.pair_ref), channel_id=1, source_target_pairs={{0,12},{1,13},{2,14},{3,15},{4,8},{5,9},{6,10},{7,11},{8,4},{9,5},... | collective-permute-start | bytes 737288 | tf_op jit(solution)/shard_map/ppermute | solution.py:29
  21.5 0.9 %collective-permute-start.4 = (bf16[2,96,640]{2,1,0:T(8,128)(2,1)S(1)}, bf16[2,96,640]{2,1,0:T(8,128)(2,1)S(1)}, u32[]{:S(2)}, u32[]{:S(2)}) collective-permute-start(bf16[2,96,640]{2,1,0:T(8,128)(2,1)S(1)} %get-tuple-element.20.pair_ref), channel_id=1, source_target_pairs={{0,4},{1,5},{2,6},{3,7},{4,0},{5,1},{6,2},{7,3},{8,12},{9,13},{10,... | collective-permute-start | bytes 737288 | tf_op jit(solution)/shard_map/ppermute | solution.py:29
  22.3 7.2 %collective-permute-done.6.r3_ref = bf16[2,96,640]{2,1,0:T(8,128)(2,1)S(1)} collective-permute-done((bf16[2,96,640]{2,1,0:T(8,128)(2,1)S(1)}, bf16[2,96,640]{2,1,0:T(8,128)(2,1)S(1)}, u32[]{:S(2)}, u32[]{:S(2)}) %collective-permute-start.6) | collective-permute-done | bytes 245792 | tf_op jit(solution)/shard_map/ppermute | solution.py:29
  29.5 1.1 %collective-permute-done.5.r2_ref = bf16[2,96,640]{2,1,0:T(8,128)(2,1)S(1)} collective-permute-done((bf16[2,96,640]{2,1,0:T(8,128)(2,1)S(1)}, bf16[2,96,640]{2,1,0:T(8,128)(2,1)S(1)}, u32[]{:S(2)}, u32[]{:S(2)}) %collective-permute-start.5) | collective-permute-done | bytes 245792 | tf_op jit(solution)/shard_map/ppermute | solution.py:29
  30.6 0.2 collective-permute-done.4.r1_ref
  31.0 3.1 %collective-permute-start.11 = (bf16[4,592,128]{2,1,0:T(8,128)(2,1)S(1)}, bf16[4,592,128]{2,1,0:T(8,128)(2,1)S(1)}, u32[]{:S(2)}, u32[]{:S(2)}) collective-permute-start(bf16[4,592,128]{2,1,0:T(8,128)(2,1)S(1)} %get-tuple-element.21.a_ref), channel_id=1, source_target_pairs={{0,32},{1,33},{2,66},{3,67},{4,36},{5,37},{6,70},{7,71},{8,40},{9,... | collective-permute-start | bytes 1818632 | tf_op jit(solution)/shard_map/ppermute | solution.py:29
  34.1 4.8 %shard_map.70 = (f32[4,576,128]{2,1,0:T(8,128)S(1)}, f32[4,576,128]{2,1,0:T(8,128)S(1)}, f32[768,1152]{1,0:T(8,128)S(1)}, bf16[768,1152]{1,0:T(8,128)(2,1)S(1)},...) custom-call(s32[1]{0:T(128)} %bitcast.place_ref, bf16[4,2,96,640]{3,2,1,0:T(8,128)(2,1)S(1)} %shard_map.69.near_ref, ...), custom_call_target="tpu_custom_call" | custom-call | flops 2717908992 | bytes 8000000 | tf_op jit(solution)/shard_map/pallas_call | solution.py:256
  39.0 1.0 %collective-permute-start.10 = (f16[4,576,128]{2,1,0:T(8,128)(2,1)S(1)}, f16[4,576,128]{2,1,0:T(8,128)(2,1)S(1)}, u32[]{:S(2)}, u32[]{:S(2)}) collective-permute-start(f16[4,576,128]{2,1,0:T(8,128)(2,1)S(1)} %convert_element_type.72), channel_id=1, source_target_pairs={{0,16},{1,17},{2,3},{3,2},{4,20},{5,21},{6,7},{7,6},{8,24},{9,25},... | collective-permute-start | bytes 1769480 | tf_op jit(solution)/shard_map/ppermute | solution.py:29
  40.0 2.7 %collective-permute-done.11.a_ref = bf16[4,592,128]{2,1,0:T(8,128)(2,1)S(1)} collective-permute-done((bf16[4,592,128]{2,1,0:T(8,128)(2,1)S(1)}, bf16[4,592,128]{2,1,0:T(8,128)(2,1)S(1)}, u32[]{:S(2)}, u32[]{:S(2)}) %collective-permute-start.11) | collective-permute-done | bytes 606240 | tf_op jit(solution)/shard_map/ppermute | solution.py:29
  42.7 4.1 %shard_map.71 = (f32[4,576,128]{2,1,0:T(8,128)S(1)}, f32[4,576,128]{2,1,0:T(8,128)S(1)}, f32[384,1152]{1,0:T(8,128)S(1)}, f32[384,1152]{1,0:T(8,128)S(1)}) custom-call(s32[1]{0:T(128)} %bitcast.place_ref, bf16[768,1152]{1,0:T(8,128)(2,1)S(1)} %get-tuple-element.24.captions_ref, bf16[1152,768]{1,0:T(8,128)(2,1)S(1)} %get-tuple-element.25.turned_ref, ...), custom_call_target="tpu_custom_call" | custom-call | flops 2717908992 | bytes 8000000 | tf_op jit(solution)/shard_map/pallas_call | solution.py:268
  47.0 2.2 %collective-permute-done.10 = f16[4,576,128]{2,1,0:T(8,128)(2,1)S(1)} collective-permute-done((f16[4,576,128]{2,1,0:T(8,128)(2,1)S(1)}, f16[4,576,128]{2,1,0:T(8,128)(2,1)S(1)}, u32[]{:S(2)}, u32[]{:S(2)}) %collective-permute-start.10) | collective-permute-done | bytes 589856 | tf_op jit(solution)/shard_map/ppermute | solution.py:29
  49.2 0.1 convert_element_type.75
  49.3 0.3 collective-permute-start.14
  49.5 2.2 %collective-permute-start.13 = (f16[4,576,128]{2,1,0:T(8,128)(2,1)S(1)}, f16[4,576,128]{2,1,0:T(8,128)(2,1)S(1)}, u32[]{:S(2)}, u32[]{:S(2)}) collective-permute-start(f16[4,576,128]{2,1,0:T(8,128)(2,1)S(1)} %convert_element_type.74), channel_id=1, source_target_pairs={{0,48},{1,49},{2,67},{3,66},{4,52},{5,53},{6,71},{7,70},{8,56},{9,... | collective-permute-start | bytes 1769480 | tf_op jit(solution)/shard_map/ppermute | solution.py:29
  51.7 1.3 %collective-permute-start.12 = (f16[4,576,128]{2,1,0:T(8,128)(2,1)S(1)}, f16[4,576,128]{2,1,0:T(8,128)(2,1)S(1)}, u32[]{:S(2)}, u32[]{:S(2)}) collective-permute-start(f16[4,576,128]{2,1,0:T(8,128)(2,1)S(1)} %convert_element_type.73), channel_id=1, source_target_pairs={{0,32},{1,33},{2,66},{3,67},{4,36},{5,37},{6,70},{7,71},{8,40},{9,... | collective-permute-start | bytes 1769480 | tf_op jit(solution)/shard_map/ppermute | solution.py:29
  53.0 0.2 fusion.11
  53.3 0.1 fusion.12
  53.4 3.0 %collective-permute-start.17 = (f16[96,1152]{1,0:T(8,128)(2,1)S(1)}, f16[96,1152]{1,0:T(8,128)(2,1)S(1)}, u32[]{:S(2)}, u32[]{:S(2)}) collective-permute-start(f16[96,1152]{1,0:T(8,128)(2,1)S(1)} %get-tuple-element.40), channel_id=1, source_target_pairs={{0,12},{1,13},{2,14},{3,15},{4,8},{5,9},{6,10},{7,11},{8,4},{9,5},... | collective-permute-start | bytes 663560 | tf_op jit(solution)/shard_map/ppermute | solution.py:29
  56.4 1.7 %collective-permute-start.15 = (f16[96,1152]{1,0:T(8,128)(2,1)S(1)}, f16[96,1152]{1,0:T(8,128)(2,1)S(1)}, u32[]{:S(2)}, u32[]{:S(2)}) collective-permute-start(f16[96,1152]{1,0:T(8,128)(2,1)S(1)} %get-tuple-element.42), channel_id=1, source_target_pairs={{0,8},{1,9},{2,10},{3,11},{4,12},{5,13},{6,14},{7,15},{8,0},{9,1},... | collective-permute-start | bytes 663560 | tf_op jit(solution)/shard_map/ppermute | solution.py:29
  58.2 8.9 %collective-permute-done.13 = f16[4,576,128]{2,1,0:T(8,128)(2,1)S(1)} collective-permute-done((f16[4,576,128]{2,1,0:T(8,128)(2,1)S(1)}, f16[4,576,128]{2,1,0:T(8,128)(2,1)S(1)}, u32[]{:S(2)}, u32[]{:S(2)}) %collective-permute-start.13) | collective-permute-done | bytes 589856 | tf_op jit(solution)/shard_map/ppermute | solution.py:29
  67.0 0.2 convert_add_fusion.1
  67.3 0.9 %collective-permute-done.15 = f16[96,1152]{1,0:T(8,128)(2,1)S(1)} collective-permute-done((f16[96,1152]{1,0:T(8,128)(2,1)S(1)}, f16[96,1152]{1,0:T(8,128)(2,1)S(1)}, u32[]{:S(2)}, u32[]{:S(2)}) %collective-permute-start.15) | collective-permute-done | bytes 221216 | tf_op jit(solution)/shard_map/ppermute | solution.py:29
  68.3 0.1 fusion.2
  68.4 0.1 fusion.13
  68.5 0.9 %collective-permute-start.21 = (bf16[96,576]{1,0:T(8,128)(2,1)S(1)}, bf16[96,576]{1,0:T(8,128)(2,1)S(1)}, u32[]{:S(2)}, u32[]{:S(2)}) collective-permute-start(bf16[96,576]{1,0:T(8,128)(2,1)S(1)} %get-tuple-element.47), channel_id=1, source_target_pairs={{0,1},{1,0},{2,3},{3,2},{4,5},{5,4},{6,7},{7,6},{8,9},{9,8},{10,11... | collective-permute-start | bytes 331784 | tf_op jit(solution)/shard_map/ppermute | solution.py:29
  69.5 0.1 slice_bitcast_fusion.2
  69.6 1.6 %collective-permute-start.18 = (f16[576,128]{1,0:T(8,128)(2,1)S(1)}, f16[576,128]{1,0:T(8,128)(2,1)S(1)}, u32[]{:S(2)}, u32[]{:S(2)}) collective-permute-start(f16[576,128]{1,0:T(8,128)(2,1)S(1)} %get-tuple-element.43), channel_id=1, source_target_pairs={{0,64},{1,65},{2,34},{3,35},{4,68},{5,69},{6,38},{7,39},{8,72},{9,... | collective-permute-start | bytes 442376 | tf_op jit(solution)/shard_map/ppermute | solution.py:29
  71.2 2.3 %collective-permute-start.20 = (f16[576,128]{1,0:T(8,128)(2,1)S(1)}, f16[576,128]{1,0:T(8,128)(2,1)S(1)}, u32[]{:S(2)}, u32[]{:S(2)}) collective-permute-start(f16[576,128]{1,0:T(8,128)(2,1)S(1)} %get-tuple-element.44), channel_id=1, source_target_pairs={{0,65},{1,64},{2,50},{3,51},{4,69},{5,68},{6,54},{7,55},{8,73},{9,... | collective-permute-start | bytes 442376 | tf_op jit(solution)/shard_map/ppermute | solution.py:29
  73.5 0.7 maximum_select_fusion
  74.3 2.0 %collective-permute-done.18 = f16[576,128]{1,0:T(8,128)(2,1)S(1)} collective-permute-done((f16[576,128]{1,0:T(8,128)(2,1)S(1)}, f16[576,128]{1,0:T(8,128)(2,1)S(1)}, u32[]{:S(2)}, u32[]{:S(2)}) %collective-permute-start.18) | collective-permute-done | bytes 147488 | tf_op jit(solution)/shard_map/ppermute | solution.py:29
  76.3 1.5 %collective-permute-done.20 = f16[576,128]{1,0:T(8,128)(2,1)S(1)} collective-permute-done((f16[576,128]{1,0:T(8,128)(2,1)S(1)}, f16[576,128]{1,0:T(8,128)(2,1)S(1)}, u32[]{:S(2)}, u32[]{:S(2)}) %collective-permute-start.20) | collective-permute-done | bytes 147488 | tf_op jit(solution)/shard_map/ppermute | solution.py:29
  77.9 0.8 %collective-permute-done.19 = f16[576,128]{1,0:T(8,128)(2,1)S(1)} collective-permute-done((f16[576,128]{1,0:T(8,128)(2,1)S(1)}, f16[576,128]{1,0:T(8,128)(2,1)S(1)}, u32[]{:S(2)}, u32[]{:S(2)}) %collective-permute-start.19) | collective-permute-done | bytes 147488 | tf_op jit(solution)/shard_map/ppermute | solution.py:29
  78.7 0.7 fusion.7
  (27 shorter events, 0.8 us)
Async XLA Ops:
  2.4 11.6 %collective-permute-start.2 = (bf16[592,128]{1,0:T(8,128)(2,1)S(1)}, bf16[592,128]{1,0:T(8,128)(2,1)S(1)}, u32[]{:S(2)}, u32[]{:S(2)}) collective-permute-start(bf16[592,128]{1,0:T(8,128)(2,1)S(1)} %pad_maximum_fusion.piece_ref), channel_id=1, source_target_pairs={{0,65},{1,64},{2,50},{3,51},{4,69},{5,68},{6,54},{7,55},{8,73},{9,... | collective-permute-start | bytes 454664 | tf_op jit(solution)/shard_map/ppermute | solution.py:29
  5.3 8.7 %collective-permute-start.1 = (bf16[592,128]{1,0:T(8,128)(2,1)S(1)}, bf16[592,128]{1,0:T(8,128)(2,1)S(1)}, u32[]{:S(2)}, u32[]{:S(2)}) collective-permute-start(bf16[592,128]{1,0:T(8,128)(2,1)S(1)} %pad_maximum_fusion.piece_ref), channel_id=1, source_target_pairs={{0,64},{1,65},{2,34},{3,35},{4,68},{5,69},{6,38},{7,39},{8,72},{9,... | collective-permute-start | bytes 454664 | tf_op jit(solution)/shard_map/ppermute | solution.py:29
  6.1 7.9 %collective-permute-start = (bf16[592,128]{1,0:T(8,128)(2,1)S(1)}, bf16[592,128]{1,0:T(8,128)(2,1)S(1)}, u32[]{:S(2)}, u32[]{:S(2)}) collective-permute-start(bf16[592,128]{1,0:T(8,128)(2,1)S(1)} %pad_maximum_fusion.piece_ref), channel_id=1, source_target_pairs={{0,1},{1,0},{2,18},{3,19},{4,5},{5,4},{6,22},{7,23},{8,9},{9,8},{1... | collective-permute-start | bytes 454664 | tf_op jit(solution)/shard_map/ppermute | solution.py:29
  7.5 6.5 %collective-permute-start.3 = (bf16[96,576]{1,0:T(8,128)(2,1)S(1)}, bf16[96,576]{1,0:T(8,128)(2,1)S(1)}, u32[]{:S(2)}, u32[]{:S(2)}) collective-permute-start(bf16[96,576]{1,0:T(8,128)(2,1)S(1)} %constant_dynamic-slice_fusion), channel_id=1, source_target_pairs={{0,1},{1,0},{2,3},{3,2},{4,5},{5,4},{6,7},{7,6},{8,9},{9,8},{10,11... | collective-permute-start | bytes 331784 | tf_op jit(solution)/shard_map/ppermute | solution.py:29
  14.1 16.7 %collective-permute-start.8 = (bf16[4,592,128]{2,1,0:T(8,128)(2,1)S(1)}, bf16[4,592,128]{2,1,0:T(8,128)(2,1)S(1)}, u32[]{:S(2)}, u32[]{:S(2)}) collective-permute-start(bf16[4,592,128]{2,1,0:T(8,128)(2,1)S(1)} %get-tuple-element.21.a_ref), channel_id=1, source_target_pairs={{0,48},{1,49},{2,67},{3,66},{4,52},{5,53},{6,71},{7,70},{8,56},{9,... | collective-permute-start | bytes 1818632 | tf_op jit(solution)/shard_map/ppermute | solution.py:29
  17.3 13.6 %collective-permute-start.7 = (bf16[4,592,128]{2,1,0:T(8,128)(2,1)S(1)}, bf16[4,592,128]{2,1,0:T(8,128)(2,1)S(1)}, u32[]{:S(2)}, u32[]{:S(2)}) collective-permute-start(bf16[4,592,128]{2,1,0:T(8,128)(2,1)S(1)} %get-tuple-element.21.a_ref), channel_id=1, source_target_pairs={{0,16},{1,17},{2,3},{3,2},{4,20},{5,21},{6,7},{7,6},{8,24},{9,25},... | collective-permute-start | bytes 1818632 | tf_op jit(solution)/shard_map/ppermute | solution.py:29
  17.4 12.1 %collective-permute-start.6 = (bf16[2,96,640]{2,1,0:T(8,128)(2,1)S(1)}, bf16[2,96,640]{2,1,0:T(8,128)(2,1)S(1)}, u32[]{:S(2)}, u32[]{:S(2)}) collective-permute-start(bf16[2,96,640]{2,1,0:T(8,128)(2,1)S(1)} %get-tuple-element.20.pair_ref), channel_id=1, source_target_pairs={{0,12},{1,13},{2,14},{3,15},{4,8},{5,9},{6,10},{7,11},{8,4},{9,5},... | collective-permute-start | bytes 737288 | tf_op jit(solution)/shard_map/ppermute | solution.py:29
  21.5 9.1 %collective-permute-start.5 = (bf16[2,96,640]{2,1,0:T(8,128)(2,1)S(1)}, bf16[2,96,640]{2,1,0:T(8,128)(2,1)S(1)}, u32[]{:S(2)}, u32[]{:S(2)}) collective-permute-start(bf16[2,96,640]{2,1,0:T(8,128)(2,1)S(1)} %get-tuple-element.20.pair_ref), channel_id=1, source_target_pairs={{0,8},{1,9},{2,10},{3,11},{4,12},{5,13},{6,14},{7,15},{8,0},{9,1},... | collective-permute-start | bytes 737288 | tf_op jit(solution)/shard_map/ppermute | solution.py:29
  21.5 9.4 %collective-permute-start.4 = (bf16[2,96,640]{2,1,0:T(8,128)(2,1)S(1)}, bf16[2,96,640]{2,1,0:T(8,128)(2,1)S(1)}, u32[]{:S(2)}, u32[]{:S(2)}) collective-permute-start(bf16[2,96,640]{2,1,0:T(8,128)(2,1)S(1)} %get-tuple-element.20.pair_ref), channel_id=1, source_target_pairs={{0,4},{1,5},{2,6},{3,7},{4,0},{5,1},{6,2},{7,3},{8,12},{9,13},{10,... | collective-permute-start | bytes 737288 | tf_op jit(solution)/shard_map/ppermute | solution.py:29
  30.9 3.2 %collective-permute-start.9 = (bf16[4,2,96,640]{3,2,1,0:T(8,128)(2,1)S(1)}, bf16[4,2,96,640]{3,2,1,0:T(8,128)(2,1)S(1)}, u32[]{:S(2)}, u32[]{:S(2)}) collective-permute-start(bf16[4,2,96,640]{3,2,1,0:T(8,128)(2,1)S(1)} %shard_map.69.near_ref), channel_id=1, source_target_pairs={{0,2},{1,3},{2,0},{3,1},{4,6},{5,7},{6,4},{7,5},{8,10},{9,11},{10,... | collective-permute-start | bytes 2949128 | tf_op jit(solution)/shard_map/ppermute | solution.py:29
  31.0 11.6 %collective-permute-start.11 = (bf16[4,592,128]{2,1,0:T(8,128)(2,1)S(1)}, bf16[4,592,128]{2,1,0:T(8,128)(2,1)S(1)}, u32[]{:S(2)}, u32[]{:S(2)}) collective-permute-start(bf16[4,592,128]{2,1,0:T(8,128)(2,1)S(1)} %get-tuple-element.21.a_ref), channel_id=1, source_target_pairs={{0,32},{1,33},{2,66},{3,67},{4,36},{5,37},{6,70},{7,71},{8,40},{9,... | collective-permute-start | bytes 1818632 | tf_op jit(solution)/shard_map/ppermute | solution.py:29
  39.0 10.1 %collective-permute-start.10 = (f16[4,576,128]{2,1,0:T(8,128)(2,1)S(1)}, f16[4,576,128]{2,1,0:T(8,128)(2,1)S(1)}, u32[]{:S(2)}, u32[]{:S(2)}) collective-permute-start(f16[4,576,128]{2,1,0:T(8,128)(2,1)S(1)} %convert_element_type.72), channel_id=1, source_target_pairs={{0,16},{1,17},{2,3},{3,2},{4,20},{5,21},{6,7},{7,6},{8,24},{9,25},... | collective-permute-start | bytes 1769480 | tf_op jit(solution)/shard_map/ppermute | solution.py:29
  49.3 3.8 %collective-permute-start.14 = (f16[384,1152]{1,0:T(8,128)(2,1)S(1)}, f16[384,1152]{1,0:T(8,128)(2,1)S(1)}, u32[]{:S(2)}, u32[]{:S(2)}) collective-permute-start(f16[384,1152]{1,0:T(8,128)(2,1)S(1)} %convert_element_type.75), channel_id=1, source_target_pairs={{0,2},{1,3},{2,0},{3,1},{4,6},{5,7},{6,4},{7,5},{8,10},{9,11},{10,... | collective-permute-start | bytes 2654216 | tf_op jit(solution)/shard_map/ppermute | solution.py:29
  49.5 17.5 %collective-permute-start.13 = (f16[4,576,128]{2,1,0:T(8,128)(2,1)S(1)}, f16[4,576,128]{2,1,0:T(8,128)(2,1)S(1)}, u32[]{:S(2)}, u32[]{:S(2)}) collective-permute-start(f16[4,576,128]{2,1,0:T(8,128)(2,1)S(1)} %convert_element_type.74), channel_id=1, source_target_pairs={{0,48},{1,49},{2,67},{3,66},{4,52},{5,53},{6,71},{7,70},{8,56},{9,... | collective-permute-start | bytes 1769480 | tf_op jit(solution)/shard_map/ppermute | solution.py:29
  51.7 15.3 %collective-permute-start.12 = (f16[4,576,128]{2,1,0:T(8,128)(2,1)S(1)}, f16[4,576,128]{2,1,0:T(8,128)(2,1)S(1)}, u32[]{:S(2)}, u32[]{:S(2)}) collective-permute-start(f16[4,576,128]{2,1,0:T(8,128)(2,1)S(1)} %convert_element_type.73), channel_id=1, source_target_pairs={{0,32},{1,33},{2,66},{3,67},{4,36},{5,37},{6,70},{7,71},{8,40},{9,... | collective-permute-start | bytes 1769480 | tf_op jit(solution)/shard_map/ppermute | solution.py:29
  53.4 13.9 %collective-permute-start.17 = (f16[96,1152]{1,0:T(8,128)(2,1)S(1)}, f16[96,1152]{1,0:T(8,128)(2,1)S(1)}, u32[]{:S(2)}, u32[]{:S(2)}) collective-permute-start(f16[96,1152]{1,0:T(8,128)(2,1)S(1)} %get-tuple-element.40), channel_id=1, source_target_pairs={{0,12},{1,13},{2,14},{3,15},{4,8},{5,9},{6,10},{7,11},{8,4},{9,5},... | collective-permute-start | bytes 663560 | tf_op jit(solution)/shard_map/ppermute | solution.py:29
  56.4 10.9 %collective-permute-start.16 = (f16[96,1152]{1,0:T(8,128)(2,1)S(1)}, f16[96,1152]{1,0:T(8,128)(2,1)S(1)}, u32[]{:S(2)}, u32[]{:S(2)}) collective-permute-start(f16[96,1152]{1,0:T(8,128)(2,1)S(1)} %get-tuple-element.41), channel_id=1, source_target_pairs={{0,4},{1,5},{2,6},{3,7},{4,0},{5,1},{6,2},{7,3},{8,12},{9,13},{10,... | collective-permute-start | bytes 663560 | tf_op jit(solution)/shard_map/ppermute | solution.py:29
  56.4 11.9 %collective-permute-start.15 = (f16[96,1152]{1,0:T(8,128)(2,1)S(1)}, f16[96,1152]{1,0:T(8,128)(2,1)S(1)}, u32[]{:S(2)}, u32[]{:S(2)}) collective-permute-start(f16[96,1152]{1,0:T(8,128)(2,1)S(1)} %get-tuple-element.42), channel_id=1, source_target_pairs={{0,8},{1,9},{2,10},{3,11},{4,12},{5,13},{6,14},{7,15},{8,0},{9,1},... | collective-permute-start | bytes 663560 | tf_op jit(solution)/shard_map/ppermute | solution.py:29
  68.5 5.0 %collective-permute-start.21 = (bf16[96,576]{1,0:T(8,128)(2,1)S(1)}, bf16[96,576]{1,0:T(8,128)(2,1)S(1)}, u32[]{:S(2)}, u32[]{:S(2)}) collective-permute-start(bf16[96,576]{1,0:T(8,128)(2,1)S(1)} %get-tuple-element.47), channel_id=1, source_target_pairs={{0,1},{1,0},{2,3},{3,2},{4,5},{5,4},{6,7},{7,6},{8,9},{9,8},{10,11... | collective-permute-start | bytes 331784 | tf_op jit(solution)/shard_map/ppermute | solution.py:29
  69.6 6.8 %collective-permute-start.18 = (f16[576,128]{1,0:T(8,128)(2,1)S(1)}, f16[576,128]{1,0:T(8,128)(2,1)S(1)}, u32[]{:S(2)}, u32[]{:S(2)}) collective-permute-start(f16[576,128]{1,0:T(8,128)(2,1)S(1)} %get-tuple-element.43), channel_id=1, source_target_pairs={{0,64},{1,65},{2,34},{3,35},{4,68},{5,69},{6,38},{7,39},{8,72},{9,... | collective-permute-start | bytes 442376 | tf_op jit(solution)/shard_map/ppermute | solution.py:29
  71.2 6.7 %collective-permute-start.20 = (f16[576,128]{1,0:T(8,128)(2,1)S(1)}, f16[576,128]{1,0:T(8,128)(2,1)S(1)}, u32[]{:S(2)}, u32[]{:S(2)}) collective-permute-start(f16[576,128]{1,0:T(8,128)(2,1)S(1)} %get-tuple-element.44), channel_id=1, source_target_pairs={{0,65},{1,64},{2,50},{3,51},{4,69},{5,68},{6,54},{7,55},{8,73},{9,... | collective-permute-start | bytes 442376 | tf_op jit(solution)/shard_map/ppermute | solution.py:29
  73.5 5.1 %collective-permute-start.19 = (f16[576,128]{1,0:T(8,128)(2,1)S(1)}, f16[576,128]{1,0:T(8,128)(2,1)S(1)}, u32[]{:S(2)}, u32[]{:S(2)}) collective-permute-start(f16[576,128]{1,0:T(8,128)(2,1)S(1)} %get-tuple-element.45), channel_id=1, source_target_pairs={{0,1},{1,0},{2,18},{3,19},{4,5},{5,4},{6,22},{7,23},{8,9},{9,8},{1... | collective-permute-start | bytes 442376 | tf_op jit(solution)/shard_map/ppermute | solution.py:29

commit v5 on v4

--- a/solution.py
+++ b/solution.py
@@ -272,14 +272,14 @@
         scratch=STAGE_SCRATCH, megabytes=10, flops=3 * DOT_FLOPS, nbytes=8_000_000,
     )(place, captions, turned, marks, groups[2], groups[3], caption_near)
     image_2, image_3 = image_2.astype(half), image_3.astype(half)
-    caption_far = after(caption_far, (received_1, image_2, image_3)).astype(half)
+    caption_far = after(caption_far, (received_1, image_2, image_3))
     crossed = exchange(caption_far, other_core)
     image_received = [
         received_1,
         exchange(image_2, second_axis(2)),
         exchange(image_3, second_axis(3)),
     ]
-    group_total = (caption_own + crossed.astype(jnp.float32)).reshape(4, HALF, 2 * F)
+    group_total = (caption_own + crossed).reshape(4, HALF, 2 * F)
     messages = [group_total[j].astype(half) for j in (2, 1, 3)]
     caption_received = [exchange(m, along_z(j)) for m, j in zip(messages, (2, 1, 3))]
     image_received = after(image_received, messages)

time: 79.6 us -> 79.5 us (level)
  no operation moved by 1% of the time
where the time goes in v5:
time: 79.5 us; the launch traced here: 79.3 us
  starting transfers between devices  31.8 us (40%)
  waiting for transfers between devices  29.4 us (37%)
  Pallas kernels  9.05 us (11%)
  other arithmetic  6.67 us (8%)
  local copies, waits for them, and re-layouts  1.55 us (2%)
  between operations  0.83 us (1%)
    ppermute x22, starting transfers between devices, exchange(): return lax.ppermute(value, ('dp', 'mp'), pairs)  31.8 us
    ppermute x22, waiting for transfers between devices, exchange(): return lax.ppermute(value, ('dp', 'mp'), pairs)  29.4 us
    pallas_call x1, Pallas kernels, body(): call(near_stage_kernel, (f32(4, F, IMG), f32(4, F, IMG), f32(CAPS, 2 * F)...  4.79 us
    pallas_call x1, Pallas kernels, body(): call(far_stage_kernel, (f32(4, F, IMG), f32(4, F, IMG), f32(CAPS // 2, 2...  4.12 us
  transfers between devices with their start and end apart: 22, of which 11 were waited for; matrix products, arithmetic and copies ran while one was open for 7% of the time, Pallas kernels for 11%

profile of v5, /device:TPU:0, one launch (start us, length us, event | category | flops | bytes accessed | tf_op | source)
XLA Modules:
  0.0 79.3 jit_solution(12676928497090888214)
XLA Ops:
  0.7 0.8 add_add_fusion
  1.5 0.9 %pad_maximum_fusion.piece_ref = bf16[592,128]{1,0:T(8,128)(2,1)S(1)} fusion(bf16[16,128]{1,0:T(8,128)(2,1)S(1)} %convert_element_type.64, bf16[576,128]{1,0:T(8,128)(2,1)} %bitcast.22), kind=kLoop, calls=%fused_computation.16 | loop fusion | flops 303104 | bytes 303104 | tf_op jit(solution)/shard_map/concatenate | solution.py:236
  2.4 2.9 %collective-permute-start.2 = (bf16[592,128]{1,0:T(8,128)(2,1)S(1)}, bf16[592,128]{1,0:T(8,128)(2,1)S(1)}, u32[]{:S(2)}, u32[]{:S(2)}) collective-permute-start(bf16[592,128]{1,0:T(8,128)(2,1)S(1)} %pad_maximum_fusion.piece_ref), channel_id=1, source_target_pairs={{0,65},{1,64},{2,50},{3,51},{4,69},{5,68},{6,54},{7,55},{8,73},{9,... | collective-permute-start | bytes 454664 | tf_op jit(solution)/shard_map/ppermute | solution.py:29
  5.3 0.8 %collective-permute-start.1 = (bf16[592,128]{1,0:T(8,128)(2,1)S(1)}, bf16[592,128]{1,0:T(8,128)(2,1)S(1)}, u32[]{:S(2)}, u32[]{:S(2)}) collective-permute-start(bf16[592,128]{1,0:T(8,128)(2,1)S(1)} %pad_maximum_fusion.piece_ref), channel_id=1, source_target_pairs={{0,64},{1,65},{2,34},{3,35},{4,68},{5,69},{6,38},{7,39},{8,72},{9,... | collective-permute-start | bytes 454664 | tf_op jit(solution)/shard_map/ppermute | solution.py:29
  6.1 0.5 collective-permute-start
  6.6 0.9 %constant_dynamic-slice_fusion = bf16[96,576]{1,0:T(8,128)(2,1)S(1)} fusion(bf16[192,576]{1,0:T(8,128)(2,1)} %param.6, s32[]{:T(128)S(6)} %select_n.15), kind=kLoop, calls=%fused_computation.26 | loop fusion | bytes 221188 | tf_op jit(solution)/shard_map/dynamic_slice | solution.py:229
  7.5 1.7 %collective-permute-start.3 = (bf16[96,576]{1,0:T(8,128)(2,1)S(1)}, bf16[96,576]{1,0:T(8,128)(2,1)S(1)}, u32[]{:S(2)}, u32[]{:S(2)}) collective-permute-start(bf16[96,576]{1,0:T(8,128)(2,1)S(1)} %constant_dynamic-slice_fusion), channel_id=1, source_target_pairs={{0,1},{1,0},{2,3},{3,2},{4,5},{5,4},{6,7},{7,6},{8,9},{9,8},{10,11... | collective-permute-start | bytes 331784 | tf_op jit(solution)/shard_map/ppermute | solution.py:29
  9.1 0.7 convert.18
  9.8 0.9 %convert_reduce_fusion = s32[192]{0:T(256)S(1)} fusion(s32[192]{0:T(256)} %param.8), kind=kLoop, calls=%fused_computation.13 | loop fusion | flops 184128 | bytes 1536 | tf_op jit(solution)/shard_map/reduce_sum | solution.py:242
  10.8 0.1 add.67
  10.9 0.1 stack.8
  11.1 1.0 %fusion.10.kept_ref = bf16[96,640]{1,0:T(8,128)(2,1)S(1)} fusion(s32[]{:T(128)S(6)} %select_n.14, bf16[192,576]{1,0:T(8,128)(2,1)} %param.6, bf16[192,1]{1,0:T(8,128)(2,1)S(1)} %stack.8, bf16[192,1]{1,0:T(8,128)(2,1)S(1)} %add.67, bf16[640]{0:T(1024)(128)(2,1)S(1)} %pad.7.clone), kind=kLoop, calls=%fused_computation.23 | loop fusion | flops 491520 | bytes 346116 | tf_op jit(solution)/shard_map/concatenate | solution.py:244
  12.1 2.0 %collective-permute-done.3.gained_ref = bf16[96,576]{1,0:T(8,128)(2,1)S(1)} collective-permute-done((bf16[96,576]{1,0:T(8,128)(2,1)S(1)}, bf16[96,576]{1,0:T(8,128)(2,1)S(1)}, u32[]{:S(2)}, u32[]{:S(2)}) %collective-permute-start.3) | collective-permute-done | bytes 110624 | tf_op jit(solution)/shard_map/ppermute | solution.py:29
  14.1 3.2 %collective-permute-start.8 = (bf16[4,592,128]{2,1,0:T(8,128)(2,1)S(1)}, bf16[4,592,128]{2,1,0:T(8,128)(2,1)S(1)}, u32[]{:S(2)}, u32[]{:S(2)}) collective-permute-start(bf16[4,592,128]{2,1,0:T(8,128)(2,1)S(1)} %get-tuple-element.21.a_ref), channel_id=1, source_target_pairs={{0,48},{1,49},{2,67},{3,66},{4,52},{5,53},{6,71},{7,70},{8,56},{9,... | collective-permute-start | bytes 1818632 | tf_op jit(solution)/shard_map/ppermute | solution.py:29
  17.3 0.1 collective-permute-start.7
  17.4 4.0 %collective-permute-start.6 = (bf16[2,96,640]{2,1,0:T(8,128)(2,1)S(1)}, bf16[2,96,640]{2,1,0:T(8,128)(2,1)S(1)}, u32[]{:S(2)}, u32[]{:S(2)}) collective-permute-start(bf16[2,96,640]{2,1,0:T(8,128)(2,1)S(1)} %get-tuple-element.20.pair_ref), channel_id=1, source_target_pairs={{0,12},{1,13},{2,14},{3,15},{4,8},{5,9},{6,10},{7,11},{8,4},{9,5},... | collective-permute-start | bytes 737288 | tf_op jit(solution)/shard_map/ppermute | solution.py:29
  21.5 0.9 %collective-permute-start.4 = (bf16[2,96,640]{2,1,0:T(8,128)(2,1)S(1)}, bf16[2,96,640]{2,1,0:T(8,128)(2,1)S(1)}, u32[]{:S(2)}, u32[]{:S(2)}) collective-permute-start(bf16[2,96,640]{2,1,0:T(8,128)(2,1)S(1)} %get-tuple-element.20.pair_ref), channel_id=1, source_target_pairs={{0,4},{1,5},{2,6},{3,7},{4,0},{5,1},{6,2},{7,3},{8,12},{9,13},{10,... | collective-permute-start | bytes 737288 | tf_op jit(solution)/shard_map/ppermute | solution.py:29
  22.3 7.2 %collective-permute-done.6.r3_ref = bf16[2,96,640]{2,1,0:T(8,128)(2,1)S(1)} collective-permute-done((bf16[2,96,640]{2,1,0:T(8,128)(2,1)S(1)}, bf16[2,96,640]{2,1,0:T(8,128)(2,1)S(1)}, u32[]{:S(2)}, u32[]{:S(2)}) %collective-permute-start.6) | collective-permute-done | bytes 245792 | tf_op jit(solution)/shard_map/ppermute | solution.py:29
  29.5 1.1 %collective-permute-done.5.r2_ref = bf16[2,96,640]{2,1,0:T(8,128)(2,1)S(1)} collective-permute-done((bf16[2,96,640]{2,1,0:T(8,128)(2,1)S(1)}, bf16[2,96,640]{2,1,0:T(8,128)(2,1)S(1)}, u32[]{:S(2)}, u32[]{:S(2)}) %collective-permute-start.5) | collective-permute-done | bytes 245792 | tf_op jit(solution)/shard_map/ppermute | solution.py:29
  30.6 0.2 collective-permute-done.4.r1_ref
  30.9 0.1 collective-permute-start.9
  31.0 3.1 %collective-permute-start.11 = (bf16[4,592,128]{2,1,0:T(8,128)(2,1)S(1)}, bf16[4,592,128]{2,1,0:T(8,128)(2,1)S(1)}, u32[]{:S(2)}, u32[]{:S(2)}) collective-permute-start(bf16[4,592,128]{2,1,0:T(8,128)(2,1)S(1)} %get-tuple-element.21.a_ref), channel_id=1, source_target_pairs={{0,32},{1,33},{2,66},{3,67},{4,36},{5,37},{6,70},{7,71},{8,40},{9,... | collective-permute-start | bytes 1818632 | tf_op jit(solution)/shard_map/ppermute | solution.py:29
  34.1 4.8 %shard_map.70 = (f32[4,576,128]{2,1,0:T(8,128)S(1)}, f32[4,576,128]{2,1,0:T(8,128)S(1)}, f32[768,1152]{1,0:T(8,128)S(1)}, bf16[768,1152]{1,0:T(8,128)(2,1)S(1)},...) custom-call(s32[1]{0:T(128)} %bitcast.place_ref, bf16[4,2,96,640]{3,2,1,0:T(8,128)(2,1)S(1)} %shard_map.69.near_ref, ...), custom_call_target="tpu_custom_call" | custom-call | flops 2717908992 | bytes 8000000 | tf_op jit(solution)/shard_map/pallas_call | solution.py:256
  39.0 1.0 %collective-permute-start.10 = (f16[4,576,128]{2,1,0:T(8,128)(2,1)S(1)}, f16[4,576,128]{2,1,0:T(8,128)(2,1)S(1)}, u32[]{:S(2)}, u32[]{:S(2)}) collective-permute-start(f16[4,576,128]{2,1,0:T(8,128)(2,1)S(1)} %convert_element_type.66), channel_id=1, source_target_pairs={{0,16},{1,17},{2,3},{3,2},{4,20},{5,21},{6,7},{7,6},{8,24},{9,25},... | collective-permute-start | bytes 1769480 | tf_op jit(solution)/shard_map/ppermute | solution.py:29
  40.0 2.7 %collective-permute-done.11.a_ref = bf16[4,592,128]{2,1,0:T(8,128)(2,1)S(1)} collective-permute-done((bf16[4,592,128]{2,1,0:T(8,128)(2,1)S(1)}, bf16[4,592,128]{2,1,0:T(8,128)(2,1)S(1)}, u32[]{:S(2)}, u32[]{:S(2)}) %collective-permute-start.11) | collective-permute-done | bytes 606240 | tf_op jit(solution)/shard_map/ppermute | solution.py:29
  42.7 4.1 %shard_map.71 = (f32[4,576,128]{2,1,0:T(8,128)S(1)}, f32[4,576,128]{2,1,0:T(8,128)S(1)}, f32[384,1152]{1,0:T(8,128)S(1)}, f32[384,1152]{1,0:T(8,128)S(1)}) custom-call(s32[1]{0:T(128)} %bitcast.place_ref, bf16[768,1152]{1,0:T(8,128)(2,1)S(1)} %get-tuple-element.24.captions_ref, bf16[1152,768]{1,0:T(8,128)(2,1)S(1)} %get-tuple-element.25.turned_ref, ...), custom_call_target="tpu_custom_call" | custom-call | flops 2717908992 | bytes 8000000 | tf_op jit(solution)/shard_map/pallas_call | solution.py:268
  47.0 2.2 %collective-permute-done.10 = f16[4,576,128]{2,1,0:T(8,128)(2,1)S(1)} collective-permute-done((f16[4,576,128]{2,1,0:T(8,128)(2,1)S(1)}, f16[4,576,128]{2,1,0:T(8,128)(2,1)S(1)}, u32[]{:S(2)}, u32[]{:S(2)}) %collective-permute-start.10) | collective-permute-done | bytes 589856 | tf_op jit(solution)/shard_map/ppermute | solution.py:29
  49.2 2.1 %collective-permute-start.13 = (f16[4,576,128]{2,1,0:T(8,128)(2,1)S(1)}, f16[4,576,128]{2,1,0:T(8,128)(2,1)S(1)}, u32[]{:S(2)}, u32[]{:S(2)}) collective-permute-start(f16[4,576,128]{2,1,0:T(8,128)(2,1)S(1)} %convert_element_type.68), channel_id=1, source_target_pairs={{0,48},{1,49},{2,67},{3,66},{4,52},{5,53},{6,71},{7,70},{8,56},{9,... | collective-permute-start | bytes 1769480 | tf_op jit(solution)/shard_map/ppermute | solution.py:29
  51.3 1.3 %collective-permute-start.12 = (f16[4,576,128]{2,1,0:T(8,128)(2,1)S(1)}, f16[4,576,128]{2,1,0:T(8,128)(2,1)S(1)}, u32[]{:S(2)}, u32[]{:S(2)}) collective-permute-start(f16[4,576,128]{2,1,0:T(8,128)(2,1)S(1)} %convert_element_type.67), channel_id=1, source_target_pairs={{0,32},{1,33},{2,66},{3,67},{4,36},{5,37},{6,70},{7,71},{8,40},{9,... | collective-permute-start | bytes 1769480 | tf_op jit(solution)/shard_map/ppermute | solution.py:29
  52.6 0.3 collective-permute-done.14
  52.9 0.2 fusion.11
  53.1 0.1 fusion.12
  53.2 3.0 %collective-permute-start.17 = (f16[96,1152]{1,0:T(8,128)(2,1)S(1)}, f16[96,1152]{1,0:T(8,128)(2,1)S(1)}, u32[]{:S(2)}, u32[]{:S(2)}) collective-permute-start(f16[96,1152]{1,0:T(8,128)(2,1)S(1)} %get-tuple-element.40), channel_id=1, source_target_pairs={{0,12},{1,13},{2,14},{3,15},{4,8},{5,9},{6,10},{7,11},{8,4},{9,5},... | collective-permute-start | bytes 663560 | tf_op jit(solution)/shard_map/ppermute | solution.py:29
  56.2 1.7 %collective-permute-start.15 = (f16[96,1152]{1,0:T(8,128)(2,1)S(1)}, f16[96,1152]{1,0:T(8,128)(2,1)S(1)}, u32[]{:S(2)}, u32[]{:S(2)}) collective-permute-start(f16[96,1152]{1,0:T(8,128)(2,1)S(1)} %get-tuple-element.42), channel_id=1, source_target_pairs={{0,8},{1,9},{2,10},{3,11},{4,12},{5,13},{6,14},{7,15},{8,0},{9,1},... | collective-permute-start | bytes 663560 | tf_op jit(solution)/shard_map/ppermute | solution.py:29
  58.0 8.6 %collective-permute-done.13 = f16[4,576,128]{2,1,0:T(8,128)(2,1)S(1)} collective-permute-done((f16[4,576,128]{2,1,0:T(8,128)(2,1)S(1)}, f16[4,576,128]{2,1,0:T(8,128)(2,1)S(1)}, u32[]{:S(2)}, u32[]{:S(2)}) %collective-permute-start.13) | collective-permute-done | bytes 589856 | tf_op jit(solution)/shard_map/ppermute | solution.py:29
  66.6 0.2 convert_add_fusion
  66.9 1.1 %collective-permute-done.15 = f16[96,1152]{1,0:T(8,128)(2,1)S(1)} collective-permute-done((f16[96,1152]{1,0:T(8,128)(2,1)S(1)}, f16[96,1152]{1,0:T(8,128)(2,1)S(1)}, u32[]{:S(2)}, u32[]{:S(2)}) %collective-permute-start.15) | collective-permute-done | bytes 221216 | tf_op jit(solution)/shard_map/ppermute | solution.py:29
  68.0 0.1 fusion.2
  68.1 0.1 fusion.13
  68.2 1.8 %collective-permute-start.21 = (bf16[96,576]{1,0:T(8,128)(2,1)S(1)}, bf16[96,576]{1,0:T(8,128)(2,1)S(1)}, u32[]{:S(2)}, u32[]{:S(2)}) collective-permute-start(bf16[96,576]{1,0:T(8,128)(2,1)S(1)} %get-tuple-element.47), channel_id=1, source_target_pairs={{0,1},{1,0},{2,3},{3,2},{4,5},{5,4},{6,7},{7,6},{8,9},{9,8},{10,11... | collective-permute-start | bytes 331784 | tf_op jit(solution)/shard_map/ppermute | solution.py:29
  70.1 0.1 slice_bitcast_fusion.2
  70.2 0.9 %collective-permute-start.18 = (f16[576,128]{1,0:T(8,128)(2,1)S(1)}, f16[576,128]{1,0:T(8,128)(2,1)S(1)}, u32[]{:S(2)}, u32[]{:S(2)}) collective-permute-start(f16[576,128]{1,0:T(8,128)(2,1)S(1)} %get-tuple-element.43), channel_id=1, source_target_pairs={{0,64},{1,65},{2,34},{3,35},{4,68},{5,69},{6,38},{7,39},{8,72},{9,... | collective-permute-start | bytes 442376 | tf_op jit(solution)/shard_map/ppermute | solution.py:29
  71.1 2.2 %collective-permute-start.20 = (f16[576,128]{1,0:T(8,128)(2,1)S(1)}, f16[576,128]{1,0:T(8,128)(2,1)S(1)}, u32[]{:S(2)}, u32[]{:S(2)}) collective-permute-start(f16[576,128]{1,0:T(8,128)(2,1)S(1)} %get-tuple-element.44), channel_id=1, source_target_pairs={{0,65},{1,64},{2,50},{3,51},{4,69},{5,68},{6,54},{7,55},{8,73},{9,... | collective-permute-start | bytes 442376 | tf_op jit(solution)/shard_map/ppermute | solution.py:29
  73.2 0.5 collective-permute-start.19
  73.8 0.7 maximum_select_fusion
  74.5 2.5 %collective-permute-done.18 = f16[576,128]{1,0:T(8,128)(2,1)S(1)} collective-permute-done((f16[576,128]{1,0:T(8,128)(2,1)S(1)}, f16[576,128]{1,0:T(8,128)(2,1)S(1)}, u32[]{:S(2)}, u32[]{:S(2)}) %collective-permute-start.18) | collective-permute-done | bytes 147488 | tf_op jit(solution)/shard_map/ppermute | solution.py:29
  77.0 1.5 %collective-permute-done.20 = f16[576,128]{1,0:T(8,128)(2,1)S(1)} collective-permute-done((f16[576,128]{1,0:T(8,128)(2,1)S(1)}, f16[576,128]{1,0:T(8,128)(2,1)S(1)}, u32[]{:S(2)}, u32[]{:S(2)}) %collective-permute-start.20) | collective-permute-done | bytes 147488 | tf_op jit(solution)/shard_map/ppermute | solution.py:29
  78.5 0.7 fusion.7
  (26 shorter events, 0.7 us)
Async XLA Ops:
  2.4 11.6 %collective-permute-start.2 = (bf16[592,128]{1,0:T(8,128)(2,1)S(1)}, bf16[592,128]{1,0:T(8,128)(2,1)S(1)}, u32[]{:S(2)}, u32[]{:S(2)}) collective-permute-start(bf16[592,128]{1,0:T(8,128)(2,1)S(1)} %pad_maximum_fusion.piece_ref), channel_id=1, source_target_pairs={{0,65},{1,64},{2,50},{3,51},{4,69},{5,68},{6,54},{7,55},{8,73},{9,... | collective-permute-start | bytes 454664 | tf_op jit(solution)/shard_map/ppermute | solution.py:29
  5.3 8.7 %collective-permute-start.1 = (bf16[592,128]{1,0:T(8,128)(2,1)S(1)}, bf16[592,128]{1,0:T(8,128)(2,1)S(1)}, u32[]{:S(2)}, u32[]{:S(2)}) collective-permute-start(bf16[592,128]{1,0:T(8,128)(2,1)S(1)} %pad_maximum_fusion.piece_ref), channel_id=1, source_target_pairs={{0,64},{1,65},{2,34},{3,35},{4,68},{5,69},{6,38},{7,39},{8,72},{9,... | collective-permute-start | bytes 454664 | tf_op jit(solution)/shard_map/ppermute | solution.py:29
  6.1 7.9 %collective-permute-start = (bf16[592,128]{1,0:T(8,128)(2,1)S(1)}, bf16[592,128]{1,0:T(8,128)(2,1)S(1)}, u32[]{:S(2)}, u32[]{:S(2)}) collective-permute-start(bf16[592,128]{1,0:T(8,128)(2,1)S(1)} %pad_maximum_fusion.piece_ref), channel_id=1, source_target_pairs={{0,1},{1,0},{2,18},{3,19},{4,5},{5,4},{6,22},{7,23},{8,9},{9,8},{1... | collective-permute-start | bytes 454664 | tf_op jit(solution)/shard_map/ppermute | solution.py:29
  7.5 6.5 %collective-permute-start.3 = (bf16[96,576]{1,0:T(8,128)(2,1)S(1)}, bf16[96,576]{1,0:T(8,128)(2,1)S(1)}, u32[]{:S(2)}, u32[]{:S(2)}) collective-permute-start(bf16[96,576]{1,0:T(8,128)(2,1)S(1)} %constant_dynamic-slice_fusion), channel_id=1, source_target_pairs={{0,1},{1,0},{2,3},{3,2},{4,5},{5,4},{6,7},{7,6},{8,9},{9,8},{10,11... | collective-permute-start | bytes 331784 | tf_op jit(solution)/shard_map/ppermute | solution.py:29
  14.1 16.7 %collective-permute-start.8 = (bf16[4,592,128]{2,1,0:T(8,128)(2,1)S(1)}, bf16[4,592,128]{2,1,0:T(8,128)(2,1)S(1)}, u32[]{:S(2)}, u32[]{:S(2)}) collective-permute-start(bf16[4,592,128]{2,1,0:T(8,128)(2,1)S(1)} %get-tuple-element.21.a_ref), channel_id=1, source_target_pairs={{0,48},{1,49},{2,67},{3,66},{4,52},{5,53},{6,71},{7,70},{8,56},{9,... | collective-permute-start | bytes 1818632 | tf_op jit(solution)/shard_map/ppermute | solution.py:29
  17.3 13.6 %collective-permute-start.7 = (bf16[4,592,128]{2,1,0:T(8,128)(2,1)S(1)}, bf16[4,592,128]{2,1,0:T(8,128)(2,1)S(1)}, u32[]{:S(2)}, u32[]{:S(2)}) collective-permute-start(bf16[4,592,128]{2,1,0:T(8,128)(2,1)S(1)} %get-tuple-element.21.a_ref), channel_id=1, source_target_pairs={{0,16},{1,17},{2,3},{3,2},{4,20},{5,21},{6,7},{7,6},{8,24},{9,25},... | collective-permute-start | bytes 1818632 | tf_op jit(solution)/shard_map/ppermute | solution.py:29
  17.4 12.1 %collective-permute-start.6 = (bf16[2,96,640]{2,1,0:T(8,128)(2,1)S(1)}, bf16[2,96,640]{2,1,0:T(8,128)(2,1)S(1)}, u32[]{:S(2)}, u32[]{:S(2)}) collective-permute-start(bf16[2,96,640]{2,1,0:T(8,128)(2,1)S(1)} %get-tuple-element.20.pair_ref), channel_id=1, source_target_pairs={{0,12},{1,13},{2,14},{3,15},{4,8},{5,9},{6,10},{7,11},{8,4},{9,5},... | collective-permute-start | bytes 737288 | tf_op jit(solution)/shard_map/ppermute | solution.py:29
  21.5 9.1 %collective-permute-start.5 = (bf16[2,96,640]{2,1,0:T(8,128)(2,1)S(1)}, bf16[2,96,640]{2,1,0:T(8,128)(2,1)S(1)}, u32[]{:S(2)}, u32[]{:S(2)}) collective-permute-start(bf16[2,96,640]{2,1,0:T(8,128)(2,1)S(1)} %get-tuple-element.20.pair_ref), channel_id=1, source_target_pairs={{0,8},{1,9},{2,10},{3,11},{4,12},{5,13},{6,14},{7,15},{8,0},{9,1},... | collective-permute-start | bytes 737288 | tf_op jit(solution)/shard_map/ppermute | solution.py:29
  21.5 9.4 %collective-permute-start.4 = (bf16[2,96,640]{2,1,0:T(8,128)(2,1)S(1)}, bf16[2,96,640]{2,1,0:T(8,128)(2,1)S(1)}, u32[]{:S(2)}, u32[]{:S(2)}) collective-permute-start(bf16[2,96,640]{2,1,0:T(8,128)(2,1)S(1)} %get-tuple-element.20.pair_ref), channel_id=1, source_target_pairs={{0,4},{1,5},{2,6},{3,7},{4,0},{5,1},{6,2},{7,3},{8,12},{9,13},{10,... | collective-permute-start | bytes 737288 | tf_op jit(solution)/shard_map/ppermute | solution.py:29
  30.9 3.2 %collective-permute-start.9 = (bf16[4,2,96,640]{3,2,1,0:T(8,128)(2,1)S(1)}, bf16[4,2,96,640]{3,2,1,0:T(8,128)(2,1)S(1)}, u32[]{:S(2)}, u32[]{:S(2)}) collective-permute-start(bf16[4,2,96,640]{3,2,1,0:T(8,128)(2,1)S(1)} %shard_map.69.near_ref), channel_id=1, source_target_pairs={{0,2},{1,3},{2,0},{3,1},{4,6},{5,7},{6,4},{7,5},{8,10},{9,11},{10,... | collective-permute-start | bytes 2949128 | tf_op jit(solution)/shard_map/ppermute | solution.py:29
  31.0 11.6 %collective-permute-start.11 = (bf16[4,592,128]{2,1,0:T(8,128)(2,1)S(1)}, bf16[4,592,128]{2,1,0:T(8,128)(2,1)S(1)}, u32[]{:S(2)}, u32[]{:S(2)}) collective-permute-start(bf16[4,592,128]{2,1,0:T(8,128)(2,1)S(1)} %get-tuple-element.21.a_ref), channel_id=1, source_target_pairs={{0,32},{1,33},{2,66},{3,67},{4,36},{5,37},{6,70},{7,71},{8,40},{9,... | collective-permute-start | bytes 1818632 | tf_op jit(solution)/shard_map/ppermute | solution.py:29
  39.0 10.1 %collective-permute-start.10 = (f16[4,576,128]{2,1,0:T(8,128)(2,1)S(1)}, f16[4,576,128]{2,1,0:T(8,128)(2,1)S(1)}, u32[]{:S(2)}, u32[]{:S(2)}) collective-permute-start(f16[4,576,128]{2,1,0:T(8,128)(2,1)S(1)} %convert_element_type.66), channel_id=1, source_target_pairs={{0,16},{1,17},{2,3},{3,2},{4,20},{5,21},{6,7},{7,6},{8,24},{9,25},... | collective-permute-start | bytes 1769480 | tf_op jit(solution)/shard_map/ppermute | solution.py:29
  49.2 3.7 %collective-permute-start.14 = (f32[384,1152]{1,0:T(8,128)S(1)}, f32[384,1152]{1,0:T(8,128)S(1)}, u32[]{:S(2)}, u32[]{:S(2)}) collective-permute-start(f32[384,1152]{1,0:T(8,128)S(1)} %get-tuple-element.33), channel_id=1, source_target_pairs={{0,2},{1,3},{2,0},{3,1},{4,6},{5,7},{6,4},{7,5},{8,10},{9,11},{10,... | collective-permute-start | bytes 5308424 | tf_op jit(solution)/shard_map/ppermute | solution.py:29
  49.2 17.4 %collective-permute-start.13 = (f16[4,576,128]{2,1,0:T(8,128)(2,1)S(1)}, f16[4,576,128]{2,1,0:T(8,128)(2,1)S(1)}, u32[]{:S(2)}, u32[]{:S(2)}) collective-permute-start(f16[4,576,128]{2,1,0:T(8,128)(2,1)S(1)} %convert_element_type.68), channel_id=1, source_target_pairs={{0,48},{1,49},{2,67},{3,66},{4,52},{5,53},{6,71},{7,70},{8,56},{9,... | collective-permute-start | bytes 1769480 | tf_op jit(solution)/shard_map/ppermute | solution.py:29
  51.3 15.3 %collective-permute-start.12 = (f16[4,576,128]{2,1,0:T(8,128)(2,1)S(1)}, f16[4,576,128]{2,1,0:T(8,128)(2,1)S(1)}, u32[]{:S(2)}, u32[]{:S(2)}) collective-permute-start(f16[4,576,128]{2,1,0:T(8,128)(2,1)S(1)} %convert_element_type.67), channel_id=1, source_target_pairs={{0,32},{1,33},{2,66},{3,67},{4,36},{5,37},{6,70},{7,71},{8,40},{9,... | collective-permute-start | bytes 1769480 | tf_op jit(solution)/shard_map/ppermute | solution.py:29
  53.2 13.6 %collective-permute-start.17 = (f16[96,1152]{1,0:T(8,128)(2,1)S(1)}, f16[96,1152]{1,0:T(8,128)(2,1)S(1)}, u32[]{:S(2)}, u32[]{:S(2)}) collective-permute-start(f16[96,1152]{1,0:T(8,128)(2,1)S(1)} %get-tuple-element.40), channel_id=1, source_target_pairs={{0,12},{1,13},{2,14},{3,15},{4,8},{5,9},{6,10},{7,11},{8,4},{9,5},... | collective-permute-start | bytes 663560 | tf_op jit(solution)/shard_map/ppermute | solution.py:29
  56.2 10.6 %collective-permute-start.16 = (f16[96,1152]{1,0:T(8,128)(2,1)S(1)}, f16[96,1152]{1,0:T(8,128)(2,1)S(1)}, u32[]{:S(2)}, u32[]{:S(2)}) collective-permute-start(f16[96,1152]{1,0:T(8,128)(2,1)S(1)} %get-tuple-element.41), channel_id=1, source_target_pairs={{0,4},{1,5},{2,6},{3,7},{4,0},{5,1},{6,2},{7,3},{8,12},{9,13},{10,... | collective-permute-start | bytes 663560 | tf_op jit(solution)/shard_map/ppermute | solution.py:29
  56.2 11.7 %collective-permute-start.15 = (f16[96,1152]{1,0:T(8,128)(2,1)S(1)}, f16[96,1152]{1,0:T(8,128)(2,1)S(1)}, u32[]{:S(2)}, u32[]{:S(2)}) collective-permute-start(f16[96,1152]{1,0:T(8,128)(2,1)S(1)} %get-tuple-element.42), channel_id=1, source_target_pairs={{0,8},{1,9},{2,10},{3,11},{4,12},{5,13},{6,14},{7,15},{8,0},{9,1},... | collective-permute-start | bytes 663560 | tf_op jit(solution)/shard_map/ppermute | solution.py:29
  68.2 5.6 %collective-permute-start.21 = (bf16[96,576]{1,0:T(8,128)(2,1)S(1)}, bf16[96,576]{1,0:T(8,128)(2,1)S(1)}, u32[]{:S(2)}, u32[]{:S(2)}) collective-permute-start(bf16[96,576]{1,0:T(8,128)(2,1)S(1)} %get-tuple-element.47), channel_id=1, source_target_pairs={{0,1},{1,0},{2,3},{3,2},{4,5},{5,4},{6,7},{7,6},{8,9},{9,8},{10,11... | collective-permute-start | bytes 331784 | tf_op jit(solution)/shard_map/ppermute | solution.py:29
  70.2 6.8 %collective-permute-start.18 = (f16[576,128]{1,0:T(8,128)(2,1)S(1)}, f16[576,128]{1,0:T(8,128)(2,1)S(1)}, u32[]{:S(2)}, u32[]{:S(2)}) collective-permute-start(f16[576,128]{1,0:T(8,128)(2,1)S(1)} %get-tuple-element.43), channel_id=1, source_target_pairs={{0,64},{1,65},{2,34},{3,35},{4,68},{5,69},{6,38},{7,39},{8,72},{9,... | collective-permute-start | bytes 442376 | tf_op jit(solution)/shard_map/ppermute | solution.py:29
  71.1 7.4 %collective-permute-start.20 = (f16[576,128]{1,0:T(8,128)(2,1)S(1)}, f16[576,128]{1,0:T(8,128)(2,1)S(1)}, u32[]{:S(2)}, u32[]{:S(2)}) collective-permute-start(f16[576,128]{1,0:T(8,128)(2,1)S(1)} %get-tuple-element.44), channel_id=1, source_target_pairs={{0,65},{1,64},{2,50},{3,51},{4,69},{5,68},{6,54},{7,55},{8,73},{9,... | collective-permute-start | bytes 442376 | tf_op jit(solution)/shard_map/ppermute | solution.py:29
  73.2 5.3 %collective-permute-start.19 = (f16[576,128]{1,0:T(8,128)(2,1)S(1)}, f16[576,128]{1,0:T(8,128)(2,1)S(1)}, u32[]{:S(2)}, u32[]{:S(2)}) collective-permute-start(f16[576,128]{1,0:T(8,128)(2,1)S(1)} %get-tuple-element.45), channel_id=1, source_target_pairs={{0,1},{1,0},{2,18},{3,19},{4,5},{5,4},{6,22},{7,23},{8,9},{9,8},{1... | collective-permute-start | bytes 442376 | tf_op jit(solution)/shard_map/ppermute | solution.py:29
